TPU v7x, 512 devices: a whole 4x8x8 slice. The times are simulated.
512 devices in a mesh: ij: 4 (over x), cd: 128 (over y, z, core).
Axes of the slice: x: 4, y: 8, z: 8, core: 2. Of those that a mesh axis runs over, the one named last changes fastest.
Arguments:
- amplitudes: bfloat16 [131072, 1024], P('cd', 'ij'), may hold values from -6 to 6
- owned_columns: int32 [128, 2048], replicated, may hold values from -1 to 131071, as said below
- ladder_ints: bfloat16 [1024, 262144], P('ij', 'cd'), may hold values from -0.0625 to 0.0625
Outputs:
- ladder: bfloat16 [1024, 1024], P(('ij', 'cd'))
Inputs may be any that keep to these rules, and one draw needn't show every extreme that they name: `owned_columns`: row k lists in increasing order the packed cd columns whose integrals device k of cd holds, followed by -1 in its unused slots; every column stands in exactly one row. Of each range of 1024 consecutive columns at most 16 stand in one row; some rows take exactly 16 from every range and so fill all 2048 slots.
All inputs are finite; a program needn't handle non-finite values.
Results may differ from a plain program's by a relative error of at most 0.0023.
Values may be sent and summed in bfloat16 or wider, within the bound.
No kernel may reach another device: no remote copies, remote signals or barrier semaphores. Data moves between devices by JAX's collectives and lax.ppermute only.
A program may use at most 64 MiB of HBM per device.

v0:
```python
import jax
import jax.numpy as jnp
from jax import lax
from jax.sharding import PartitionSpec as P


def body(amplitudes, owned_columns, ladder_ints):
    device = lax.axis_index("cd")
    devices_cd = lax.axis_size("cd")
    width = amplitudes.shape[0]
    capacity = 2 * width // devices_cd
    slot_total = owned_columns.shape[1]
    base_column = device * width
    table_live = owned_columns >= 0
    below = jnp.sum(table_live & (owned_columns < base_column), axis=1)
    in_range = table_live & (owned_columns >= base_column) & (owned_columns < base_column + width)
    sent_count = jnp.sum(in_range, axis=1)
    slot_pick = jnp.minimum(below[:, None] + jnp.arange(capacity)[None, :], slot_total - 1)
    chosen = jnp.take_along_axis(owned_columns, slot_pick, axis=1) - base_column
    valid = jnp.arange(capacity)[None, :] < sent_count[:, None]
    chosen = jnp.where(valid, chosen, 0)
    outgoing = jnp.where(valid[:, :, None], amplitudes[chosen], jnp.zeros((), amplitudes.dtype))
    incoming = lax.all_to_all(outgoing, "cd", split_axis=0, concat_axis=0, tiled=True)
    own_row = lax.dynamic_index_in_dim(owned_columns, device, 0, keepdims=False)
    row_live = own_row >= 0
    source_dev = jnp.where(row_live, own_row // width, 0)
    range_starts = jnp.arange(devices_cd) * width
    starts_at = jnp.sum(row_live[None, :] & (own_row[None, :] < range_starts[:, None]), axis=1)
    first_of = jnp.sum(
        jnp.where(source_dev[:, None] == jnp.arange(devices_cd)[None, :], starts_at[None, :], 0),
        axis=1,
    )
    position = jnp.arange(slot_total) - first_of
    flat_index = jnp.where(row_live, source_dev * capacity + position, 0)
    received = incoming.reshape(devices_cd * capacity, incoming.shape[2])[flat_index]
    own_amps = jnp.where(row_live[:, None], received, jnp.zeros((), received.dtype))
    partial_value = jnp.dot(
        lax.all_gather(ladder_ints, "ij", axis=0, tiled=True),
        own_amps,
        preferred_element_type=jnp.float32,
    )
    pair_groups = lax.axis_size("ij")
    shaped = partial_value.reshape(
        pair_groups, partial_value.shape[0] // pair_groups, partial_value.shape[1]
    )
    summed = lax.psum_scatter(shaped, "cd", scatter_dimension=1, tiled=True)
    finished = summed.astype(jnp.bfloat16)
    spread = lax.all_to_all(finished, "ij", split_axis=0, concat_axis=2, tiled=True)
    return spread[0]


def solution(mesh):
    return jax.shard_map(
        body,
        mesh=mesh,
        in_specs=(P("cd", "ij"), P(), P("ij", "cd")),
        out_specs=P(("ij", "cd"), None),
        check_vma=False,
    )
```

profile of v0, /device:TPU:2, one launch (start us, length us, event | category | flops | bytes accessed | tf_op | source)
XLA Modules:
  0.0 608.8 jit_solution(9674760693623711589)
XLA Ops:
  6.5 0.0 copy-start
  6.5 0.0 copy-start.1
  6.5 0.0 all-gather.2.cloned.1.call-start
  6.5 0.7 all-gather.2.cloned.1.call-update
  7.3 1.7 convert_reduce_fusion.2
  9.0 0.1 shift-left_or_fusion
  9.1 0.1 reshape.313
  9.2 0.0 copy-done.1
  9.2 16.6 %gather_fusion.2 = s32[2048]{0:T(1024)S(1)} fusion(s32[128,2048]{1,0:T(8,128)S(1)} %copy-done.1, s32[2048]{0:T(1024)S(1)} %reshape.313), kind=kCustom, calls=%fused_computation.2 | custom fusion | bytes 32768 | tf_op jit(solution)/shard_map/jit(take_along_axis)/gather | solution.py:19
  25.9 0.1 gather.13
  25.9 0.1 compare_select_fusion
  26.1 0.1 reshape.299
  26.1 0.0 copy-done
  26.2 7.5 %gather_fusion = bf16[2048,256]{1,0:T(8,128)(2,1)S(1)} fusion(bf16[1024,256]{1,0:T(8,128)(2,1)S(1)} %copy-done, s32[2048]{0:T(1024)S(1)} %broadcast_clamp_fusion.1), kind=kCustom, calls=%fused_computation | custom fusion | bytes 2105344 | tf_op jit(solution)/shard_map/gather | solution.py:22
  33.7 0.1 iota_compare_fusion.2
  33.8 1.3 broadcast_select_fusion
  35.0 17.8 %all-to-all-start = ((bf16[128,16,256]{2,1,0:T(8,128)(2,1)}), bf16[128,16,256]{2,1,0:T(8,128)(2,1)S(1)}, u32[]{:S(2)}, u32[]{:S(2)}) async-start(bf16[128,16,256]{2,1,0:T(8,128)(2,1)} %broadcast_select_fusion), calls=%async_computation | async-start | bytes 2097152 | tf_op jit(solution)/shard_map/all_to_all | solution.py:23
  52.8 1.3 dynamic-slice
  54.8 0.3 convert_reduce_fusion
  55.1 0.6 select_reduce_fusion
  55.8 0.1 compare_select_fusion.2
  55.8 27.9 %all-to-all-done = bf16[128,16,256]{2,1,0:T(8,128)(2,1)S(1)} async-done(((bf16[128,16,256]{2,1,0:T(8,128)(2,1)}), bf16[128,16,256]{2,1,0:T(8,128)(2,1)S(1)}, u32[]{:S(2)}, u32[]{:S(2)}) %all-to-all-start) | async-done | bytes 1048608 | tf_op jit(solution)/shard_map/all_to_all | solution.py:23
  83.7 7.5 %gather_fusion.1 = bf16[2048,256]{1,0:T(8,128)(2,1)S(1)} fusion(bf16[2048,256]{1,0:T(8,128)(2,1)S(1)} %bitcast.30, s32[2048]{0:T(1024)S(1)} %broadcast_clamp_fusion), kind=kCustom, calls=%fused_computation.1 | custom fusion | bytes 2105344 | tf_op jit(solution)/shard_map/gather | solution.py:35
  91.2 0.0 all-gather.2.cloned.1.call-done
  91.2 3.9 convolution_bitcast_fusion
  95.1 0.5 reshape.296
  95.6 0.7 copy.8
  96.3 496.6 %all-reduce.2 = bf16[4,256,256]{2,0,1:T(4,128)(2,1)S(1)} all-reduce(f32[4,256,256]{2,0,1:T(4,128)S(1)} %copy.8), channel_id=2, replica_groups=mesh['ij'=4,'cd'=128] {'cd'}, use_global_device_ids=true, to_apply=%region_4.5.clone | all-reduce | flops 262144 | bytes 1572864
  592.9 8.5 %all_to_all.20 = bf16[4,2,256]{2,1,0:T(2,128)(2,1)S(1)} all-to-all(bf16[4,2,256]{2,1,0:T(2,128)(2,1)S(1)} %copy.9), channel_id=1, replica_groups=mesh['ij'=4,'cd'=128] {'ij'}, dimensions={0} | all-to-all | bytes 8192 | tf_op jit(solution)/shard_map/all_to_all | solution.py:48
  601.4 0.6 copy.13
  (8 shorter events, 0.1 us)
Async XLA Ops:
  6.5 19.6 %copy-start = (bf16[1024,256]{1,0:T(8,128)(2,1)S(1)}, bf16[1024,256]{1,0:T(8,128)(2,1)}, u32[]{:S(2)}) copy-start(bf16[1024,256]{1,0:T(8,128)(2,1)} %param.3) | copy-start | bytes 1572868
  6.5 2.7 copy-start.1
  6.5 84.7 %all-gather.2.cloned.1.call-start = ((), (), s32[]{:S(2)}) async-start(), calls=%async_computation.2 | async-start | bytes 5242880 | tf_op jit(solution)/shard_map/all_gather | solution.py:38
  35.0 48.7 %all-to-all-start = ((bf16[128,16,256]{2,1,0:T(8,128)(2,1)}), bf16[128,16,256]{2,1,0:T(8,128)(2,1)S(1)}, u32[]{:S(2)}, u32[]{:S(2)}) async-start(bf16[128,16,256]{2,1,0:T(8,128)(2,1)} %broadcast_select_fusion), calls=%async_computation | async-start | bytes 2097152 | tf_op jit(solution)/shard_map/all_to_all | solution.py:23
Sparse Core Ops, SparseCore 0:
  9.5 57.5 all-gather.1
where the time goes:
time: 609 us
  blocking collectives  505 us (83%)
  local copies, waits for them, and re-layouts  35 us (6%)
  waiting for transfers between devices  28.6 us (5%)
  starting transfers between devices  17.8 us (3%)
  between operations  14.2 us (2%)
    unnamed x1, blocking collectives  497 us
    all_to_all x1, waiting for transfers between devices, body(): lax.all_to_all(outgoing, 'cd', split_axis=0, concat_axis=0, tiled=True)  27.9 us
    all_to_all x1, starting transfers between devices, body(): lax.all_to_all(outgoing, 'cd', split_axis=0, concat_axis=0, tiled=True)  17.8 us
    gather x3, local copies, waits for them, and re-layouts, body(): chosen = jnp.take_along_axis(owned_columns, slot_pick, axis=1) - base_column  16.8 us
  transfers between devices with their start and end apart: 2, of which 1 were waited for; matrix products, arithmetic and copies ran while one was open for 6% of the time, Pallas kernels for 0%

commit v1 on v0

v1 whole, which is shorter than its diff:
```python
import jax
import jax.numpy as jnp
from jax import lax
from jax.experimental import pallas as pl
from jax.experimental.pallas import tpu as pltpu
from jax.sharding import PartitionSpec as P

F32 = jnp.float32
BF16 = jnp.bfloat16
NT = (((1,), (1,)), ((), ()))
VMEM_LIMIT = 48 * 1024 * 1024


def vmem_spec():
    return pl.BlockSpec(memory_space=pltpu.VMEM)


def identity(size):
    rows = lax.broadcasted_iota(jnp.int32, (size, size), 0)
    cols = lax.broadcasted_iota(jnp.int32, (size, size), 1)
    return jnp.where(rows == cols, 1.0, 0.0).astype(BF16)


def pack_kernel(starts, ints, out, slots):
    capacity = out.shape[1]
    total, chunk = ints.shape[1], 256
    eye = identity(chunk)
    for step in range(total // chunk):
        at = pl.ds(step * chunk, chunk)
        slots[at, :] = lax.dot_general(eye, ints[:, at], NT, preferred_element_type=F32)
    slots[pl.ds(total, capacity + 8), :] = jnp.zeros((capacity + 8, slots.shape[1]), F32)
    for dest in range(out.shape[0]):
        start = starts[dest]
        aligned = pl.multiple_of((start // 8) * 8, 8)
        window = slots[pl.ds(aligned, capacity + 8), :]
        window = pltpu.roll(window, capacity + 8 - (start - aligned), 0)
        out[dest] = window[:capacity].astype(BF16)


def order_kernel(capacity, base_ref, owned, amps, out, offsets):
    base = base_ref[0]
    holders, total = owned.shape
    width = amps.shape[0]
    beyond = jnp.int32(1 << 30)
    table = owned[...]
    table = jnp.where(table < 0, beyond, table - base)
    below = jnp.zeros((holders, 128), F32)
    ended = jnp.zeros((holders, 128), F32)
    for tile in range(total // 128):
        part = table[:, tile * 128:(tile + 1) * 128]
        below = below + jnp.where(part < 0, 1.0, 0.0)
        ended = ended + jnp.where(part < width, 1.0, 0.0)
    ones = jnp.ones((128, 128), BF16)
    below = jnp.dot(below.astype(BF16), ones, preferred_element_type=F32)
    ended = jnp.dot(ended.astype(BF16), ones, preferred_element_type=F32)
    counts = (ended - below).astype(BF16)
    rows = lax.broadcasted_iota(jnp.int32, (holders, holders), 0)
    cols = lax.broadcasted_iota(jnp.int32, (holders, holders), 1)
    earlier = jnp.where(cols < rows, 1.0, 0.0).astype(BF16)
    first = jnp.dot(earlier, counts, preferred_element_type=F32).astype(jnp.int32)
    offsets[...] = first
    start = below.astype(jnp.int32)
    window = jnp.concatenate([table, jnp.full((holders, 128), beyond, jnp.int32)], axis=1)
    shift = total // 2
    while shift >= 128:
        keep = shift + 128
        taken = (start & shift) != 0
        taken = jnp.concatenate([taken[:, :128]] * (keep // 128), axis=1)
        window = jnp.where(taken, window[:, shift:shift + keep], window[:, :keep])
        shift //= 2
    while shift >= 1:
        taken = (start & shift) != 0
        taken = jnp.concatenate([taken, taken], axis=1)
        window = jnp.where(taken, pltpu.roll(window, 256 - shift, 1), window)
        shift //= 2
    column = lax.broadcasted_iota(jnp.int32, (holders, width), 1)
    place = jnp.zeros((holders, width), jnp.int32)
    for slot in range(capacity):
        here = window[:, slot:slot + 1] == column
        place = place + jnp.where(here, first[:, :1] + slot, 0)
    place = jnp.sum(place, axis=0, keepdims=True)
    chunk = 256
    values = amps[...]
    for step in range(width // chunk):
        wanted = lax.broadcasted_iota(jnp.int32, (chunk, width), 0) + step * chunk
        pick = jnp.where(wanted == place, 1.0, 0.0).astype(BF16)
        out[pl.ds(step * chunk, chunk), :] = jnp.dot(
            pick, values, preferred_element_type=F32
        ).astype(BF16)


def multiply_kernel(offsets, where_ref, received, amps0, amps1, amps2, amps3, kept, given, rows_ref, result):
    group, core = where_ref[0], where_ref[1]
    holders, capacity, pairs = received.shape
    width = amps0.shape[0]
    line = lax.broadcasted_iota(jnp.int32, (capacity + 8, pairs), 0)
    blank = jnp.zeros((8, pairs), F32)
    for holder in range(holders):
        start = offsets[holder]
        aligned = pl.multiple_of((start // 8) * 8, 8)
        at = pl.ds(aligned, capacity + 8)
        window = jnp.concatenate([received[holder].astype(F32), blank], axis=0)
        window = pltpu.roll(window, start - aligned, 0)
        rows_ref[at, :] = jnp.where(line < start - aligned, rows_ref[at, :], window)
    new = lax.broadcasted_iota(jnp.int32, (pairs, pairs), 0)
    old = lax.broadcasted_iota(jnp.int32, (pairs, pairs), 1)
    half = pairs // 2
    chips = half // 2
    side = jnp.where(new < half, core, 1 - core)
    in_half = jnp.where(new < half, new, new - half)
    row = jnp.where(in_half < chips, 0, 1)
    chip = jnp.where(in_half < chips, in_half, in_half - chips)
    pick = jnp.where(old == 4 * chip + 2 * side + row, 1.0, 0.0).astype(BF16)
    left = jnp.concatenate(
        [
            lax.dot_general(
                pick,
                rows_ref[pl.ds(step * 256, 256), :].astype(BF16),
                NT,
                preferred_element_type=F32,
            ).astype(BF16)
            for step in range(width // 256)
        ],
        axis=1,
    )
    for step, amps in enumerate((amps0, amps1, amps2, amps3)):
        block = lax.rem(group + step, 4)
        product = jnp.dot(left, amps[...], preferred_element_type=F32)
        result[:, pl.ds(pl.multiple_of(block * 256, 256), 256)] = product
    for target, at in ((kept, 0), (given, half)):
        for r in range(2):
            for j in range(8):
                target[pl.ds(r * 8 + j, chips, stride=16), :] = result[
                    at + r * chips:at + (r + 1) * chips, j * 128:(j + 1) * 128
                ]


def body(amplitudes, owned_columns, ladder_ints):
    device = lax.axis_index("cd")
    group = lax.axis_index("ij")
    devices_cd = lax.axis_size("cd")
    width, pairs_ij = amplitudes.shape
    pairs_ab, slot_total = ladder_ints.shape
    capacity = 2 * width // devices_cd
    base = device * width
    params = pltpu.CompilerParams(vmem_limit_bytes=VMEM_LIMIT)
    smem = pl.BlockSpec(memory_space=pltpu.SMEM)

    own_row = lax.dynamic_index_in_dim(owned_columns, device, 0, keepdims=False)
    range_starts = jnp.arange(devices_cd, dtype=jnp.int32) * width
    starts = jnp.sum(
        (own_row >= 0)[None, :] & (own_row[None, :] < range_starts[:, None]), axis=1, dtype=jnp.int32
    )
    outgoing = pl.pallas_call(
        pack_kernel,
        out_shape=jax.ShapeDtypeStruct((devices_cd, capacity, pairs_ab), BF16),
        in_specs=[smem, vmem_spec()],
        out_specs=vmem_spec(),
        scratch_shapes=[pltpu.VMEM((slot_total + capacity + 8, pairs_ab), F32)],
        compiler_params=params,
        name="pack",
    )(starts, ladder_ints)
    incoming = lax.all_to_all(outgoing, "cd", split_axis=0, concat_axis=0, tiled=True)

    ordered, offsets = pl.pallas_call(
        lambda *refs: order_kernel(capacity, *refs),
        out_shape=[
            jax.ShapeDtypeStruct((width, pairs_ij), BF16),
            jax.ShapeDtypeStruct((devices_cd, 128), jnp.int32),
        ],
        in_specs=[smem, vmem_spec(), vmem_spec()],
        out_specs=[vmem_spec(), vmem_spec()],
        compiler_params=params,
        name="order",
    )(base[None].astype(jnp.int32), owned_columns, amplitudes)
    groups = lax.axis_size("ij")
    others = [
        lax.ppermute(ordered, "ij", [((i + step) % groups, i) for i in range(groups)])
        for step in range(1, groups)
    ]
    core = lax.rem(device, 2)
    half = pairs_ab // 2
    kept, given = pl.pallas_call(
        multiply_kernel,
        out_shape=[jax.ShapeDtypeStruct((8 * pairs_ab // 2 // 2 * 2, 128), F32)] * 2,
        in_specs=[smem, smem] + [vmem_spec()] * 5,
        out_specs=[vmem_spec(), vmem_spec()],
        scratch_shapes=[
            pltpu.VMEM((width + capacity + 8, pairs_ab), F32),
            pltpu.VMEM((pairs_ab, groups * pairs_ij), F32),
        ],
        compiler_params=params,
        name="multiply",
    )(offsets[:, 0], jnp.stack([group, core]).astype(jnp.int32), incoming, ordered, *others)
    taken = lax.ppermute(given, "cd", [(i, i ^ 1) for i in range(devices_cd)])
    both = (kept + taken).reshape(devices_cd // 2, 16, 128)
    same_core = [[2 * k + c for k in range(devices_cd // 2)] for c in range(2)]
    shares = lax.all_to_all(both, "cd", 0, 0, tiled=True, axis_index_groups=same_core)
    summed = jnp.sum(shares, axis=0)
    return summed.astype(BF16).reshape(2, 1024)


def solution(mesh):
    return jax.shard_map(
        body,
        mesh=mesh,
        in_specs=(P("cd", "ij"), P(), P("ij", "cd")),
        out_specs=P(("ij", "cd"), None),
        check_vma=False,
    )
```

time: 609 us -> 99 us (0.16)
  the two profiles are of different devices: /device:TPU:2 before, /device:TPU:16 now
where the time goes in v1:
time: 99 us; the launch traced here: 98.6 us
  blocking collectives  32.4 us (33%)
  starting transfers between devices  29.6 us (30%)
  waiting for transfers between devices  24.5 us (25%)
  Pallas kernels  8.81 us (9%)
  local copies, waits for them, and re-layouts  1.94 us (2%)
  other arithmetic  1.38 us (1%)
    all_to_all x1, blocking collectives, body(): lax.all_to_all(both, 'cd', 0, 0, tiled=True, axis_index_groups=same_core)  32.4 us
    ppermute x3, waiting for transfers between devices, body(): lax.ppermute(ordered, 'ij', [((i + step) % groups, i) for i in range(grou...  22.6 us
    all_to_all x1, starting transfers between devices, body(): lax.all_to_all(outgoing, 'cd', split_axis=0, concat_axis=0, tiled=True)  17.5 us
    ppermute x3, starting transfers between devices, body(): lax.ppermute(ordered, 'ij', [((i + step) % groups, i) for i in range(grou...  10.2 us
    pallas_call x1, Pallas kernels, body(): pl.pallas_call(lambda *refs: order_kernel(capacity, *refs), out_shape=[ja...  2.96 us
    pallas_call x1, Pallas kernels, body(): pl.pallas_call(pack_kernel, out_shape=jax.ShapeDtypeStruct((devices_cd, c...  2.94 us
    pallas_call x1, Pallas kernels, body(): pl.pallas_call(multiply_kernel, out_shape=[jax.ShapeDtypeStruct((8 * pair...  2.92 us
  transfers between devices with their start and end apart: 5, of which 3 were waited for; matrix products, arithmetic and copies ran while one was open for 0% of the time, Pallas kernels for 3%

profile of v1, /device:TPU:16, one launch (start us, length us, event | category | flops | bytes accessed | tf_op | source)
XLA Modules:
  0.0 98.6 jit_solution(18194097315627339194)
XLA Ops:
  0.0 0.9 compare_reduce_fusion
  0.9 0.3 convert_reduce_fusion.starts
  1.2 0.0 copy-start.1
  1.2 1.2 %copy-done.1 = bf16[256,2048]{1,0:T(8,128)(2,1)S(1)} copy-done((bf16[256,2048]{1,0:T(8,128)(2,1)S(1)}, bf16[256,2048]{1,0:T(8,128)(2,1)}, u32[]{:S(2)}) %copy-start.1) | copy-done | bytes 1048600
  2.4 2.9 %pack.1 = bf16[128,16,256]{2,1,0:T(8,128)(2,1)} custom-call(s32[128]{0:T(128)S(1)} %convert_reduce_fusion.starts, bf16[256,2048]{1,0:T(8,128)(2,1)S(1)} %copy-done.1), custom_call_target="tpu_custom_call" | custom-call | tf_op jit(solution)/shard_map/pack/pallas_call | solution.py:154
  5.3 0.0 copy-start
  5.3 0.0 copy-start.2
  5.3 17.5 %all-to-all-start = ((bf16[128,16,256]{2,1,0:T(8,128)(2,1)}), bf16[128,16,256]{2,1,0:T(8,128)(2,1)S(1)}, u32[]{:S(2)}, u32[]{:S(2)}) async-start(bf16[128,16,256]{2,1,0:T(8,128)(2,1)} %pack.1), calls=%async_computation | async-start | bytes 2097152 | tf_op jit(solution)/shard_map/all_to_all | solution.py:163
  22.8 0.0 copy-done
  22.8 0.0 copy-done.2
  22.8 3.0 %order.1 = (bf16[1024,256]{1,0:T(8,128)(2,1)S(1)}, s32[128,128]{1,0:T(8,128)S(1)}) custom-call(s32[1]{0:T(128)} %bitcast.refs_0_, s32[128,2048]{1,0:T(8,128)S(1)} %copy-done, bf16[1024,256]{1,0:T(8,128)(2,1)S(1)} %copy-done.2), custom_call_target="tpu_custom_call" | custom-call | tf_op jit(solution)/shard_map/order/pallas_call | solution.py:165
  25.8 4.7 %collective-permute-start = (bf16[1024,256]{1,0:T(8,128)(2,1)S(1)}, bf16[1024,256]{1,0:T(8,128)(2,1)S(1)}, u32[]{:S(2)}, u32[]{:S(2)}) collective-permute-start(bf16[1024,256]{1,0:T(8,128)(2,1)S(1)} %get-tuple-element.10.amps0), channel_id=1, source_target_pairs={{128,0},{256,128},{384,256},{0,384},{129,1},{257,129},{385,257},{1... | collective-permute-start | bytes 1572872 | tf_op jit(solution)/shard_map/ppermute | solution.py:178
  30.5 2.7 %collective-permute-start.1 = (bf16[1024,256]{1,0:T(8,128)(2,1)S(1)}, bf16[1024,256]{1,0:T(8,128)(2,1)S(1)}, u32[]{:S(2)}, u32[]{:S(2)}) collective-permute-start(bf16[1024,256]{1,0:T(8,128)(2,1)S(1)} %get-tuple-element.10.amps0), channel_id=1, source_target_pairs={{256,0},{384,128},{0,256},{128,384},{257,1},{385,129},{1,257},{129... | collective-permute-start | bytes 1572872 | tf_op jit(solution)/shard_map/ppermute | solution.py:178
  33.2 2.8 %collective-permute-start.2 = (bf16[1024,256]{1,0:T(8,128)(2,1)S(1)}, bf16[1024,256]{1,0:T(8,128)(2,1)S(1)}, u32[]{:S(2)}, u32[]{:S(2)}) collective-permute-start(bf16[1024,256]{1,0:T(8,128)(2,1)S(1)} %get-tuple-element.10.amps0), channel_id=1, source_target_pairs={{384,0},{0,128},{128,256},{256,384},{385,1},{1,129},{129,257},{257... | collective-permute-start | bytes 1572872 | tf_op jit(solution)/shard_map/ppermute | solution.py:178
  36.0 0.1 pad_add_fusion.where_ref
  36.1 0.1 slice_reduce_fusion.offsets
  36.2 17.0 %collective-permute-done.amps1 = bf16[1024,256]{1,0:T(8,128)(2,1)S(1)} collective-permute-done((bf16[1024,256]{1,0:T(8,128)(2,1)S(1)}, bf16[1024,256]{1,0:T(8,128)(2,1)S(1)}, u32[]{:S(2)}, u32[]{:S(2)}) %collective-permute-start) | collective-permute-done | bytes 524320 | tf_op jit(solution)/shard_map/ppermute | solution.py:178
  53.2 0.0 collective-permute-done.1.amps2
  53.2 5.6 %collective-permute-done.2.amps3 = bf16[1024,256]{1,0:T(8,128)(2,1)S(1)} collective-permute-done((bf16[1024,256]{1,0:T(8,128)(2,1)S(1)}, bf16[1024,256]{1,0:T(8,128)(2,1)S(1)}, u32[]{:S(2)}, u32[]{:S(2)}) %collective-permute-start.2) | collective-permute-done | bytes 524320 | tf_op jit(solution)/shard_map/ppermute | solution.py:178
  58.8 0.0 all-to-all-done.received
  58.8 2.9 %multiply.1 = (f32[1024,128]{1,0:T(8,128)S(1)}, f32[1024,128]{1,0:T(8,128)S(1)}) custom-call(s32[128]{0:T(128)S(1)} %slice_reduce_fusion.offsets, s32[2]{0:T(128)S(1)} %pad_add_fusion.where_ref, bf16[128,16,256]{2,1,0:T(8,128)(2,1)S(1)} %all-to-all-done.received, bf16[1024,256]{1,0:T(8,128)(2,1)S(1)} %get-tuple-element.10.amps0, ...), custom_call_target="tpu_custom_call" | custom-call | tf_op jit(solution)/shard_map/multiply/pallas_call | solution.py:183
  61.7 1.9 %collective-permute-start.3 = (f32[1024,128]{1,0:T(8,128)S(1)}, f32[1024,128]{1,0:T(8,128)S(1)}, u32[]{:S(2)}, u32[]{:S(2)}) collective-permute-start(f32[1024,128]{1,0:T(8,128)S(1)} %get-tuple-element.12), channel_id=1, source_target_pairs={{0,1},{1,0},{2,3},{3,2},{4,5},{5,4},{6,7},{7,6},{8,9},{9,8},{10,11... | collective-permute-start | bytes 1572872 | tf_op jit(solution)/shard_map/ppermute | solution.py:195
  63.7 1.9 %collective-permute-done.3 = f32[1024,128]{1,0:T(8,128)S(1)} collective-permute-done((f32[1024,128]{1,0:T(8,128)S(1)}, f32[1024,128]{1,0:T(8,128)S(1)}, u32[]{:S(2)}, u32[]{:S(2)}) %collective-permute-start.3) | collective-permute-done | bytes 524320 | tf_op jit(solution)/shard_map/ppermute | solution.py:195
  65.5 0.1 add.8
  65.6 32.4 %all_to_all.10 = f32[64,16,128]{2,1,0:T(8,128)S(1)} all-to-all(f32[64,16,128]{2,1,0:T(8,128)S(1)} %bitcast.5), channel_id=1, replica_groups={{0,2,4,6,8,10,12,14,16,18,20,22,24,26,28,30,32,34,36,38,40,42,44,46,48,..., dimensions={0} | all-to-all | bytes 1048576 | tf_op jit(solution)/shard_map/all_to_all | solution.py:198
  98.0 0.1 reduce_sum.19
  98.0 0.6 convert_element_type.12
  (1 shorter events, 0.0 us)
Async XLA Ops:
  1.2 1.2 %copy-start.1 = (bf16[256,2048]{1,0:T(8,128)(2,1)S(1)}, bf16[256,2048]{1,0:T(8,128)(2,1)}, u32[]{:S(2)}) copy-start(bf16[256,2048]{1,0:T(8,128)(2,1)} %ints.1) | copy-start | bytes 3145732
  5.3 17.5 %copy-start = (s32[128,2048]{1,0:T(8,128)S(1)}, s32[128,2048]{1,0:T(8,128)}, u32[]{:S(2)}) copy-start(s32[128,2048]{1,0:T(8,128)} %refs_1_.1) | copy-start | bytes 3145732
  5.3 17.5 %copy-start.2 = (bf16[1024,256]{1,0:T(8,128)(2,1)S(1)}, bf16[1024,256]{1,0:T(8,128)(2,1)}, u32[]{:S(2)}) copy-start(bf16[1024,256]{1,0:T(8,128)(2,1)} %refs_2_.1) | copy-start | bytes 1572868
  5.3 53.5 %all-to-all-start = ((bf16[128,16,256]{2,1,0:T(8,128)(2,1)}), bf16[128,16,256]{2,1,0:T(8,128)(2,1)S(1)}, u32[]{:S(2)}, u32[]{:S(2)}) async-start(bf16[128,16,256]{2,1,0:T(8,128)(2,1)} %pack.1), calls=%async_computation | async-start | bytes 2097152 | tf_op jit(solution)/shard_map/all_to_all | solution.py:163
  25.8 27.4 %collective-permute-start = (bf16[1024,256]{1,0:T(8,128)(2,1)S(1)}, bf16[1024,256]{1,0:T(8,128)(2,1)S(1)}, u32[]{:S(2)}, u32[]{:S(2)}) collective-permute-start(bf16[1024,256]{1,0:T(8,128)(2,1)S(1)} %get-tuple-element.10.amps0), channel_id=1, source_target_pairs={{128,0},{256,128},{384,256},{0,384},{129,1},{257,129},{385,257},{1... | collective-permute-start | bytes 1572872 | tf_op jit(solution)/shard_map/ppermute | solution.py:178
  30.5 22.7 %collective-permute-start.1 = (bf16[1024,256]{1,0:T(8,128)(2,1)S(1)}, bf16[1024,256]{1,0:T(8,128)(2,1)S(1)}, u32[]{:S(2)}, u32[]{:S(2)}) collective-permute-start(bf16[1024,256]{1,0:T(8,128)(2,1)S(1)} %get-tuple-element.10.amps0), channel_id=1, source_target_pairs={{256,0},{384,128},{0,256},{128,384},{257,1},{385,129},{1,257},{129... | collective-permute-start | bytes 1572872 | tf_op jit(solution)/shard_map/ppermute | solution.py:178
  33.2 25.6 %collective-permute-start.2 = (bf16[1024,256]{1,0:T(8,128)(2,1)S(1)}, bf16[1024,256]{1,0:T(8,128)(2,1)S(1)}, u32[]{:S(2)}, u32[]{:S(2)}) collective-permute-start(bf16[1024,256]{1,0:T(8,128)(2,1)S(1)} %get-tuple-element.10.amps0), channel_id=1, source_target_pairs={{384,0},{0,128},{128,256},{256,384},{385,1},{1,129},{129,257},{257... | collective-permute-start | bytes 1572872 | tf_op jit(solution)/shard_map/ppermute | solution.py:178
  61.7 3.8 %collective-permute-start.3 = (f32[1024,128]{1,0:T(8,128)S(1)}, f32[1024,128]{1,0:T(8,128)S(1)}, u32[]{:S(2)}, u32[]{:S(2)}) collective-permute-start(f32[1024,128]{1,0:T(8,128)S(1)} %get-tuple-element.12), channel_id=1, source_target_pairs={{0,1},{1,0},{2,3},{3,2},{4,5},{5,4},{6,7},{7,6},{8,9},{9,8},{10,11... | collective-permute-start | bytes 1572872 | tf_op jit(solution)/shard_map/ppermute | solution.py:195

commit v2 on v1

v2 whole, which is shorter than its diff:
```python
import jax
import jax.numpy as jnp
from jax import lax
from jax.experimental import pallas as pl
from jax.experimental.pallas import tpu as pltpu
from jax.sharding import PartitionSpec as P

F32 = jnp.float32
BF16 = jnp.bfloat16
NT = (((1,), (1,)), ((), ()))
VMEM_LIMIT = 48 * 1024 * 1024


def vmem_spec():
    return pl.BlockSpec(memory_space=pltpu.VMEM)


def identity(size):
    rows = lax.broadcasted_iota(jnp.int32, (size, size), 0)
    cols = lax.broadcasted_iota(jnp.int32, (size, size), 1)
    return jnp.where(rows == cols, 1.0, 0.0).astype(BF16)


def pack_kernel(starts, ints, out, slots):
    capacity = out.shape[1]
    total, chunk = ints.shape[1], 256
    eye = identity(chunk)
    for step in range(total // chunk):
        at = pl.ds(step * chunk, chunk)
        slots[at, :] = lax.dot_general(eye, ints[:, at], NT, preferred_element_type=F32)
    slots[pl.ds(total, capacity + 8), :] = jnp.zeros((capacity + 8, slots.shape[1]), F32)
    for dest in range(out.shape[0]):
        start = starts[dest]
        aligned = pl.multiple_of((start // 8) * 8, 8)
        window = slots[pl.ds(aligned, capacity + 8), :]
        window = pltpu.roll(window, capacity + 8 - (start - aligned), 0)
        out[dest] = window[:capacity].astype(BF16)


def order_kernel(capacity, base_ref, owned, out):
    base = base_ref[0]
    holders, total = owned.shape
    width = out.shape[0]
    beyond = jnp.int32(1 << 30)
    table = owned[...]
    table = jnp.where(table < 0, beyond, table - base)
    below = jnp.zeros((holders, 128), F32)
    for tile in range(total // 128):
        below = below + jnp.where(table[:, tile * 128:(tile + 1) * 128] < 0, 1.0, 0.0)
    ones = jnp.ones((128, 128), BF16)
    start = jnp.dot(below.astype(BF16), ones, preferred_element_type=F32).astype(jnp.int32)
    window = jnp.concatenate([table, jnp.full((holders, 128), beyond, jnp.int32)], axis=1)
    shift = total // 2
    while shift >= 128:
        keep = shift + 128
        taken = (start & shift) != 0
        taken = jnp.concatenate([taken] * (keep // 128), axis=1)
        window = jnp.where(taken, window[:, shift:shift + keep], window[:, :keep])
        shift //= 2
    while shift >= 1:
        taken = (start & shift) != 0
        taken = jnp.concatenate([taken, taken], axis=1)
        window = jnp.where(taken, pltpu.roll(window, 256 - shift, 1), window)
        shift //= 2
    lane = lax.broadcasted_iota(jnp.int32, (holders, 128), 1)
    spread = jnp.where(lane < capacity, window[:, :128], 0)
    shift = capacity
    while shift < 128:
        spread = spread + pltpu.roll(spread, shift, 1)
        shift *= 2
    each = 128 // capacity
    mine = lax.broadcasted_iota(jnp.int32, (each, 128), 0)
    mine = mine == lax.broadcasted_iota(jnp.int32, (each, 128), 1) // capacity
    columns = jnp.concatenate(
        [
            jnp.sum(jnp.where(mine, spread[at:at + each], 0), axis=0, keepdims=True)
            for at in range(0, holders, each)
        ],
        axis=1,
    )
    chunk = 128
    for step in range(width // chunk):
        wanted = lax.broadcasted_iota(jnp.int32, (chunk, holders * capacity), 0) + step * chunk
        out[pl.ds(step * chunk, chunk), :] = jnp.where(wanted == columns, 1.0, 0.0).astype(BF16)


def multiply_kernel(where_ref, received, order, amps0, amps1, amps2, amps3, kept, given, result):
    group, core = where_ref[0], where_ref[1]
    holders, capacity, pairs = received.shape
    new = lax.broadcasted_iota(jnp.int32, (pairs, pairs), 0)
    old = lax.broadcasted_iota(jnp.int32, (pairs, pairs), 1)
    half = pairs // 2
    chips = half // 2
    side = jnp.where(new < half, core, 1 - core)
    in_half = jnp.where(new < half, new, new - half)
    row = jnp.where(in_half < chips, 0, 1)
    chip = jnp.where(in_half < chips, in_half, in_half - chips)
    pick = jnp.where(old == 4 * chip + 2 * side + row, 1.0, 0.0).astype(BF16)
    columns = received[...].reshape(holders * capacity, pairs)
    slots = lax.dot_general(pick, columns, NT, preferred_element_type=F32).astype(BF16)
    left = lax.dot_general(slots, order[...], NT, preferred_element_type=F32).astype(BF16)
    for step, amps in enumerate((amps0, amps1, amps2, amps3)):
        block = lax.rem(group + step, 4)
        product = jnp.dot(left, amps[...], preferred_element_type=F32)
        result[:, pl.ds(pl.multiple_of(block * 256, 256), 256)] = product
    for target, at in ((kept, 0), (given, half)):
        for r in range(2):
            for j in range(8):
                target[pl.ds(r * 8 + j, chips, stride=16), :] = result[
                    at + r * chips:at + (r + 1) * chips, j * 128:(j + 1) * 128
                ]


def body(amplitudes, owned_columns, ladder_ints):
    device = lax.axis_index("cd")
    group = lax.axis_index("ij")
    devices_cd = lax.axis_size("cd")
    width, pairs_ij = amplitudes.shape
    pairs_ab, slot_total = ladder_ints.shape
    capacity = 2 * width // devices_cd
    base = device * width
    params = pltpu.CompilerParams(vmem_limit_bytes=VMEM_LIMIT)
    smem = pl.BlockSpec(memory_space=pltpu.SMEM)

    own_row = lax.dynamic_index_in_dim(owned_columns, device, 0, keepdims=False)
    range_starts = jnp.arange(devices_cd, dtype=jnp.int32) * width
    starts = jnp.sum(
        (own_row >= 0)[None, :] & (own_row[None, :] < range_starts[:, None]), axis=1, dtype=jnp.int32
    )
    outgoing = pl.pallas_call(
        pack_kernel,
        out_shape=jax.ShapeDtypeStruct((devices_cd, capacity, pairs_ab), BF16),
        in_specs=[smem, vmem_spec()],
        out_specs=vmem_spec(),
        scratch_shapes=[pltpu.VMEM((slot_total + capacity + 8, pairs_ab), F32)],
        compiler_params=params,
        name="pack",
    )(starts, ladder_ints)
    incoming = lax.all_to_all(outgoing, "cd", split_axis=0, concat_axis=0, tiled=True)

    order = pl.pallas_call(
        lambda *refs: order_kernel(capacity, *refs),
        out_shape=jax.ShapeDtypeStruct((width, devices_cd * capacity), BF16),
        in_specs=[smem, vmem_spec()],
        out_specs=vmem_spec(),
        compiler_params=params,
        name="order",
    )(base[None].astype(jnp.int32), owned_columns)
    groups = lax.axis_size("ij")
    others = [
        lax.ppermute(amplitudes, "ij", [((i + step) % groups, i) for i in range(groups)])
        for step in range(1, groups)
    ]
    core = lax.rem(device, 2)
    half = pairs_ab // 2
    kept, given = pl.pallas_call(
        multiply_kernel,
        out_shape=[jax.ShapeDtypeStruct((half * groups * pairs_ij // 128, 128), F32)] * 2,
        in_specs=[smem] + [vmem_spec()] * 6,
        out_specs=[vmem_spec(), vmem_spec()],
        scratch_shapes=[pltpu.VMEM((pairs_ab, groups * pairs_ij), F32)],
        compiler_params=params,
        name="multiply",
    )(jnp.stack([group, core]).astype(jnp.int32), incoming, order, amplitudes, *others)
    taken = lax.ppermute(given, "cd", [(i, i ^ 1) for i in range(devices_cd)])
    both = (kept + taken).reshape(devices_cd // 2, 16, 128)
    same_core = [[2 * k + c for k in range(devices_cd // 2)] for c in range(2)]
    shares = lax.all_to_all(both, "cd", 0, 0, tiled=True, axis_index_groups=same_core)
    summed = jnp.sum(shares, axis=0)
    return summed.astype(BF16).reshape(2, 1024)


def solution(mesh):
    return jax.shard_map(
        body,
        mesh=mesh,
        in_specs=(P("cd", "ij"), P(), P("ij", "cd")),
        out_specs=P(("ij", "cd"), None),
        check_vma=False,
    )
```

time: 99 us -> 93.8 us (0.947)
  waiting for transfers between devices: 24.5 us -> 16.5 us
  local copies, waits for them, and re-layouts: 1.94 us -> 3.77 us
  Pallas kernels: 8.81 us -> 9.88 us
    ppermute x3, waiting for transfers between devices: 22.6 us -> 13.9 us  [body(): lax.ppermute(amplitudes, 'ij', [((i + step) % groups, i) for i in range(g...]
    unnamed x6 -> x8, local copies, waits for them, and re-layouts: 1.23 us -> 3.17 us
    pallas_call x2, Pallas kernels: 5.87 us -> 6.97 us  [the longest x1 4.9 us: body(): pl.pallas_call(multiply_kernel, out_shape=[jax.ShapeDtypeStruct((half * g...]
  transfers between devices with their start and end apart: 5 -> 5, of which waited for: 3 -> 4; matrix products, arithmetic and copies ran while one was open for 0% -> 0% of each run, Pallas kernels for 3% -> 2%
where the time goes in v2:
time: 93.8 us; the launch traced here: 93.4 us
  blocking collectives  31.7 us (34%)
  starting transfers between devices  30 us (32%)
  waiting for transfers between devices  16.5 us (18%)
  Pallas kernels  9.88 us (11%)
  local copies, waits for them, and re-layouts  3.77 us (4%)
  other arithmetic  1.45 us (2%)
    all_to_all x1, blocking collectives, body(): lax.all_to_all(both, 'cd', 0, 0, tiled=True, axis_index_groups=same_core)  31.7 us
    all_to_all x1, starting transfers between devices, body(): lax.all_to_all(outgoing, 'cd', split_axis=0, concat_axis=0, tiled=True)  17.4 us
    ppermute x3, waiting for transfers between devices, body(): lax.ppermute(amplitudes, 'ij', [((i + step) % groups, i) for i in range(g...  13.9 us
    ppermute x3, starting transfers between devices, body(): lax.ppermute(amplitudes, 'ij', [((i + step) % groups, i) for i in range(g...  10.8 us
    pallas_call x1, Pallas kernels, body(): pl.pallas_call(multiply_kernel, out_shape=[jax.ShapeDtypeStruct((half * g...  4.9 us
    unnamed x8, local copies, waits for them, and re-layouts  3.17 us
    pallas_call x1, Pallas kernels, body(): pl.pallas_call(pack_kernel, out_shape=jax.ShapeDtypeStruct((devices_cd, c...  2.91 us
    pallas_call x1, Pallas kernels, body(): pl.pallas_call(lambda *refs: order_kernel(capacity, *refs), out_shape=jax...  2.07 us
  transfers between devices with their start and end apart: 5, of which 4 were waited for; matrix products, arithmetic and copies ran while one was open for 0% of the time, Pallas kernels for 2%

profile of v2, /device:TPU:16, one launch (start us, length us, event | category | flops | bytes accessed | tf_op | source)
XLA Modules:
  0.0 93.4 jit_solution(6452245902503633334)
XLA Ops:
  0.0 0.0 copy-start.1
  0.0 1.0 %compare_reduce_fusion = (pred[2048]{0:T(1024)(128)(4,1)S(1)}, s32[1,2048]{1,0:T(1,128)S(1)}) fusion(s32[128,2048]{1,0:T(8,128)} %refs_1_.1, s32[]{:T(128)S(6)} %select_n.4), kind=kLoop, calls=%fused_computation.1 | loop fusion | flops 2048 | bytes 18436 | tf_op jit(solution)/shard_map/ge | solution.py:128
  1.0 0.3 convert_reduce_fusion.starts
  1.3 0.0 copy-start.2
  1.3 1.2 %copy-done.2 = bf16[256,2048]{1,0:T(8,128)(2,1)S(1)} copy-done((bf16[256,2048]{1,0:T(8,128)(2,1)S(1)}, bf16[256,2048]{1,0:T(8,128)(2,1)}, u32[]{:S(2)}) %copy-start.2) | copy-done | bytes 1048600
  2.5 0.0 copy-start.3
  2.5 2.9 %pack.1 = bf16[128,16,256]{2,1,0:T(8,128)(2,1)} custom-call(s32[128]{0:T(128)S(1)} %convert_reduce_fusion.starts, bf16[256,2048]{1,0:T(8,128)(2,1)S(1)} %copy-done.2), custom_call_target="tpu_custom_call" | custom-call | tf_op jit(solution)/shard_map/pack/pallas_call | solution.py:130
  5.4 17.4 %all-to-all-start = ((bf16[128,16,256]{2,1,0:T(8,128)(2,1)}), bf16[128,16,256]{2,1,0:T(8,128)(2,1)S(1)}, u32[]{:S(2)}, u32[]{:S(2)}) async-start(bf16[128,16,256]{2,1,0:T(8,128)(2,1)} %pack.1), calls=%async_computation | async-start | bytes 2097152 | tf_op jit(solution)/shard_map/all_to_all | solution.py:139
  22.8 0.0 copy-done.3
  22.8 4.9 %collective-permute-start.1 = (bf16[1024,256]{1,0:T(8,128)(2,1)S(1)}, bf16[1024,256]{1,0:T(8,128)(2,1)S(1)}, u32[]{:S(2)}, u32[]{:S(2)}) collective-permute-start(bf16[1024,256]{1,0:T(8,128)(2,1)S(1)} %copy-done.3), channel_id=1, source_target_pairs={{256,0},{384,128},{0,256},{128,384},{257,1},{385,129},{1,257},{129... | collective-permute-start | bytes 1572872 | tf_op jit(solution)/shard_map/ppermute | solution.py:151
  27.7 3.1 %collective-permute-start = (bf16[1024,256]{1,0:T(8,128)(2,1)S(1)}, bf16[1024,256]{1,0:T(8,128)(2,1)}, u32[]{:S(2)}, u32[]{:S(2)}) collective-permute-start(bf16[1024,256]{1,0:T(8,128)(2,1)S(1)} %copy-done.3), channel_id=1, source_target_pairs={{128,0},{256,128},{384,256},{0,384},{129,1},{257,129},{385,257},{1... | collective-permute-start | bytes 1572872 | tf_op jit(solution)/shard_map/ppermute | solution.py:151
  30.8 2.8 %collective-permute-start.2 = (bf16[1024,256]{1,0:T(8,128)(2,1)S(1)}, bf16[1024,256]{1,0:T(8,128)(2,1)}, u32[]{:S(2)}, u32[]{:S(2)}) collective-permute-start(bf16[1024,256]{1,0:T(8,128)(2,1)S(1)} %copy-done.3), channel_id=1, source_target_pairs={{384,0},{0,128},{128,256},{256,384},{385,1},{1,129},{129,257},{257... | collective-permute-start | bytes 1572872 | tf_op jit(solution)/shard_map/ppermute | solution.py:151
  33.6 0.0 copy-done.1
  33.6 2.1 %order.1 = bf16[1024,2048]{1,0:T(8,128)(2,1)S(1)} custom-call(s32[1]{0:T(128)} %bitcast.3.refs_0_, s32[128,2048]{1,0:T(8,128)S(1)} %copy-done.1), custom_call_target="tpu_custom_call" | custom-call | tf_op jit(solution)/shard_map/order/pallas_call | solution.py:141
  35.7 0.0 copy-start
  35.7 1.9 %copy-done = bf16[1024,2048]{1,0:T(8,128)(2,1)} copy-done((bf16[1024,2048]{1,0:T(8,128)(2,1)}, bf16[1024,2048]{1,0:T(8,128)(2,1)S(1)}, u32[]{:S(2)}) %copy-start) | copy-done | bytes 4194328
  37.6 0.1 pad_add_fusion.where_ref
  37.7 3.3 %collective-permute-done.1.amps2 = bf16[1024,256]{1,0:T(8,128)(2,1)S(1)} collective-permute-done((bf16[1024,256]{1,0:T(8,128)(2,1)S(1)}, bf16[1024,256]{1,0:T(8,128)(2,1)S(1)}, u32[]{:S(2)}, u32[]{:S(2)}) %collective-permute-start.1) | collective-permute-done | bytes 524320 | tf_op jit(solution)/shard_map/ppermute | solution.py:151
  41.0 10.6 %collective-permute-done.amps1 = bf16[1024,256]{1,0:T(8,128)(2,1)} collective-permute-done((bf16[1024,256]{1,0:T(8,128)(2,1)S(1)}, bf16[1024,256]{1,0:T(8,128)(2,1)}, u32[]{:S(2)}, u32[]{:S(2)}) %collective-permute-start) | collective-permute-done | bytes 524320 | tf_op jit(solution)/shard_map/ppermute | solution.py:151
  51.6 0.0 collective-permute-done.2.amps3
  51.6 0.7 all-to-all-done.received
  52.3 4.9 %multiply.1 = (f32[1024,128]{1,0:T(8,128)S(1)}, f32[1024,128]{1,0:T(8,128)S(1)}) custom-call(s32[2]{0:T(128)S(1)} %pad_add_fusion.where_ref, bf16[128,16,256]{2,1,0:T(8,128)(2,1)S(1)} %all-to-all-done.received, bf16[1024,2048]{1,0:T(8,128)(2,1)} %copy-done, bf16[1024,256]{1,0:T(8,128)(2,1)S(1)} %copy-done.3, bf16[1024,256]{1,0:T(8,128)(2,1)} %collective-permute-done.amps1, ...), custom_call_target="tpu_custom_call" | custom-call | tf_op jit(solution)/shard_map/multiply/pallas_call | solution.py:156
  57.2 1.9 %collective-permute-start.3 = (f32[1024,128]{1,0:T(8,128)S(1)}, f32[1024,128]{1,0:T(8,128)S(1)}, u32[]{:S(2)}, u32[]{:S(2)}) collective-permute-start(f32[1024,128]{1,0:T(8,128)S(1)} %get-tuple-element.8), channel_id=1, source_target_pairs={{0,1},{1,0},{2,3},{3,2},{4,5},{5,4},{6,7},{7,6},{8,9},{9,8},{10,11... | collective-permute-start | bytes 1572872 | tf_op jit(solution)/shard_map/ppermute | solution.py:165
  59.1 1.9 %collective-permute-done.3 = f32[1024,128]{1,0:T(8,128)S(1)} collective-permute-done((f32[1024,128]{1,0:T(8,128)S(1)}, f32[1024,128]{1,0:T(8,128)S(1)}, u32[]{:S(2)}, u32[]{:S(2)}) %collective-permute-start.3) | collective-permute-done | bytes 524320 | tf_op jit(solution)/shard_map/ppermute | solution.py:165
  61.0 0.1 add.8
  61.0 31.7 %all_to_all.10 = f32[64,16,128]{2,1,0:T(8,128)S(1)} all-to-all(f32[64,16,128]{2,1,0:T(8,128)S(1)} %bitcast.5), channel_id=1, replica_groups={{0,2,4,6,8,10,12,14,16,18,20,22,24,26,28,30,32,34,36,38,40,42,44,46,48,..., dimensions={0} | all-to-all | bytes 1048576 | tf_op jit(solution)/shard_map/all_to_all | solution.py:168
  92.8 0.1 reduce_sum.19
  92.8 0.6 convert_element_type.12
  (1 shorter events, 0.0 us)
Async XLA Ops:
  0.0 33.6 %copy-start.1 = (s32[128,2048]{1,0:T(8,128)S(1)}, s32[128,2048]{1,0:T(8,128)}, u32[]{:S(2)}) copy-start(s32[128,2048]{1,0:T(8,128)} %refs_1_.1) | copy-start | bytes 3145732
  1.3 1.2 %copy-start.2 = (bf16[256,2048]{1,0:T(8,128)(2,1)S(1)}, bf16[256,2048]{1,0:T(8,128)(2,1)}, u32[]{:S(2)}) copy-start(bf16[256,2048]{1,0:T(8,128)(2,1)} %ints.1) | copy-start | bytes 3145732
  2.5 20.3 %copy-start.3 = (bf16[1024,256]{1,0:T(8,128)(2,1)S(1)}, bf16[1024,256]{1,0:T(8,128)(2,1)}, u32[]{:S(2)}) copy-start(bf16[1024,256]{1,0:T(8,128)(2,1)} %amps0.1) | copy-start | bytes 1572868
  5.4 46.9 %all-to-all-start = ((bf16[128,16,256]{2,1,0:T(8,128)(2,1)}), bf16[128,16,256]{2,1,0:T(8,128)(2,1)S(1)}, u32[]{:S(2)}, u32[]{:S(2)}) async-start(bf16[128,16,256]{2,1,0:T(8,128)(2,1)} %pack.1), calls=%async_computation | async-start | bytes 2097152 | tf_op jit(solution)/shard_map/all_to_all | solution.py:139
  22.8 18.2 %collective-permute-start.1 = (bf16[1024,256]{1,0:T(8,128)(2,1)S(1)}, bf16[1024,256]{1,0:T(8,128)(2,1)S(1)}, u32[]{:S(2)}, u32[]{:S(2)}) collective-permute-start(bf16[1024,256]{1,0:T(8,128)(2,1)S(1)} %copy-done.3), channel_id=1, source_target_pairs={{256,0},{384,128},{0,256},{128,384},{257,1},{385,129},{1,257},{129... | collective-permute-start | bytes 1572872 | tf_op jit(solution)/shard_map/ppermute | solution.py:151
  27.7 23.9 %collective-permute-start = (bf16[1024,256]{1,0:T(8,128)(2,1)S(1)}, bf16[1024,256]{1,0:T(8,128)(2,1)}, u32[]{:S(2)}, u32[]{:S(2)}) collective-permute-start(bf16[1024,256]{1,0:T(8,128)(2,1)S(1)} %copy-done.3), channel_id=1, source_target_pairs={{128,0},{256,128},{384,256},{0,384},{129,1},{257,129},{385,257},{1... | collective-permute-start | bytes 1572872 | tf_op jit(solution)/shard_map/ppermute | solution.py:151
  30.8 20.8 %collective-permute-start.2 = (bf16[1024,256]{1,0:T(8,128)(2,1)S(1)}, bf16[1024,256]{1,0:T(8,128)(2,1)}, u32[]{:S(2)}, u32[]{:S(2)}) collective-permute-start(bf16[1024,256]{1,0:T(8,128)(2,1)S(1)} %copy-done.3), channel_id=1, source_target_pairs={{384,0},{0,128},{128,256},{256,384},{385,1},{1,129},{129,257},{257... | collective-permute-start | bytes 1572872 | tf_op jit(solution)/shard_map/ppermute | solution.py:151
  35.7 1.9 %copy-start = (bf16[1024,2048]{1,0:T(8,128)(2,1)}, bf16[1024,2048]{1,0:T(8,128)(2,1)S(1)}, u32[]{:S(2)}) copy-start(bf16[1024,2048]{1,0:T(8,128)(2,1)S(1)} %order.1) | copy-start | bytes 12582916
  57.2 3.8 %collective-permute-start.3 = (f32[1024,128]{1,0:T(8,128)S(1)}, f32[1024,128]{1,0:T(8,128)S(1)}, u32[]{:S(2)}, u32[]{:S(2)}) collective-permute-start(f32[1024,128]{1,0:T(8,128)S(1)} %get-tuple-element.8), channel_id=1, source_target_pairs={{0,1},{1,0},{2,3},{3,2},{4,5},{5,4},{6,7},{7,6},{8,9},{9,8},{10,11... | collective-permute-start | bytes 1572872 | tf_op jit(solution)/shard_map/ppermute | solution.py:165

commit v3 on v2

--- a/solution.py
+++ b/solution.py
@@ -8,7 +8,7 @@
 F32 = jnp.float32
 BF16 = jnp.bfloat16
 NT = (((1,), (1,)), ((), ()))
-VMEM_LIMIT = 48 * 1024 * 1024
+VMEM_LIMIT = 24 * 1024 * 1024
 
 
 def vmem_spec():
@@ -21,16 +21,45 @@
     return jnp.where(rows == cols, 1.0, 0.0).astype(BF16)
 
 
-def pack_kernel(starts, ints, out, slots):
-    capacity = out.shape[1]
+def pack_kernel(where_ref, owned, ints, out, group, staged, slots, firsts, starts, sems):
+    device = where_ref[0]
+    devices, capacity, _ = out.shape
     total, chunk = ints.shape[1], 256
+    steps = total // chunk
+    eight = pl.multiple_of((device // 8) * 8, 8)
+    own_copy = pltpu.make_async_copy(owned.at[pl.ds(eight, 8)], group, sems.at[steps])
+    own_copy.start()
+    copies = []
+    for step in range(steps):
+        at = pl.ds(step * chunk, chunk)
+        copies.append(pltpu.make_async_copy(ints.at[:, at], staged.at[:, at], sems.at[step]))
+        copies[-1].start()
+    slots[pl.ds(total, capacity + 8), :] = jnp.zeros((capacity + 8, slots.shape[1]), F32)
+    own_copy.wait()
+    line = lax.broadcasted_iota(jnp.int32, group.shape, 0)
+    row = jnp.sum(jnp.where(line == device - eight, group[...], 0), axis=0, keepdims=True)
+    row = jnp.where(row < 0, jnp.int32(1 << 30), row)
+    width = lax.broadcasted_iota(jnp.int32, (devices, 128), 0) * where_ref[1]
+    before = jnp.zeros((devices, 128), F32)
+    for tile in range(total // 128):
+        before = before + jnp.where(row[:, tile * 128:(tile + 1) * 128] < width, 1.0, 0.0)
+    ones = jnp.ones((128, 128), BF16)
+    before = jnp.dot(before.astype(BF16), ones, preferred_element_type=F32)
+    same = lax.broadcasted_iota(jnp.int32, (devices, 128), 0) == lax.broadcasted_iota(
+        jnp.int32, (devices, 128), 1
+    )
+    first = jnp.sum(jnp.where(same, before, 0.0), axis=0, keepdims=True).astype(jnp.int32)
+    firsts[...] = jnp.broadcast_to(first, firsts.shape)
+    out_copy = pltpu.make_async_copy(firsts, starts, sems.at[steps + 1])
+    out_copy.start()
     eye = identity(chunk)
-    for step in range(total // chunk):
+    for step in range(steps):
         at = pl.ds(step * chunk, chunk)
-        slots[at, :] = lax.dot_general(eye, ints[:, at], NT, preferred_element_type=F32)
-    slots[pl.ds(total, capacity + 8), :] = jnp.zeros((capacity + 8, slots.shape[1]), F32)
-    for dest in range(out.shape[0]):
-        start = starts[dest]
+        copies[step].wait()
+        slots[at, :] = lax.dot_general(eye, staged[:, at], NT, preferred_element_type=F32)
+    out_copy.wait()
+    for dest in range(devices):
+        start = starts[0, dest]
         aligned = pl.multiple_of((start // 8) * 8, 8)
         window = slots[pl.ds(aligned, capacity + 8), :]
         window = pltpu.roll(window, capacity + 8 - (start - aligned), 0)
@@ -111,6 +140,18 @@
                 ]
 
 
+SCALE = 2.0 ** 22
+
+
+def squeeze(value):
+    return (jnp.sign(value) * jnp.sqrt(jnp.abs(value) * SCALE)).astype(jnp.float16)
+
+
+def unsqueeze(root):
+    root = root.astype(F32)
+    return root * jnp.abs(root) * (1.0 / SCALE)
+
+
 def body(amplitudes, owned_columns, ladder_ints):
     device = lax.axis_index("cd")
     group = lax.axis_index("ij")
@@ -122,20 +163,22 @@
     params = pltpu.CompilerParams(vmem_limit_bytes=VMEM_LIMIT)
     smem = pl.BlockSpec(memory_space=pltpu.SMEM)
 
-    own_row = lax.dynamic_index_in_dim(owned_columns, device, 0, keepdims=False)
-    range_starts = jnp.arange(devices_cd, dtype=jnp.int32) * width
-    starts = jnp.sum(
-        (own_row >= 0)[None, :] & (own_row[None, :] < range_starts[:, None]), axis=1, dtype=jnp.int32
-    )
     outgoing = pl.pallas_call(
         pack_kernel,
         out_shape=jax.ShapeDtypeStruct((devices_cd, capacity, pairs_ab), BF16),
-        in_specs=[smem, vmem_spec()],
+        in_specs=[smem] + [pl.BlockSpec(memory_space=pltpu.HBM)] * 2,
         out_specs=vmem_spec(),
-        scratch_shapes=[pltpu.VMEM((slot_total + capacity + 8, pairs_ab), F32)],
+        scratch_shapes=[
+            pltpu.VMEM((8, slot_total), jnp.int32),
+            pltpu.VMEM((pairs_ab, slot_total), BF16),
+            pltpu.VMEM((slot_total + capacity + 8, pairs_ab), F32),
+            pltpu.VMEM((8, 128), jnp.int32),
+            pltpu.SMEM((8, 128), jnp.int32),
+            pltpu.SemaphoreType.DMA((slot_total // 256 + 2,)),
+        ],
         compiler_params=params,
         name="pack",
-    )(starts, ladder_ints)
+    )(jnp.stack([device, jnp.int32(width)]).astype(jnp.int32), owned_columns, ladder_ints)
     incoming = lax.all_to_all(outgoing, "cd", split_axis=0, concat_axis=0, tiled=True)
 
     order = pl.pallas_call(
@@ -163,10 +206,10 @@
         name="multiply",
     )(jnp.stack([group, core]).astype(jnp.int32), incoming, order, amplitudes, *others)
     taken = lax.ppermute(given, "cd", [(i, i ^ 1) for i in range(devices_cd)])
-    both = (kept + taken).reshape(devices_cd // 2, 16, 128)
+    both = squeeze(kept + taken).reshape(devices_cd // 2, 16, 128)
     same_core = [[2 * k + c for k in range(devices_cd // 2)] for c in range(2)]
     shares = lax.all_to_all(both, "cd", 0, 0, tiled=True, axis_index_groups=same_core)
-    summed = jnp.sum(shares, axis=0)
+    summed = jnp.sum(unsqueeze(shares), axis=0)
     return summed.astype(BF16).reshape(2, 1024)
 
 

time: 93.8 us -> 93 us (level)
  the two profiles are of different devices: /device:TPU:16 before, /device:TPU:2 now
where the time goes in v3:
time: 93 us; the launch traced here: 92.6 us
  starting transfers between devices  29.6 us (32%)
  blocking collectives  25.5 us (27%)
  waiting for transfers between devices  18.7 us (20%)
  Pallas kernels  10.8 us (12%)
  local copies, waits for them, and re-layouts  7.19 us (8%)
    all_to_all x1, blocking collectives, body(): lax.all_to_all(both, 'cd', 0, 0, tiled=True, axis_index_groups=same_core)  25.5 us
    all_to_all x1, starting transfers between devices, body(): lax.all_to_all(outgoing, 'cd', split_axis=0, concat_axis=0, tiled=True)  17.8 us
    ppermute x3, waiting for transfers between devices, body(): lax.ppermute(amplitudes, 'ij', [((i + step) % groups, i) for i in range(g...  14.2 us
    ppermute x3, starting transfers between devices, body(): lax.ppermute(amplitudes, 'ij', [((i + step) % groups, i) for i in range(g...  9.88 us
    unnamed x12, local copies, waits for them, and re-layouts  6.59 us
    pallas_call x1, Pallas kernels, body(): pl.pallas_call(pack_kernel, out_shape=jax.ShapeDtypeStruct((devices_cd, c...  5.14 us
    pallas_call x1, Pallas kernels, body(): pl.pallas_call(multiply_kernel, out_shape=[jax.ShapeDtypeStruct((half * g...  3.64 us
    all_to_all x1, waiting for transfers between devices, body(): lax.all_to_all(outgoing, 'cd', split_axis=0, concat_axis=0, tiled=True)  2.61 us
  transfers between devices with their start and end apart: 5, of which 5 were waited for; matrix products, arithmetic and copies ran while one was open for 0% of the time, Pallas kernels for 2%

profile of v3, /device:TPU:2, one launch (start us, length us, event | category | flops | bytes accessed | tf_op | source)
XLA Modules:
  0.0 92.6 jit_solution(12845292609095267735)
XLA Ops:
  0.0 0.1 pad_add_fusion.1.where_ref
  0.1 0.0 copy-start.2
  0.1 1.2 %copy-done.2 = s32[128,2048]{1,0:T(8,128)S(1)} copy-done((s32[128,2048]{1,0:T(8,128)S(1)}, s32[128,2048]{1,0:T(8,128)}, u32[]{:S(2)}) %copy-start.2) | copy-done | bytes 1048600
  1.3 0.0 copy-start.4
  1.3 1.2 %copy-done.4 = bf16[256,2048]{1,0:T(8,128)(2,1)S(1)} copy-done((bf16[256,2048]{1,0:T(8,128)(2,1)S(1)}, bf16[256,2048]{1,0:T(8,128)(2,1)}, u32[]{:S(2)}) %copy-start.4) | copy-done | bytes 1048600
  2.5 0.0 copy-start.5
  2.5 0.0 copy-start.3
  2.5 5.1 %pack.1 = bf16[128,16,256]{2,1,0:T(8,128)(2,1)} custom-call(s32[2]{0:T(128)S(1)} %pad_add_fusion.1.where_ref, s32[128,2048]{1,0:T(8,128)S(1)} %copy-done.2, bf16[256,2048]{1,0:T(8,128)(2,1)S(1)} %copy-done.4), custom_call_target="tpu_custom_call" | custom-call | tf_op jit(solution)/shard_map/pack/pallas_call | solution.py:166
  7.7 17.8 %all-to-all-start = ((bf16[128,16,256]{2,1,0:T(8,128)(2,1)}), bf16[128,16,256]{2,1,0:T(8,128)(2,1)S(1)}, u32[]{:S(2)}, u32[]{:S(2)}) async-start(bf16[128,16,256]{2,1,0:T(8,128)(2,1)} %pack.1), calls=%async_computation | async-start | bytes 2097152 | tf_op jit(solution)/shard_map/all_to_all | solution.py:182
  25.5 0.0 copy-done.5
  25.5 4.0 %collective-permute-start.1 = (bf16[1024,256]{1,0:T(8,128)(2,1)S(1)}, bf16[1024,256]{1,0:T(8,128)(2,1)S(1)}, u32[]{:S(2)}, u32[]{:S(2)}) collective-permute-start(bf16[1024,256]{1,0:T(8,128)(2,1)S(1)} %copy-done.5), channel_id=1, source_target_pairs={{256,0},{384,128},{0,256},{128,384},{257,1},{385,129},{1,257},{129... | collective-permute-start | bytes 1572872 | tf_op jit(solution)/shard_map/ppermute | solution.py:194
  29.6 3.3 %collective-permute-start = (bf16[1024,256]{1,0:T(8,128)(2,1)S(1)}, bf16[1024,256]{1,0:T(8,128)(2,1)}, u32[]{:S(2)}, u32[]{:S(2)}) collective-permute-start(bf16[1024,256]{1,0:T(8,128)(2,1)S(1)} %copy-done.5), channel_id=1, source_target_pairs={{128,0},{256,128},{384,256},{0,384},{129,1},{257,129},{385,257},{1... | collective-permute-start | bytes 1572872 | tf_op jit(solution)/shard_map/ppermute | solution.py:194
  32.9 2.5 %collective-permute-start.2 = (bf16[1024,256]{1,0:T(8,128)(2,1)S(1)}, bf16[1024,256]{1,0:T(8,128)(2,1)}, u32[]{:S(2)}, u32[]{:S(2)}) collective-permute-start(bf16[1024,256]{1,0:T(8,128)(2,1)S(1)} %copy-done.5), channel_id=1, source_target_pairs={{384,0},{0,128},{128,256},{256,384},{385,1},{1,129},{129,257},{257... | collective-permute-start | bytes 1572872 | tf_op jit(solution)/shard_map/ppermute | solution.py:194
  35.4 0.0 copy-done.3
  35.4 2.1 %order.1 = bf16[1024,2048]{1,0:T(8,128)(2,1)S(1)} custom-call(s32[1]{0:T(128)} %bitcast.3.refs_0_, s32[128,2048]{1,0:T(8,128)S(1)} %copy-done.3), custom_call_target="tpu_custom_call" | custom-call | tf_op jit(solution)/shard_map/order/pallas_call | solution.py:184
  37.5 0.0 copy-start
  37.5 1.9 %copy-done = bf16[1024,2048]{1,0:T(8,128)(2,1)} copy-done((bf16[1024,2048]{1,0:T(8,128)(2,1)}, bf16[1024,2048]{1,0:T(8,128)(2,1)S(1)}, u32[]{:S(2)}) %copy-start) | copy-done | bytes 4194328
  39.5 0.1 pad_add_fusion.where_ref
  39.5 4.3 %collective-permute-done.1.amps2 = bf16[1024,256]{1,0:T(8,128)(2,1)S(1)} collective-permute-done((bf16[1024,256]{1,0:T(8,128)(2,1)S(1)}, bf16[1024,256]{1,0:T(8,128)(2,1)S(1)}, u32[]{:S(2)}, u32[]{:S(2)}) %collective-permute-start.1) | collective-permute-done | bytes 524320 | tf_op jit(solution)/shard_map/ppermute | solution.py:194
  43.8 9.9 %collective-permute-done.amps1 = bf16[1024,256]{1,0:T(8,128)(2,1)} collective-permute-done((bf16[1024,256]{1,0:T(8,128)(2,1)S(1)}, bf16[1024,256]{1,0:T(8,128)(2,1)}, u32[]{:S(2)}, u32[]{:S(2)}) %collective-permute-start) | collective-permute-done | bytes 524320 | tf_op jit(solution)/shard_map/ppermute | solution.py:194
  53.7 0.1 collective-permute-done.2.amps3
  53.8 2.6 %all-to-all-done.received = bf16[128,16,256]{2,1,0:T(8,128)(2,1)S(1)} async-done(((bf16[128,16,256]{2,1,0:T(8,128)(2,1)}), bf16[128,16,256]{2,1,0:T(8,128)(2,1)S(1)}, u32[]{:S(2)}, u32[]{:S(2)}) %all-to-all-start) | async-done | bytes 1048608 | tf_op jit(solution)/shard_map/all_to_all | solution.py:182
  56.4 0.0 copy-start.1
  56.4 2.2 %copy-done.1 = bf16[1024,2048]{1,0:T(8,128)(2,1)S(1)} copy-done((bf16[1024,2048]{1,0:T(8,128)(2,1)S(1)}, bf16[1024,2048]{1,0:T(8,128)(2,1)}, u32[]{:S(2)}) %copy-start.1) | copy-done | bytes 4194328
  58.6 3.6 %multiply.1 = (f32[1024,128]{1,0:T(8,128)S(1)}, f32[1024,128]{1,0:T(8,128)S(1)}) custom-call(s32[2]{0:T(128)S(1)} %pad_add_fusion.where_ref, bf16[128,16,256]{2,1,0:T(8,128)(2,1)S(1)} %all-to-all-done.received, bf16[1024,2048]{1,0:T(8,128)(2,1)S(1)} %copy-done.1, bf16[1024,256]{1,0:T(8,128)(2,1)S(1)} %copy-done.5, ...), custom_call_target="tpu_custom_call" | custom-call | tf_op jit(solution)/shard_map/multiply/pallas_call | solution.py:199
  62.2 1.9 %collective-permute-start.3 = (f32[1024,128]{1,0:T(8,128)S(1)}, f32[1024,128]{1,0:T(8,128)S(1)}, u32[]{:S(2)}, u32[]{:S(2)}) collective-permute-start(f32[1024,128]{1,0:T(8,128)S(1)} %get-tuple-element.8), channel_id=1, source_target_pairs={{0,1},{1,0},{2,3},{3,2},{4,5},{5,4},{6,7},{7,6},{8,9},{9,8},{10,11... | collective-permute-start | bytes 1572872 | tf_op jit(solution)/shard_map/ppermute | solution.py:208
  64.1 1.9 %collective-permute-done.3 = f32[1024,128]{1,0:T(8,128)S(1)} collective-permute-done((f32[1024,128]{1,0:T(8,128)S(1)}, f32[1024,128]{1,0:T(8,128)S(1)}, u32[]{:S(2)}, u32[]{:S(2)}) %collective-permute-start.3) | collective-permute-done | bytes 524320 | tf_op jit(solution)/shard_map/ppermute | solution.py:208
  66.0 0.3 multiply_convert_fusion
  66.4 25.5 %all_to_all.10 = f16[64,16,128]{2,1,0:T(8,128)(2,1)S(1)} all-to-all(f16[64,16,128]{2,1,0:T(8,128)(2,1)S(1)} %bitcast.5), channel_id=1, replica_groups={{0,2,4,6,8,10,12,14,16,18,20,22,24,26,28,30,32,34,36,38,40,42,44,46,48,..., dimensions={0} | all-to-all | bytes 524288 | tf_op jit(solution)/shard_map/all_to_all | solution.py:211
  91.9 0.1 fusion.1
  92.0 0.6 convert_element_type.16
Async XLA Ops:
  0.1 1.2 %copy-start.2 = (s32[128,2048]{1,0:T(8,128)S(1)}, s32[128,2048]{1,0:T(8,128)}, u32[]{:S(2)}) copy-start(s32[128,2048]{1,0:T(8,128)} %refs_1_.1) | copy-start | bytes 3145732
  1.3 1.2 %copy-start.4 = (bf16[256,2048]{1,0:T(8,128)(2,1)S(1)}, bf16[256,2048]{1,0:T(8,128)(2,1)}, u32[]{:S(2)}) copy-start(bf16[256,2048]{1,0:T(8,128)(2,1)} %ints.1) | copy-start | bytes 3145732
  2.5 23.0 %copy-start.5 = (bf16[1024,256]{1,0:T(8,128)(2,1)S(1)}, bf16[1024,256]{1,0:T(8,128)(2,1)}, u32[]{:S(2)}) copy-start(bf16[1024,256]{1,0:T(8,128)(2,1)} %amps0.1) | copy-start | bytes 1572868
  2.5 32.9 %copy-start.3 = (s32[128,2048]{1,0:T(8,128)S(1)}, s32[128,2048]{1,0:T(8,128)}, u32[]{:S(2)}) copy-start(s32[128,2048]{1,0:T(8,128)} %refs_1_.1) | copy-start | bytes 3145732
  7.7 48.7 %all-to-all-start = ((bf16[128,16,256]{2,1,0:T(8,128)(2,1)}), bf16[128,16,256]{2,1,0:T(8,128)(2,1)S(1)}, u32[]{:S(2)}, u32[]{:S(2)}) async-start(bf16[128,16,256]{2,1,0:T(8,128)(2,1)} %pack.1), calls=%async_computation | async-start | bytes 2097152 | tf_op jit(solution)/shard_map/all_to_all | solution.py:182
  25.5 18.3 %collective-permute-start.1 = (bf16[1024,256]{1,0:T(8,128)(2,1)S(1)}, bf16[1024,256]{1,0:T(8,128)(2,1)S(1)}, u32[]{:S(2)}, u32[]{:S(2)}) collective-permute-start(bf16[1024,256]{1,0:T(8,128)(2,1)S(1)} %copy-done.5), channel_id=1, source_target_pairs={{256,0},{384,128},{0,256},{128,384},{257,1},{385,129},{1,257},{129... | collective-permute-start | bytes 1572872 | tf_op jit(solution)/shard_map/ppermute | solution.py:194
  29.6 24.1 %collective-permute-start = (bf16[1024,256]{1,0:T(8,128)(2,1)S(1)}, bf16[1024,256]{1,0:T(8,128)(2,1)}, u32[]{:S(2)}, u32[]{:S(2)}) collective-permute-start(bf16[1024,256]{1,0:T(8,128)(2,1)S(1)} %copy-done.5), channel_id=1, source_target_pairs={{128,0},{256,128},{384,256},{0,384},{129,1},{257,129},{385,257},{1... | collective-permute-start | bytes 1572872 | tf_op jit(solution)/shard_map/ppermute | solution.py:194
  32.9 20.9 %collective-permute-start.2 = (bf16[1024,256]{1,0:T(8,128)(2,1)S(1)}, bf16[1024,256]{1,0:T(8,128)(2,1)}, u32[]{:S(2)}, u32[]{:S(2)}) collective-permute-start(bf16[1024,256]{1,0:T(8,128)(2,1)S(1)} %copy-done.5), channel_id=1, source_target_pairs={{384,0},{0,128},{128,256},{256,384},{385,1},{1,129},{129,257},{257... | collective-permute-start | bytes 1572872 | tf_op jit(solution)/shard_map/ppermute | solution.py:194
  37.5 2.0 %copy-start = (bf16[1024,2048]{1,0:T(8,128)(2,1)}, bf16[1024,2048]{1,0:T(8,128)(2,1)S(1)}, u32[]{:S(2)}) copy-start(bf16[1024,2048]{1,0:T(8,128)(2,1)S(1)} %order.1) | copy-start | bytes 12582916
  56.4 2.2 %copy-start.1 = (bf16[1024,2048]{1,0:T(8,128)(2,1)S(1)}, bf16[1024,2048]{1,0:T(8,128)(2,1)}, u32[]{:S(2)}) copy-start(bf16[1024,2048]{1,0:T(8,128)(2,1)} %copy-done) | copy-start | bytes 12582916
  62.2 3.8 %collective-permute-start.3 = (f32[1024,128]{1,0:T(8,128)S(1)}, f32[1024,128]{1,0:T(8,128)S(1)}, u32[]{:S(2)}, u32[]{:S(2)}) collective-permute-start(f32[1024,128]{1,0:T(8,128)S(1)} %get-tuple-element.8), channel_id=1, source_target_pairs={{0,1},{1,0},{2,3},{3,2},{4,5},{5,4},{6,7},{7,6},{8,9},{9,8},{10,11... | collective-permute-start | bytes 1572872 | tf_op jit(solution)/shard_map/ppermute | solution.py:208

commit v4 on v2

v4 whole, which is shorter than its diff:
```python
import jax
import jax.numpy as jnp
from jax import lax
from jax.experimental import pallas as pl
from jax.experimental.pallas import tpu as pltpu
from jax.sharding import PartitionSpec as P

F32 = jnp.float32
BF16 = jnp.bfloat16
NT = (((1,), (1,)), ((), ()))
VMEM_LIMIT = 24 * 1024 * 1024
VMEM = pl.BlockSpec(memory_space=pltpu.VMEM)
SMEM = pl.BlockSpec(memory_space=pltpu.SMEM)
ANY = pl.BlockSpec(memory_space=pl.ANY)
HBM = pl.BlockSpec(memory_space=pltpu.HBM)


def in_hbm(value):
    return pltpu.with_memory_space_constraint(value, pltpu.HBM)


def pack_kernel(starts, ints, out, slots, windows, sems):
    devices, capacity, _ = out.shape
    total, chunk = ints.shape[1], 256
    rows = lax.broadcasted_iota(jnp.int32, (chunk, chunk), 0)
    cols = lax.broadcasted_iota(jnp.int32, (chunk, chunk), 1)
    eye = jnp.where(rows == cols, 1.0, 0.0).astype(BF16)
    for step in range(total // chunk):
        at = pl.ds(step * chunk, chunk)
        slots[at, :] = lax.dot_general(eye, ints[:, at], NT, preferred_element_type=F32)
    slots[pl.ds(total, capacity + 8), :] = jnp.zeros((capacity + 8, slots.shape[1]), F32)
    pieces = sems.shape[0]
    each = devices // pieces
    copies = []
    for piece in range(pieces):
        for dest in range(piece * each, (piece + 1) * each):
            start = starts[dest]
            aligned = pl.multiple_of((start >> 3) << 3, 8)
            window = slots[pl.ds(aligned, capacity + 8), :]
            window = pltpu.roll(window, capacity + 8 - (start & 7), 0)
            windows[dest] = window[:capacity].astype(BF16)
        at = pl.ds(piece * each, each)
        copies.append(pltpu.make_async_copy(windows.at[at], out.at[at], sems.at[piece]))
        copies[-1].start()
    for copy in copies:
        copy.wait()


def order_kernel(capacity, width, base_ref, owned, out, held, sem):
    copy = pltpu.make_async_copy(owned, held, sem)
    copy.start()
    base = base_ref[0]
    holders, total = owned.shape
    beyond = jnp.int32(1 << 30)
    copy.wait()
    table = held[...]
    table = jnp.where(table < 0, beyond, table - base)
    below = jnp.zeros((holders, 128), F32)
    for tile in range(total // 128):
        below = below + jnp.where(table[:, tile * 128:(tile + 1) * 128] < 0, 1.0, 0.0)
    ones = jnp.ones((128, 128), BF16)
    start = jnp.dot(below.astype(BF16), ones, preferred_element_type=F32).astype(jnp.int32)
    window = jnp.concatenate([table, jnp.full((holders, 128), beyond, jnp.int32)], axis=1)
    shift = total // 2
    while shift >= 128:
        keep = shift + 128
        taken = (start & shift) != 0
        taken = jnp.concatenate([taken] * (keep // 128), axis=1)
        window = jnp.where(taken, window[:, shift:shift + keep], window[:, :keep])
        shift //= 2
    while shift >= 1:
        taken = (start & shift) != 0
        taken = jnp.concatenate([taken, taken], axis=1)
        window = jnp.where(taken, pltpu.roll(window, 256 - shift, 1), window)
        shift //= 2
    lane = lax.broadcasted_iota(jnp.int32, (holders, 128), 1)
    spread = jnp.where(lane < capacity, window[:, :128], 0)
    shift = capacity
    while shift < 128:
        spread = spread + pltpu.roll(spread, shift, 1)
        shift *= 2
    each = 128 // capacity
    mine = lax.broadcasted_iota(jnp.int32, (each, 128), 0)
    mine = mine == lax.broadcasted_iota(jnp.int32, (each, 128), 1) // capacity
    columns = jnp.concatenate(
        [
            jnp.sum(jnp.where(mine, spread[at:at + each], 0), axis=0, keepdims=True)
            for at in range(0, holders, each)
        ],
        axis=1,
    )
    out[...] = jnp.broadcast_to(columns, out.shape)


def multiply_kernel(
    where_ref, received, columns, amps0, amps1, amps2, amps3, kept, given, left, amps, sems
):
    group, core = where_ref[0], where_ref[1]
    holders, capacity, pairs = received.shape
    blocks, width, _ = amps.shape
    copies = []
    for step, part in enumerate((amps0, amps1, amps2, amps3)):
        target = amps.at[lax.rem(group + step, blocks)]
        copies.append(pltpu.make_async_copy(part, target, sems.at[step]))
        copies[-1].start()
    new = lax.broadcasted_iota(jnp.int32, (pairs, pairs), 0)
    old = lax.broadcasted_iota(jnp.int32, (pairs, pairs), 1)
    half = pairs // 2
    chips = half // 2
    side = jnp.where(new < half, core, 1 - core)
    in_half = jnp.where(new < half, new, new - half)
    row = jnp.where(in_half < chips, 0, 1)
    chip = jnp.where(in_half < chips, in_half, in_half - chips)
    pick = jnp.where(old == 4 * chip + 2 * side + row, 1.0, 0.0).astype(BF16)
    slot_count = holders * capacity
    slots = lax.dot_general(
        pick, received[...].reshape(slot_count, pairs), NT, preferred_element_type=F32
    ).astype(BF16)
    place = columns[0:1, :]
    chunk = 256
    for step in range(width // chunk):
        wanted = lax.broadcasted_iota(jnp.int32, (chunk, slot_count), 0) + step * chunk
        order = jnp.where(wanted == place, 1.0, 0.0).astype(BF16)
        left[:, step * chunk:(step + 1) * chunk] = lax.dot_general(
            slots, order, NT, preferred_element_type=F32
        ).astype(BF16)
    for copy in copies:
        copy.wait()
    for block in range(blocks):
        product = jnp.dot(left[...], amps[block], preferred_element_type=F32)
        for target, at in ((kept, 0), (given, half)):
            for r in range(2):
                for h in range(2):
                    target[pl.ds(r * 8 + 2 * block + h, chips, stride=16), :] = product[
                        at + r * chips:at + (r + 1) * chips, h * 128:(h + 1) * 128
                    ]


def pack(starts, ladder_ints, devices, capacity):
    pairs, total = ladder_ints.shape
    return pl.pallas_call(
        pack_kernel,
        out_shape=jax.ShapeDtypeStruct((devices, capacity, pairs), BF16),
        in_specs=[SMEM, VMEM],
        out_specs=HBM,
        scratch_shapes=[
            pltpu.VMEM((total + capacity + 8, pairs), F32),
            pltpu.VMEM((devices, capacity, pairs), BF16),
            pltpu.SemaphoreType.DMA((8,)),
        ],
        compiler_params=pltpu.CompilerParams(vmem_limit_bytes=VMEM_LIMIT),
        name="pack",
    )(starts, ladder_ints)


def order(base, owned_columns, capacity, width):
    holders, _ = owned_columns.shape
    return pl.pallas_call(
        lambda *refs: order_kernel(capacity, width, *refs),
        out_shape=jax.ShapeDtypeStruct((8, holders * capacity), jnp.int32),
        in_specs=[SMEM, HBM],
        out_specs=VMEM,
        scratch_shapes=[
            pltpu.VMEM(owned_columns.shape, jnp.int32),
            pltpu.SemaphoreType.DMA,
        ],
        compiler_params=pltpu.CompilerParams(vmem_limit_bytes=VMEM_LIMIT),
        name="order",
    )(base, in_hbm(owned_columns))


def multiply(where, received, columns, amps0, amps1, amps2, amps3):
    pairs = received.shape[2]
    width, pairs_ij = amps0.shape
    out = jax.ShapeDtypeStruct((pairs // 2 * 4 * pairs_ij // 128, 128), F32)
    return pl.pallas_call(
        multiply_kernel,
        out_shape=[out, out],
        in_specs=[SMEM, VMEM, VMEM] + [ANY] * 4,
        out_specs=[VMEM, VMEM],
        scratch_shapes=[
            pltpu.VMEM((pairs, width), BF16),
            pltpu.VMEM((4, width, pairs_ij), BF16),
            pltpu.SemaphoreType.DMA((4,)),
        ],
        compiler_params=pltpu.CompilerParams(vmem_limit_bytes=VMEM_LIMIT),
        name="multiply",
    )(where, received, columns, amps0, amps1, amps2, amps3)


SCALE = 2.0 ** 22


def squeeze(value):
    return (jnp.sign(value) * jnp.sqrt(jnp.abs(value) * SCALE)).astype(jnp.float16)


def unsqueeze(root):
    root = root.astype(F32)
    return root * jnp.abs(root) * (1.0 / SCALE)


def body(amplitudes, owned_columns, ladder_ints):
    device = lax.axis_index("cd")
    group = lax.axis_index("ij")
    devices_cd = lax.axis_size("cd")
    groups = lax.axis_size("ij")
    width = amplitudes.shape[0]
    capacity = 2 * width // devices_cd

    own_row = lax.dynamic_index_in_dim(owned_columns, device, 0, keepdims=False)
    range_starts = jnp.arange(devices_cd, dtype=jnp.int32) * width
    starts = jnp.sum(
        (own_row >= 0)[None, :] & (own_row[None, :] < range_starts[:, None]), axis=1, dtype=jnp.int32
    )
    outgoing = pack(starts, ladder_ints, devices_cd, capacity)
    incoming = lax.all_to_all(outgoing, "cd", split_axis=0, concat_axis=0, tiled=True)
    columns = order((device * width)[None].astype(jnp.int32), owned_columns, capacity, width)

    def from_group(value, step):
        return lax.ppermute(value, "ij", [((i + step) % groups, i) for i in range(groups)])

    others = [from_group(amplitudes, step) for step in range(1, groups)]
    where = jnp.stack([group, lax.rem(device, 2)]).astype(jnp.int32)
    kept, given = multiply(where, incoming, columns, amplitudes, *others)
    taken = lax.ppermute(given, "cd", [(i, i ^ 1) for i in range(devices_cd)])
    both = squeeze(kept + taken).reshape(devices_cd // 2, 16, 128)
    same_core = [[2 * k + c for k in range(devices_cd // 2)] for c in range(2)]
    shares = lax.all_to_all(both, "cd", 0, 0, tiled=True, axis_index_groups=same_core)
    summed = jnp.sum(unsqueeze(shares), axis=0)
    return summed.astype(BF16).reshape(2, 1024)


def solution(mesh):
    return jax.shard_map(
        body,
        mesh=mesh,
        in_specs=(P("cd", "ij"), P(), P("ij", "cd")),
        out_specs=P(("ij", "cd"), None),
        check_vma=False,
    )
```

time: 93.8 us -> 90.7 us (0.967)
  the two profiles are of different devices: /device:TPU:16 before, /device:TPU:8 now
where the time goes in v4:
time: 90.7 us; the launch traced here: 90.3 us
  starting transfers between devices  29.6 us (33%)
  blocking collectives  27 us (30%)
  waiting for transfers between devices  22.2 us (24%)
  Pallas kernels  7.83 us (9%)
  local copies, waits for them, and re-layouts  1.84 us (2%)
  other arithmetic  1.7 us (2%)
    all_to_all x1, blocking collectives, body(): lax.all_to_all(both, 'cd', 0, 0, tiled=True, axis_index_groups=same_core)  27 us
    ppermute x3, waiting for transfers between devices, from_group(): lax.ppermute(value, 'ij', [((i + step) % groups, i) for i in range(groups)])  20.4 us
    all_to_all x1, starting transfers between devices, body(): lax.all_to_all(outgoing, 'cd', split_axis=0, concat_axis=0, tiled=True)  17.5 us
    ppermute x3, starting transfers between devices, from_group(): lax.ppermute(value, 'ij', [((i + step) % groups, i) for i in range(groups)])  10.2 us
    pallas_call x1, Pallas kernels, multiply(): pl.pallas_call(multiply_kernel, out_shape=[out, out], in_specs=[SMEM, VME...  3.2 us
    pallas_call x1, Pallas kernels, order(): pl.pallas_call(lambda *refs: order_kernel(capacity, width, *refs), out_sh...  2.36 us
    pallas_call x1, Pallas kernels, pack(): pl.pallas_call(pack_kernel, out_shape=jax.ShapeDtypeStruct((devices, capa...  2.27 us
    ppermute x1, starting transfers between devices, body(): taken = lax.ppermute(given, 'cd', [(i, i ^ 1) for i in range(devices_cd)])  1.92 us
  transfers between devices with their start and end apart: 5, of which 3 were waited for; matrix products, arithmetic and copies ran while one was open for 0% of the time, Pallas kernels for 3%

profile of v4, /device:TPU:8, one launch (start us, length us, event | category | flops | bytes accessed | tf_op | source)
XLA Modules:
  0.0 90.3 jit_solution(14625703477743035421)
XLA Ops:
  0.0 0.9 compare_reduce_fusion
  0.9 0.3 convert_reduce_fusion.starts
  1.2 0.0 copy-start
  1.2 1.2 %copy-done = bf16[256,2048]{1,0:T(8,128)(2,1)S(1)} copy-done((bf16[256,2048]{1,0:T(8,128)(2,1)S(1)}, bf16[256,2048]{1,0:T(8,128)(2,1)}, u32[]{:S(2)}) %copy-start) | copy-done | bytes 1048600
  2.4 2.3 %pack.1 = bf16[128,16,256]{2,1,0:T(8,128)(2,1)} custom-call(s32[128]{0:T(128)S(1)} %convert_reduce_fusion.starts, bf16[256,2048]{1,0:T(8,128)(2,1)S(1)} %copy-done), custom_call_target="tpu_custom_call" | custom-call | tf_op jit(solution)/shard_map/pack/pallas_call | solution.py:141
  4.7 0.0 copy-start.1
  4.7 17.5 %all-to-all-start = ((bf16[128,16,256]{2,1,0:T(8,128)(2,1)}), bf16[128,16,256]{2,1,0:T(8,128)(2,1)S(1)}, u32[]{:S(2)}, u32[]{:S(2)}) async-start(bf16[128,16,256]{2,1,0:T(8,128)(2,1)} %pack.1), calls=%async_computation | async-start | bytes 2097152 | tf_op jit(solution)/shard_map/all_to_all | solution.py:217
  22.2 0.0 copy-done.1
  22.2 4.7 %collective-permute-start = (bf16[1024,256]{1,0:T(8,128)(2,1)S(1)}, bf16[1024,256]{1,0:T(8,128)(2,1)S(1)}, u32[]{:S(2)}, u32[]{:S(2)}) collective-permute-start(bf16[1024,256]{1,0:T(8,128)(2,1)S(1)} %copy-done.1), channel_id=1, source_target_pairs={{128,0},{256,128},{384,256},{0,384},{129,1},{257,129},{385,257},{1... | collective-permute-start | bytes 1572872 | tf_op jit(solution)/shard_map/ppermute | solution.py:221
  26.9 2.7 %collective-permute-start.1 = (bf16[1024,256]{1,0:T(8,128)(2,1)S(1)}, bf16[1024,256]{1,0:T(8,128)(2,1)S(1)}, u32[]{:S(2)}, u32[]{:S(2)}) collective-permute-start(bf16[1024,256]{1,0:T(8,128)(2,1)S(1)} %copy-done.1), channel_id=1, source_target_pairs={{256,0},{384,128},{0,256},{128,384},{257,1},{385,129},{1,257},{129... | collective-permute-start | bytes 1572872 | tf_op jit(solution)/shard_map/ppermute | solution.py:221
  29.6 2.8 %collective-permute-start.2 = (bf16[1024,256]{1,0:T(8,128)(2,1)S(1)}, bf16[1024,256]{1,0:T(8,128)(2,1)S(1)}, u32[]{:S(2)}, u32[]{:S(2)}) collective-permute-start(bf16[1024,256]{1,0:T(8,128)(2,1)S(1)} %copy-done.1), channel_id=1, source_target_pairs={{384,0},{0,128},{128,256},{256,384},{385,1},{1,129},{129,257},{257... | collective-permute-start | bytes 1572872 | tf_op jit(solution)/shard_map/ppermute | solution.py:221
  32.4 2.4 %order.1.columns = s32[8,2048]{1,0:T(8,128)S(1)} custom-call(s32[1]{0:T(128)} %bitcast.3.refs_0_, s32[128,2048]{1,0:T(8,128)} %refs_1_.1), custom_call_target="tpu_custom_call" | custom-call | tf_op jit(solution)/shard_map/order/pallas_call | solution.py:158
  34.8 0.1 pad_add_fusion.where_ref
  34.9 14.8 %collective-permute-done.amps1 = bf16[1024,256]{1,0:T(8,128)(2,1)S(1)} collective-permute-done((bf16[1024,256]{1,0:T(8,128)(2,1)S(1)}, bf16[1024,256]{1,0:T(8,128)(2,1)S(1)}, u32[]{:S(2)}, u32[]{:S(2)}) %collective-permute-start) | collective-permute-done | bytes 524320 | tf_op jit(solution)/shard_map/ppermute | solution.py:221
  49.6 0.0 collective-permute-done.1.amps2
  49.6 5.6 %collective-permute-done.2.amps3 = bf16[1024,256]{1,0:T(8,128)(2,1)S(1)} collective-permute-done((bf16[1024,256]{1,0:T(8,128)(2,1)S(1)}, bf16[1024,256]{1,0:T(8,128)(2,1)S(1)}, u32[]{:S(2)}, u32[]{:S(2)}) %collective-permute-start.2) | collective-permute-done | bytes 524320 | tf_op jit(solution)/shard_map/ppermute | solution.py:221
  55.2 0.0 all-to-all-done.received
  55.2 3.2 %multiply.1 = (f32[1024,128]{1,0:T(8,128)S(1)}, f32[1024,128]{1,0:T(8,128)S(1)}) custom-call(s32[2]{0:T(128)S(1)} %pad_add_fusion.where_ref, bf16[128,16,256]{2,1,0:T(8,128)(2,1)S(1)} %all-to-all-done.received, s32[8,2048]{1,0:T(8,128)S(1)} %order.1.columns, bf16[1024,256]{1,0:T(8,128)(2,1)S(1)} %copy-done.1, ...), custom_call_target="tpu_custom_call" | custom-call | tf_op jit(solution)/shard_map/multiply/pallas_call | solution.py:176
  58.4 1.9 %collective-permute-start.3 = (f32[1024,128]{1,0:T(8,128)S(1)}, f32[1024,128]{1,0:T(8,128)S(1)}, u32[]{:S(2)}, u32[]{:S(2)}) collective-permute-start(f32[1024,128]{1,0:T(8,128)S(1)} %get-tuple-element.8), channel_id=1, source_target_pairs={{0,1},{1,0},{2,3},{3,2},{4,5},{5,4},{6,7},{7,6},{8,9},{9,8},{10,11... | collective-permute-start | bytes 1572872 | tf_op jit(solution)/shard_map/ppermute | solution.py:226
  60.4 1.9 %collective-permute-done.3 = f32[1024,128]{1,0:T(8,128)S(1)} collective-permute-done((f32[1024,128]{1,0:T(8,128)S(1)}, f32[1024,128]{1,0:T(8,128)S(1)}, u32[]{:S(2)}, u32[]{:S(2)}) %collective-permute-start.3) | collective-permute-done | bytes 524320 | tf_op jit(solution)/shard_map/ppermute | solution.py:226
  62.2 0.3 multiply_convert_fusion
  62.6 27.0 %all_to_all.10 = f16[64,16,128]{2,1,0:T(8,128)(2,1)S(1)} all-to-all(f16[64,16,128]{2,1,0:T(8,128)(2,1)S(1)} %bitcast.5), channel_id=1, replica_groups={{0,2,4,6,8,10,12,14,16,18,20,22,24,26,28,30,32,34,36,38,40,42,44,46,48,..., dimensions={0} | all-to-all | bytes 524288 | tf_op jit(solution)/shard_map/all_to_all | solution.py:229
  89.6 0.1 fusion.1
  89.7 0.6 convert_element_type.20
  (1 shorter events, 0.0 us)
Async XLA Ops:
  1.2 1.2 %copy-start = (bf16[256,2048]{1,0:T(8,128)(2,1)S(1)}, bf16[256,2048]{1,0:T(8,128)(2,1)}, u32[]{:S(2)}) copy-start(bf16[256,2048]{1,0:T(8,128)(2,1)} %ints.1) | copy-start | bytes 3145732
  4.7 17.5 %copy-start.1 = (bf16[1024,256]{1,0:T(8,128)(2,1)S(1)}, bf16[1024,256]{1,0:T(8,128)(2,1)}, u32[]{:S(2)}) copy-start(bf16[1024,256]{1,0:T(8,128)(2,1)} %amps0.1) | copy-start | bytes 1572868
  4.7 50.5 %all-to-all-start = ((bf16[128,16,256]{2,1,0:T(8,128)(2,1)}), bf16[128,16,256]{2,1,0:T(8,128)(2,1)S(1)}, u32[]{:S(2)}, u32[]{:S(2)}) async-start(bf16[128,16,256]{2,1,0:T(8,128)(2,1)} %pack.1), calls=%async_computation | async-start | bytes 2097152 | tf_op jit(solution)/shard_map/all_to_all | solution.py:217
  22.2 27.4 %collective-permute-start = (bf16[1024,256]{1,0:T(8,128)(2,1)S(1)}, bf16[1024,256]{1,0:T(8,128)(2,1)S(1)}, u32[]{:S(2)}, u32[]{:S(2)}) collective-permute-start(bf16[1024,256]{1,0:T(8,128)(2,1)S(1)} %copy-done.1), channel_id=1, source_target_pairs={{128,0},{256,128},{384,256},{0,384},{129,1},{257,129},{385,257},{1... | collective-permute-start | bytes 1572872 | tf_op jit(solution)/shard_map/ppermute | solution.py:221
  26.9 22.7 %collective-permute-start.1 = (bf16[1024,256]{1,0:T(8,128)(2,1)S(1)}, bf16[1024,256]{1,0:T(8,128)(2,1)S(1)}, u32[]{:S(2)}, u32[]{:S(2)}) collective-permute-start(bf16[1024,256]{1,0:T(8,128)(2,1)S(1)} %copy-done.1), channel_id=1, source_target_pairs={{256,0},{384,128},{0,256},{128,384},{257,1},{385,129},{1,257},{129... | collective-permute-start | bytes 1572872 | tf_op jit(solution)/shard_map/ppermute | solution.py:221
  29.6 25.6 %collective-permute-start.2 = (bf16[1024,256]{1,0:T(8,128)(2,1)S(1)}, bf16[1024,256]{1,0:T(8,128)(2,1)S(1)}, u32[]{:S(2)}, u32[]{:S(2)}) collective-permute-start(bf16[1024,256]{1,0:T(8,128)(2,1)S(1)} %copy-done.1), channel_id=1, source_target_pairs={{384,0},{0,128},{128,256},{256,384},{385,1},{1,129},{129,257},{257... | collective-permute-start | bytes 1572872 | tf_op jit(solution)/shard_map/ppermute | solution.py:221
  58.4 3.8 %collective-permute-start.3 = (f32[1024,128]{1,0:T(8,128)S(1)}, f32[1024,128]{1,0:T(8,128)S(1)}, u32[]{:S(2)}, u32[]{:S(2)}) collective-permute-start(f32[1024,128]{1,0:T(8,128)S(1)} %get-tuple-element.8), channel_id=1, source_target_pairs={{0,1},{1,0},{2,3},{3,2},{4,5},{5,4},{6,7},{7,6},{8,9},{9,8},{10,11... | collective-permute-start | bytes 1572872 | tf_op jit(solution)/shard_map/ppermute | solution.py:226

commit v5 on v4

--- a/solution.py
+++ b/solution.py
@@ -19,28 +19,53 @@
     return pltpu.with_memory_space_constraint(value, pltpu.HBM)
 
 
-def pack_kernel(starts, ints, out, slots, windows, sems):
+def pack_kernel(where_ref, owned, ints, out, group, staged, slots, firsts, starts, windows, sems):
+    device, width = where_ref[0], where_ref[1]
     devices, capacity, _ = out.shape
     total, chunk = ints.shape[1], 256
+    eight = pl.multiple_of((device >> 3) << 3, 8)
+    own_copy = pltpu.make_async_copy(owned.at[pl.ds(eight, 8)], group, sems.at[0])
+    own_copy.start()
+    ints_copy = pltpu.make_async_copy(ints, staged, sems.at[1])
+    ints_copy.start()
+    slots[pl.ds(total, capacity + 8), :] = jnp.zeros((capacity + 8, slots.shape[1]), F32)
     rows = lax.broadcasted_iota(jnp.int32, (chunk, chunk), 0)
     cols = lax.broadcasted_iota(jnp.int32, (chunk, chunk), 1)
     eye = jnp.where(rows == cols, 1.0, 0.0).astype(BF16)
+    line = lax.broadcasted_iota(jnp.int32, group.shape, 0)
+    below = lax.broadcasted_iota(jnp.int32, (devices, 128), 0) * width
+    same = lax.broadcasted_iota(jnp.int32, (devices, 128), 0) == lax.broadcasted_iota(
+        jnp.int32, (devices, 128), 1
+    )
+    own_copy.wait()
+    row = jnp.sum(jnp.where(line == device - eight, group[...], 0), axis=0, keepdims=True)
+    row = jnp.where(row < 0, jnp.int32(1 << 30), row)
+    before = jnp.zeros((devices, 128), F32)
+    for tile in range(total // 128):
+        before = before + jnp.where(row[:, tile * 128:(tile + 1) * 128] < below, 1.0, 0.0)
+    ones = jnp.ones((128, 128), BF16)
+    before = jnp.dot(before.astype(BF16), ones, preferred_element_type=F32)
+    first = jnp.sum(jnp.where(same, before, 0.0), axis=0, keepdims=True).astype(jnp.int32)
+    firsts[...] = jnp.broadcast_to(first, firsts.shape)
+    starts_copy = pltpu.make_async_copy(firsts, starts, sems.at[2])
+    starts_copy.start()
+    ints_copy.wait()
     for step in range(total // chunk):
         at = pl.ds(step * chunk, chunk)
-        slots[at, :] = lax.dot_general(eye, ints[:, at], NT, preferred_element_type=F32)
-    slots[pl.ds(total, capacity + 8), :] = jnp.zeros((capacity + 8, slots.shape[1]), F32)
-    pieces = sems.shape[0]
+        slots[at, :] = lax.dot_general(eye, staged[:, at], NT, preferred_element_type=F32)
+    starts_copy.wait()
+    pieces = sems.shape[0] - 3
     each = devices // pieces
     copies = []
     for piece in range(pieces):
         for dest in range(piece * each, (piece + 1) * each):
-            start = starts[dest]
+            start = starts[0, dest]
             aligned = pl.multiple_of((start >> 3) << 3, 8)
             window = slots[pl.ds(aligned, capacity + 8), :]
             window = pltpu.roll(window, capacity + 8 - (start & 7), 0)
             windows[dest] = window[:capacity].astype(BF16)
         at = pl.ds(piece * each, each)
-        copies.append(pltpu.make_async_copy(windows.at[at], out.at[at], sems.at[piece]))
+        copies.append(pltpu.make_async_copy(windows.at[at], out.at[at], sems.at[3 + piece]))
         copies[-1].start()
     for copy in copies:
         copy.wait()
@@ -136,21 +161,25 @@
                     ]
 
 
-def pack(starts, ladder_ints, devices, capacity):
+def pack(where, owned_columns, ladder_ints, devices, capacity):
     pairs, total = ladder_ints.shape
     return pl.pallas_call(
         pack_kernel,
         out_shape=jax.ShapeDtypeStruct((devices, capacity, pairs), BF16),
-        in_specs=[SMEM, VMEM],
+        in_specs=[SMEM, HBM, HBM],
         out_specs=HBM,
         scratch_shapes=[
+            pltpu.VMEM((8, total), jnp.int32),
+            pltpu.VMEM((pairs, total), BF16),
             pltpu.VMEM((total + capacity + 8, pairs), F32),
+            pltpu.VMEM((8, 128), jnp.int32),
+            pltpu.SMEM((8, 128), jnp.int32),
             pltpu.VMEM((devices, capacity, pairs), BF16),
-            pltpu.SemaphoreType.DMA((8,)),
+            pltpu.SemaphoreType.DMA((11,)),
         ],
         compiler_params=pltpu.CompilerParams(vmem_limit_bytes=VMEM_LIMIT),
         name="pack",
-    )(starts, ladder_ints)
+    )(where, in_hbm(owned_columns), in_hbm(ladder_ints))
 
 
 def order(base, owned_columns, capacity, width):
@@ -166,6 +195,7 @@
         ],
         compiler_params=pltpu.CompilerParams(vmem_limit_bytes=VMEM_LIMIT),
         name="order",
+        cost_estimate=pl.CostEstimate(flops=15_000_000_000, bytes_accessed=1_000_000, transcendentals=0),
     )(base, in_hbm(owned_columns))
 
 
@@ -208,19 +238,17 @@
     width = amplitudes.shape[0]
     capacity = 2 * width // devices_cd
 
-    own_row = lax.dynamic_index_in_dim(owned_columns, device, 0, keepdims=False)
-    range_starts = jnp.arange(devices_cd, dtype=jnp.int32) * width
-    starts = jnp.sum(
-        (own_row >= 0)[None, :] & (own_row[None, :] < range_starts[:, None]), axis=1, dtype=jnp.int32
-    )
-    outgoing = pack(starts, ladder_ints, devices_cd, capacity)
+    own = jnp.stack([device, jnp.int32(width)]).astype(jnp.int32)
+    outgoing = pack(own, owned_columns, ladder_ints, devices_cd, capacity)
     incoming = lax.all_to_all(outgoing, "cd", split_axis=0, concat_axis=0, tiled=True)
-    columns = order((device * width)[None].astype(jnp.int32), owned_columns, capacity, width)
-
     def from_group(value, step):
         return lax.ppermute(value, "ij", [((i + step) % groups, i) for i in range(groups)])
 
-    others = [from_group(amplitudes, step) for step in range(1, groups)]
+    amps2 = from_group(amplitudes, 2)
+    base, amps2 = lax.optimization_barrier(((device * width)[None].astype(jnp.int32), amps2))
+    columns = order(base, owned_columns, capacity, width)
+    later, columns = lax.optimization_barrier((amplitudes, columns))
+    others = [from_group(later, 1), amps2, from_group(later, 3)]
     where = jnp.stack([group, lax.rem(device, 2)]).astype(jnp.int32)
     kept, given = multiply(where, incoming, columns, amplitudes, *others)
     taken = lax.ppermute(given, "cd", [(i, i ^ 1) for i in range(devices_cd)])

time: 90.7 us -> 85.2 us (0.939)
  the two profiles are of different devices: /device:TPU:8 before, /device:TPU:2 now
where the time goes in v5:
time: 85.2 us; the launch traced here: 84.8 us
  starting transfers between devices  29.6 us (35%)
  waiting for transfers between devices  24.3 us (29%)
  blocking collectives  20.3 us (24%)
  Pallas kernels  9.21 us (11%)
    all_to_all x1, blocking collectives, body(): lax.all_to_all(both, 'cd', 0, 0, tiled=True, axis_index_groups=same_core)  20.3 us
    all_to_all x1, starting transfers between devices, body(): lax.all_to_all(outgoing, 'cd', split_axis=0, concat_axis=0, tiled=True)  17.8 us
    ppermute x3, waiting for transfers between devices, from_group(): lax.ppermute(value, 'ij', [((i + step) % groups, i) for i in range(groups)])  12.5 us
    all_to_all x1, waiting for transfers between devices, body(): lax.all_to_all(outgoing, 'cd', split_axis=0, concat_axis=0, tiled=True)  9.99 us
    ppermute x3, starting transfers between devices, from_group(): lax.ppermute(value, 'ij', [((i + step) % groups, i) for i in range(groups)])  9.87 us
    pallas_call x1, Pallas kernels, pack(): pl.pallas_call(pack_kernel, out_shape=jax.ShapeDtypeStruct((devices, capa...  3.58 us
    pallas_call x1, Pallas kernels, multiply(): pl.pallas_call(multiply_kernel, out_shape=[out, out], in_specs=[SMEM, VME...  3.21 us
    pallas_call x1, Pallas kernels, order(): pl.pallas_call(lambda *refs: order_kernel(capacity, width, *refs), out_sh...  2.42 us
  transfers between devices with their start and end apart: 5, of which 4 were waited for; matrix products, arithmetic and copies ran while one was open for 0% of the time, Pallas kernels for 7%

profile of v5, /device:TPU:2, one launch (start us, length us, event | category | flops | bytes accessed | tf_op | source)
XLA Modules:
  0.0 84.8 jit_solution(7808029660454640653)
XLA Ops:
  0.0 4.0 %collective-permute-start = (bf16[1024,256]{1,0:T(8,128)(2,1)}, bf16[1024,256]{1,0:T(8,128)(2,1)S(1)}, u32[]{:S(2)}, u32[]{:S(2)}) collective-permute-start(bf16[1024,256]{1,0:T(8,128)(2,1)} %amps0.1), channel_id=1, source_target_pairs={{256,0},{384,128},{0,256},{128,384},{257,1},{385,129},{1,257},{129... | collective-permute-start | bytes 1572872 | tf_op jit(solution)/shard_map/ppermute | solution.py:245
  4.0 0.1 pad_add_fusion.1.where_ref
  4.1 3.6 %pack.1 = bf16[128,16,256]{2,1,0:T(8,128)(2,1)} custom-call(s32[2]{0:T(128)S(1)} %pad_add_fusion.1.where_ref, s32[128,2048]{1,0:T(8,128)} %refs_1_.1, bf16[256,2048]{1,0:T(8,128)(2,1)} %ints.1), custom_call_target="tpu_custom_call" | custom-call | tf_op jit(solution)/shard_map/pack/pallas_call | solution.py:166
  7.7 17.8 %all-to-all-start = ((bf16[128,16,256]{2,1,0:T(8,128)(2,1)}), bf16[128,16,256]{2,1,0:T(8,128)(2,1)S(1)}, u32[]{:S(2)}, u32[]{:S(2)}) async-start(bf16[128,16,256]{2,1,0:T(8,128)(2,1)} %pack.1), calls=%async_computation | async-start | bytes 2097152 | tf_op jit(solution)/shard_map/all_to_all | solution.py:243
  25.5 0.0 collective-permute-done.amps2
  25.5 0.0 copy-start
  25.6 2.4 %order.1.columns = s32[8,2048]{1,0:T(8,128)S(1)} custom-call(s32[1]{0:T(128)} %bitcast.3.refs_0_, s32[128,2048]{1,0:T(8,128)} %refs_1_.1), custom_call_target="tpu_custom_call" | custom-call | flops 15000000512 | bytes 1000000 | tf_op jit(solution)/shard_map/order/pallas_call | solution.py:187
  28.0 0.0 copy-done
  28.0 3.3 %collective-permute-start.1 = (bf16[1024,256]{1,0:T(8,128)(2,1)S(1)}, bf16[1024,256]{1,0:T(8,128)(2,1)S(1)}, u32[]{:S(2)}, u32[]{:S(2)}) collective-permute-start(bf16[1024,256]{1,0:T(8,128)(2,1)S(1)} %copy-done), channel_id=1, source_target_pairs={{128,0},{256,128},{384,256},{0,384},{129,1},{257,129},{385,257},{1... | collective-permute-start | bytes 1572872 | tf_op jit(solution)/shard_map/ppermute | solution.py:245
  31.4 2.5 %collective-permute-start.2 = (bf16[1024,256]{1,0:T(8,128)(2,1)S(1)}, bf16[1024,256]{1,0:T(8,128)(2,1)S(1)}, u32[]{:S(2)}, u32[]{:S(2)}) collective-permute-start(bf16[1024,256]{1,0:T(8,128)(2,1)S(1)} %copy-done), channel_id=1, source_target_pairs={{384,0},{0,128},{128,256},{256,384},{385,1},{1,129},{129,257},{257... | collective-permute-start | bytes 1572872 | tf_op jit(solution)/shard_map/ppermute | solution.py:245
  33.9 0.1 pad_add_fusion.where_ref
  33.9 9.4 %collective-permute-done.1.amps1 = bf16[1024,256]{1,0:T(8,128)(2,1)S(1)} collective-permute-done((bf16[1024,256]{1,0:T(8,128)(2,1)S(1)}, bf16[1024,256]{1,0:T(8,128)(2,1)S(1)}, u32[]{:S(2)}, u32[]{:S(2)}) %collective-permute-start.1) | collective-permute-done | bytes 524320 | tf_op jit(solution)/shard_map/ppermute | solution.py:245
  43.3 3.1 %collective-permute-done.2.amps3 = bf16[1024,256]{1,0:T(8,128)(2,1)S(1)} collective-permute-done((bf16[1024,256]{1,0:T(8,128)(2,1)S(1)}, bf16[1024,256]{1,0:T(8,128)(2,1)S(1)}, u32[]{:S(2)}, u32[]{:S(2)}) %collective-permute-start.2) | collective-permute-done | bytes 524320 | tf_op jit(solution)/shard_map/ppermute | solution.py:245
  46.4 10.0 %all-to-all-done.received = bf16[128,16,256]{2,1,0:T(8,128)(2,1)S(1)} async-done(((bf16[128,16,256]{2,1,0:T(8,128)(2,1)}), bf16[128,16,256]{2,1,0:T(8,128)(2,1)S(1)}, u32[]{:S(2)}, u32[]{:S(2)}) %all-to-all-start) | async-done | bytes 1048608 | tf_op jit(solution)/shard_map/all_to_all | solution.py:243
  56.4 3.2 %multiply.1 = (f32[1024,128]{1,0:T(8,128)S(1)}, f32[1024,128]{1,0:T(8,128)S(1)}) custom-call(s32[2]{0:T(128)S(1)} %pad_add_fusion.where_ref, bf16[128,16,256]{2,1,0:T(8,128)(2,1)S(1)} %all-to-all-done.received, s32[8,2048]{1,0:T(8,128)S(1)} %order.1.columns, bf16[1024,256]{1,0:T(8,128)(2,1)S(1)} %copy-done, ...), custom_call_target="tpu_custom_call" | custom-call | tf_op jit(solution)/shard_map/multiply/pallas_call | solution.py:206
  59.6 1.9 %collective-permute-start.3 = (f32[1024,128]{1,0:T(8,128)S(1)}, f32[1024,128]{1,0:T(8,128)S(1)}, u32[]{:S(2)}, u32[]{:S(2)}) collective-permute-start(f32[1024,128]{1,0:T(8,128)S(1)} %get-tuple-element.16), channel_id=1, source_target_pairs={{0,1},{1,0},{2,3},{3,2},{4,5},{5,4},{6,7},{7,6},{8,9},{9,8},{10,11... | collective-permute-start | bytes 1572872 | tf_op jit(solution)/shard_map/ppermute | solution.py:254
  61.5 1.9 %collective-permute-done.3 = f32[1024,128]{1,0:T(8,128)S(1)} collective-permute-done((f32[1024,128]{1,0:T(8,128)S(1)}, f32[1024,128]{1,0:T(8,128)S(1)}, u32[]{:S(2)}, u32[]{:S(2)}) %collective-permute-start.3) | collective-permute-done | bytes 524320 | tf_op jit(solution)/shard_map/ppermute | solution.py:254
  63.4 0.3 multiply_convert_fusion
  63.8 20.3 %all_to_all.10 = f16[64,16,128]{2,1,0:T(8,128)(2,1)S(1)} all-to-all(f16[64,16,128]{2,1,0:T(8,128)(2,1)S(1)} %bitcast.5), channel_id=1, replica_groups={{0,2,4,6,8,10,12,14,16,18,20,22,24,26,28,30,32,34,36,38,40,42,44,46,48,..., dimensions={0} | all-to-all | bytes 524288 | tf_op jit(solution)/shard_map/all_to_all | solution.py:257
  84.1 0.1 fusion.1
  84.2 0.6 convert_element_type.16
Async XLA Ops:
  0.0 25.5 %collective-permute-start = (bf16[1024,256]{1,0:T(8,128)(2,1)}, bf16[1024,256]{1,0:T(8,128)(2,1)S(1)}, u32[]{:S(2)}, u32[]{:S(2)}) collective-permute-start(bf16[1024,256]{1,0:T(8,128)(2,1)} %amps0.1), channel_id=1, source_target_pairs={{256,0},{384,128},{0,256},{128,384},{257,1},{385,129},{1,257},{129... | collective-permute-start | bytes 1572872 | tf_op jit(solution)/shard_map/ppermute | solution.py:245
  7.7 48.7 %all-to-all-start = ((bf16[128,16,256]{2,1,0:T(8,128)(2,1)}), bf16[128,16,256]{2,1,0:T(8,128)(2,1)S(1)}, u32[]{:S(2)}, u32[]{:S(2)}) async-start(bf16[128,16,256]{2,1,0:T(8,128)(2,1)} %pack.1), calls=%async_computation | async-start | bytes 2097152 | tf_op jit(solution)/shard_map/all_to_all | solution.py:243
  25.5 2.4 %copy-start = (bf16[1024,256]{1,0:T(8,128)(2,1)S(1)}, bf16[1024,256]{1,0:T(8,128)(2,1)}, u32[]{:S(2)}) copy-start(bf16[1024,256]{1,0:T(8,128)(2,1)} %amps0.1) | copy-start | bytes 1572868
  28.0 15.3 %collective-permute-start.1 = (bf16[1024,256]{1,0:T(8,128)(2,1)S(1)}, bf16[1024,256]{1,0:T(8,128)(2,1)S(1)}, u32[]{:S(2)}, u32[]{:S(2)}) collective-permute-start(bf16[1024,256]{1,0:T(8,128)(2,1)S(1)} %copy-done), channel_id=1, source_target_pairs={{128,0},{256,128},{384,256},{0,384},{129,1},{257,129},{385,257},{1... | collective-permute-start | bytes 1572872 | tf_op jit(solution)/shard_map/ppermute | solution.py:245
  31.4 15.1 %collective-permute-start.2 = (bf16[1024,256]{1,0:T(8,128)(2,1)S(1)}, bf16[1024,256]{1,0:T(8,128)(2,1)S(1)}, u32[]{:S(2)}, u32[]{:S(2)}) collective-permute-start(bf16[1024,256]{1,0:T(8,128)(2,1)S(1)} %copy-done), channel_id=1, source_target_pairs={{384,0},{0,128},{128,256},{256,384},{385,1},{1,129},{129,257},{257... | collective-permute-start | bytes 1572872 | tf_op jit(solution)/shard_map/ppermute | solution.py:245
  59.6 3.8 %collective-permute-start.3 = (f32[1024,128]{1,0:T(8,128)S(1)}, f32[1024,128]{1,0:T(8,128)S(1)}, u32[]{:S(2)}, u32[]{:S(2)}) collective-permute-start(f32[1024,128]{1,0:T(8,128)S(1)} %get-tuple-element.16), channel_id=1, source_target_pairs={{0,1},{1,0},{2,3},{3,2},{4,5},{5,4},{6,7},{7,6},{8,9},{9,8},{10,11... | collective-permute-start | bytes 1572872 | tf_op jit(solution)/shard_map/ppermute | solution.py:254

commit v6 on v5

--- a/solution.py
+++ b/solution.py
@@ -71,7 +71,7 @@
         copy.wait()
 
 
-def order_kernel(capacity, width, base_ref, owned, out, held, sem):
+def order_kernel(capacity, width, base_ref, owned, place_out, offsets_out, held, sem):
     copy = pltpu.make_async_copy(owned, held, sem)
     copy.start()
     base = base_ref[0]
@@ -81,10 +81,22 @@
     table = held[...]
     table = jnp.where(table < 0, beyond, table - base)
     below = jnp.zeros((holders, 128), F32)
+    ended = jnp.zeros((holders, 128), F32)
     for tile in range(total // 128):
-        below = below + jnp.where(table[:, tile * 128:(tile + 1) * 128] < 0, 1.0, 0.0)
+        part = table[:, tile * 128:(tile + 1) * 128]
+        below = below + jnp.where(part < 0, 1.0, 0.0)
+        ended = ended + jnp.where(part < width, 1.0, 0.0)
     ones = jnp.ones((128, 128), BF16)
-    start = jnp.dot(below.astype(BF16), ones, preferred_element_type=F32).astype(jnp.int32)
+    below = jnp.dot(below.astype(BF16), ones, preferred_element_type=F32)
+    ended = jnp.dot(ended.astype(BF16), ones, preferred_element_type=F32)
+    counts = (ended - below).astype(BF16)
+    rows = lax.broadcasted_iota(jnp.int32, (holders, holders), 0)
+    cols = lax.broadcasted_iota(jnp.int32, (holders, holders), 1)
+    earlier = jnp.where(cols < rows, 1.0, 0.0).astype(BF16)
+    first = jnp.dot(earlier, counts, preferred_element_type=F32).astype(jnp.int32)
+    offsets = jnp.sum(jnp.where(rows == cols, first, 0), axis=0, keepdims=True)
+    offsets_out[...] = jnp.broadcast_to(offsets, offsets_out.shape)
+    start = below.astype(jnp.int32)
     window = jnp.concatenate([table, jnp.full((holders, 128), beyond, jnp.int32)], axis=1)
     shift = total // 2
     while shift >= 128:
@@ -98,36 +110,44 @@
         taken = jnp.concatenate([taken, taken], axis=1)
         window = jnp.where(taken, pltpu.roll(window, 256 - shift, 1), window)
         shift //= 2
-    lane = lax.broadcasted_iota(jnp.int32, (holders, 128), 1)
-    spread = jnp.where(lane < capacity, window[:, :128], 0)
-    shift = capacity
-    while shift < 128:
-        spread = spread + pltpu.roll(spread, shift, 1)
-        shift *= 2
-    each = 128 // capacity
-    mine = lax.broadcasted_iota(jnp.int32, (each, 128), 0)
-    mine = mine == lax.broadcasted_iota(jnp.int32, (each, 128), 1) // capacity
-    columns = jnp.concatenate(
-        [
-            jnp.sum(jnp.where(mine, spread[at:at + each], 0), axis=0, keepdims=True)
-            for at in range(0, holders, each)
-        ],
-        axis=1,
-    )
-    out[...] = jnp.broadcast_to(columns, out.shape)
+    column = lax.broadcasted_iota(jnp.int32, (holders, width), 1)
+    place = jnp.zeros((holders, width), jnp.int32)
+    for slot in range(capacity):
+        here = window[:, slot:slot + 1] == column
+        place = place + jnp.where(here, first[:, :1] + slot, 0)
+    place = jnp.sum(place, axis=0, keepdims=True)
+    place_out[...] = jnp.broadcast_to(place, place_out.shape)
+
+
+def arrange_kernel(place, *refs):
+    blocks, outs = refs[:len(refs) // 2], refs[len(refs) // 2:]
+    width = place.shape[1]
+    chunk = 256
+    where_to = place[0:1, :]
+    for step in range(width // chunk):
+        wanted = lax.broadcasted_iota(jnp.int32, (chunk, width), 0) + step * chunk
+        pick = jnp.where(wanted == where_to, 1.0, 0.0).astype(BF16)
+        for block, out in zip(blocks, outs):
+            out[pl.ds(step * chunk, chunk), :] = jnp.dot(
+                pick, block[...], preferred_element_type=F32
+            ).astype(BF16)
 
 
 def multiply_kernel(
-    where_ref, received, columns, amps0, amps1, amps2, amps3, kept, given, left, amps, sems
+    where_ref, offsets, received, amps0, amps1, amps2, amps3, given, left_kept, rows_ref, left
 ):
     group, core = where_ref[0], where_ref[1]
     holders, capacity, pairs = received.shape
-    blocks, width, _ = amps.shape
-    copies = []
-    for step, part in enumerate((amps0, amps1, amps2, amps3)):
-        target = amps.at[lax.rem(group + step, blocks)]
-        copies.append(pltpu.make_async_copy(part, target, sems.at[step]))
-        copies[-1].start()
+    width = amps0.shape[0]
+    line = lax.broadcasted_iota(jnp.int32, (8, pairs), 0)
+    blank = jnp.zeros((8, pairs), F32)
+    for holder in range(holders):
+        start = offsets[0, holder]
+        aligned = pl.multiple_of((start >> 3) << 3, 8)
+        window = jnp.concatenate([received[holder].astype(F32), blank], axis=0)
+        window = pltpu.roll(window, start & 7, 0)
+        pltpu.store(rows_ref.at[pl.ds(aligned, 8)], window[:8], mask=line >= (start & 7))
+        rows_ref[pl.ds(aligned + 8, capacity), :] = window[8:]
     new = lax.broadcasted_iota(jnp.int32, (pairs, pairs), 0)
     old = lax.broadcasted_iota(jnp.int32, (pairs, pairs), 1)
     half = pairs // 2
@@ -137,28 +157,32 @@
     row = jnp.where(in_half < chips, 0, 1)
     chip = jnp.where(in_half < chips, in_half, in_half - chips)
     pick = jnp.where(old == 4 * chip + 2 * side + row, 1.0, 0.0).astype(BF16)
-    slot_count = holders * capacity
-    slots = lax.dot_general(
-        pick, received[...].reshape(slot_count, pairs), NT, preferred_element_type=F32
-    ).astype(BF16)
-    place = columns[0:1, :]
     chunk = 256
     for step in range(width // chunk):
-        wanted = lax.broadcasted_iota(jnp.int32, (chunk, slot_count), 0) + step * chunk
-        order = jnp.where(wanted == place, 1.0, 0.0).astype(BF16)
         left[:, step * chunk:(step + 1) * chunk] = lax.dot_general(
-            slots, order, NT, preferred_element_type=F32
+            pick,
+            rows_ref[pl.ds(step * chunk, chunk), :].astype(BF16),
+            NT,
+            preferred_element_type=F32,
         ).astype(BF16)
-    for copy in copies:
-        copy.wait()
-    for block in range(blocks):
-        product = jnp.dot(left[...], amps[block], preferred_element_type=F32)
-        for target, at in ((kept, 0), (given, half)):
-            for r in range(2):
-                for h in range(2):
-                    target[pl.ds(r * 8 + 2 * block + h, chips, stride=16), :] = product[
-                        at + r * chips:at + (r + 1) * chips, h * 128:(h + 1) * 128
-                    ]
+    left_kept[...] = left[:half, :]
+    cut_product(group, left[half:, :], (amps0, amps1, amps2, amps3), given)
+
+
+def cut_product(group, left, blocks, target):
+    chips = left.shape[0] // 2
+    for step, amps in enumerate(blocks):
+        block = lax.rem(group + step, 4)
+        product = jnp.dot(left, amps[...], preferred_element_type=F32)
+        for r in range(2):
+            for h in range(2):
+                target[pl.ds(r * 8 + 2 * block + h, chips, stride=16), :] = product[
+                    r * chips:(r + 1) * chips, h * 128:(h + 1) * 128
+                ]
+
+
+def keep_kernel(where_ref, left, amps0, amps1, amps2, amps3, kept):
+    cut_product(where_ref[0], left[...], (amps0, amps1, amps2, amps3), kept)
 
 
 def pack(where, owned_columns, ladder_ints, devices, capacity):
@@ -186,36 +210,72 @@
     holders, _ = owned_columns.shape
     return pl.pallas_call(
         lambda *refs: order_kernel(capacity, width, *refs),
-        out_shape=jax.ShapeDtypeStruct((8, holders * capacity), jnp.int32),
+        out_shape=[
+            jax.ShapeDtypeStruct((8, width), jnp.int32),
+            jax.ShapeDtypeStruct((8, holders), jnp.int32),
+        ],
         in_specs=[SMEM, HBM],
-        out_specs=VMEM,
+        out_specs=[VMEM, VMEM],
         scratch_shapes=[
             pltpu.VMEM(owned_columns.shape, jnp.int32),
             pltpu.SemaphoreType.DMA,
         ],
         compiler_params=pltpu.CompilerParams(vmem_limit_bytes=VMEM_LIMIT),
         name="order",
-        cost_estimate=pl.CostEstimate(flops=15_000_000_000, bytes_accessed=1_000_000, transcendentals=0),
+        cost_estimate=pl.CostEstimate(
+            flops=15_000_000_000, bytes_accessed=1_000_000, transcendentals=0
+        ),
     )(base, in_hbm(owned_columns))
 
 
-def multiply(where, received, columns, amps0, amps1, amps2, amps3):
-    pairs = received.shape[2]
-    width, pairs_ij = amps0.shape
-    out = jax.ShapeDtypeStruct((pairs // 2 * 4 * pairs_ij // 128, 128), F32)
+def arrange(place, *blocks):
+    return pl.pallas_call(
+        arrange_kernel,
+        out_shape=[jax.ShapeDtypeStruct(block.shape, block.dtype) for block in blocks],
+        in_specs=[VMEM] * (1 + len(blocks)),
+        out_specs=[VMEM] * len(blocks),
+        compiler_params=pltpu.CompilerParams(vmem_limit_bytes=VMEM_LIMIT),
+        name="arrange",
+        cost_estimate=pl.CostEstimate(
+            flops=2_000_000_000, bytes_accessed=2_000_000, transcendentals=0
+        ),
+    )(place, *blocks)
+
+
+def multiply(where, offsets, received, *amps):
+    _, capacity, pairs = received.shape
+    width, pairs_ij = amps[0].shape
     return pl.pallas_call(
         multiply_kernel,
-        out_shape=[out, out],
-        in_specs=[SMEM, VMEM, VMEM] + [ANY] * 4,
+        out_shape=[
+            jax.ShapeDtypeStruct((pairs // 2 * 4 * pairs_ij // 128, 128), F32),
+            jax.ShapeDtypeStruct((pairs // 2, width), BF16),
+        ],
+        in_specs=[SMEM, SMEM] + [VMEM] * 5,
         out_specs=[VMEM, VMEM],
         scratch_shapes=[
+            pltpu.VMEM((width + capacity + 8, pairs), F32),
             pltpu.VMEM((pairs, width), BF16),
-            pltpu.VMEM((4, width, pairs_ij), BF16),
-            pltpu.SemaphoreType.DMA((4,)),
         ],
         compiler_params=pltpu.CompilerParams(vmem_limit_bytes=VMEM_LIMIT),
         name="multiply",
-    )(where, received, columns, amps0, amps1, amps2, amps3)
+    )(where, offsets, received, *amps)
+
+
+def keep(where, left, *amps):
+    half, _ = left.shape
+    _, pairs_ij = amps[0].shape
+    return pl.pallas_call(
+        keep_kernel,
+        out_shape=jax.ShapeDtypeStruct((half * 4 * pairs_ij // 128, 128), F32),
+        in_specs=[SMEM] + [VMEM] * 5,
+        out_specs=VMEM,
+        compiler_params=pltpu.CompilerParams(vmem_limit_bytes=VMEM_LIMIT),
+        name="keep",
+        cost_estimate=pl.CostEstimate(
+            flops=1_000_000_000, bytes_accessed=3_000_000, transcendentals=0
+        ),
+    )(where, left, *amps)
 
 
 SCALE = 2.0 ** 22
@@ -245,12 +305,14 @@
         return lax.ppermute(value, "ij", [((i + step) % groups, i) for i in range(groups)])
 
     amps2 = from_group(amplitudes, 2)
-    base, amps2 = lax.optimization_barrier(((device * width)[None].astype(jnp.int32), amps2))
-    columns = order(base, owned_columns, capacity, width)
-    later, columns = lax.optimization_barrier((amplitudes, columns))
-    others = [from_group(later, 1), amps2, from_group(later, 3)]
+    place, offsets = order((device * width)[None].astype(jnp.int32), owned_columns, capacity, width)
+    later, amps2 = lax.optimization_barrier((amplitudes, amps2))
+    amps1, amps3 = from_group(later, 1), from_group(later, 3)
+    amps0, amps2 = arrange(place, amplitudes, amps2)
+    amps1, amps3 = arrange(place, amps1, amps3)
     where = jnp.stack([group, lax.rem(device, 2)]).astype(jnp.int32)
-    kept, given = multiply(where, incoming, columns, amplitudes, *others)
+    given, left = multiply(where, offsets, incoming, amps0, amps1, amps2, amps3)
+    kept = keep(where, left, amps0, amps1, amps2, amps3)
     taken = lax.ppermute(given, "cd", [(i, i ^ 1) for i in range(devices_cd)])
     both = squeeze(kept + taken).reshape(devices_cd // 2, 16, 128)
     same_core = [[2 * k + c for k in range(devices_cd // 2)] for c in range(2)]

time: 85.2 us -> 84.1 us (0.987)
  waiting for transfers between devices: 24.3 us -> 18.4 us
  Pallas kernels: 9.21 us -> 13.8 us
    ppermute x3, waiting for transfers between devices: 12.5 us -> 6.6 us  [from_group(): lax.ppermute(value, 'ij', [((i + step) % groups, i) for i in range(groups)])]
    pallas_call x1 -> x4, Pallas kernels: 3.21 us -> 6.66 us  [the longest x2 3.7 us: arrange(): pl.pallas_call(arrange_kernel, out_shape=[jax.ShapeDtypeStruct(block.shap...]
    pallas_call x1, Pallas kernels: 2.42 us -> 3.57 us  [order(): pl.pallas_call(lambda *refs: order_kernel(capacity, width, *refs), out_sh...]
    ppermute x1, waiting for transfers between devices: 1.88 us -> 0.83 us  [body(): taken = lax.ppermute(given, 'cd', [(i, i ^ 1) for i in range(devices_cd)])]
    all_to_all x1, waiting for transfers between devices: 9.99 us -> 11 us  [body(): lax.all_to_all(outgoing, 'cd', split_axis=0, concat_axis=0, tiled=True)]
  transfers between devices with their start and end apart: 5 -> 5, of which waited for: 4 -> 4; matrix products, arithmetic and copies ran while one was open for 0% -> 0% of each run, Pallas kernels for 7% -> 14%
where the time goes in v6:
time: 84.1 us; the launch traced here: 83.7 us
  starting transfers between devices  29.7 us (35%)
  blocking collectives  20.3 us (24%)
  waiting for transfers between devices  18.4 us (22%)
  Pallas kernels  13.8 us (16%)
    all_to_all x1, blocking collectives, body(): lax.all_to_all(both, 'cd', 0, 0, tiled=True, axis_index_groups=same_core)  20.3 us
    all_to_all x1, starting transfers between devices, body(): lax.all_to_all(outgoing, 'cd', split_axis=0, concat_axis=0, tiled=True)  18 us
    all_to_all x1, waiting for transfers between devices, body(): lax.all_to_all(outgoing, 'cd', split_axis=0, concat_axis=0, tiled=True)  11 us
    ppermute x3, starting transfers between devices, from_group(): lax.ppermute(value, 'ij', [((i + step) % groups, i) for i in range(groups)])  9.87 us
    ppermute x3, waiting for transfers between devices, from_group(): lax.ppermute(value, 'ij', [((i + step) % groups, i) for i in range(groups)])  6.6 us
    pallas_call x2, Pallas kernels, arrange(): pl.pallas_call(arrange_kernel, out_shape=[jax.ShapeDtypeStruct(block.shap...  3.7 us
    pallas_call x1, Pallas kernels, pack(): pl.pallas_call(pack_kernel, out_shape=jax.ShapeDtypeStruct((devices, capa...  3.58 us
    pallas_call x1, Pallas kernels, order(): pl.pallas_call(lambda *refs: order_kernel(capacity, width, *refs), out_sh...  3.57 us
  transfers between devices with their start and end apart: 5, of which 4 were waited for; matrix products, arithmetic and copies ran while one was open for 0% of the time, Pallas kernels for 14%

profile of v6, /device:TPU:2, one launch (start us, length us, event | category | flops | bytes accessed | tf_op | source)
XLA Modules:
  0.0 83.7 jit_solution(14768591047747818886)
XLA Ops:
  0.0 4.0 %collective-permute-start = (bf16[1024,256]{1,0:T(8,128)(2,1)}, bf16[1024,256]{1,0:T(8,128)(2,1)S(1)}, u32[]{:S(2)}, u32[]{:S(2)}) collective-permute-start(bf16[1024,256]{1,0:T(8,128)(2,1)} %refs_0_.1), channel_id=1, source_target_pairs={{256,0},{384,128},{0,256},{128,384},{257,1},{385,129},{1,257},{129... | collective-permute-start | bytes 1572872 | tf_op jit(solution)/shard_map/ppermute | solution.py:305
  4.0 0.1 pad_add_fusion.1.where_ref
  4.1 3.6 %pack.1 = bf16[128,16,256]{2,1,0:T(8,128)(2,1)} custom-call(s32[2]{0:T(128)S(1)} %pad_add_fusion.1.where_ref, s32[128,2048]{1,0:T(8,128)} %owned.1, bf16[256,2048]{1,0:T(8,128)(2,1)} %ints.1), custom_call_target="tpu_custom_call" | custom-call | tf_op jit(solution)/shard_map/pack/pallas_call | solution.py:190
  7.7 0.0 copy-start
  7.7 18.0 %all-to-all-start = ((bf16[128,16,256]{2,1,0:T(8,128)(2,1)}), bf16[128,16,256]{2,1,0:T(8,128)(2,1)S(1)}, u32[]{:S(2)}, u32[]{:S(2)}) async-start(bf16[128,16,256]{2,1,0:T(8,128)(2,1)} %pack.1), calls=%async_computation | async-start | bytes 2097152 | tf_op jit(solution)/shard_map/all_to_all | solution.py:303
  25.7 0.0 collective-permute-done.refs_1_
  25.7 0.0 copy-done
  25.7 1.9 %collective-permute-start.2 = (bf16[1024,256]{1,0:T(8,128)(2,1)S(1)}, bf16[1024,256]{1,0:T(8,128)(2,1)}, u32[]{:S(2)}, u32[]{:S(2)}) collective-permute-start(bf16[1024,256]{1,0:T(8,128)(2,1)S(1)} %copy-done), channel_id=1, source_target_pairs={{384,0},{0,128},{128,256},{256,384},{385,1},{1,129},{129,257},{257... | collective-permute-start | bytes 1572872 | tf_op jit(solution)/shard_map/ppermute | solution.py:305
  27.6 3.9 %collective-permute-start.1 = (bf16[1024,256]{1,0:T(8,128)(2,1)S(1)}, bf16[1024,256]{1,0:T(8,128)(2,1)}, u32[]{:S(2)}, u32[]{:S(2)}) collective-permute-start(bf16[1024,256]{1,0:T(8,128)(2,1)S(1)} %copy-done), channel_id=1, source_target_pairs={{128,0},{256,128},{384,256},{0,384},{129,1},{257,129},{385,257},{1... | collective-permute-start | bytes 1572872 | tf_op jit(solution)/shard_map/ppermute | solution.py:305
  31.6 3.6 %order.1 = (s32[8,1024]{1,0:T(8,128)S(1)}, s32[8,128]{1,0:T(8,128)S(1)}) custom-call(s32[1]{0:T(128)} %bitcast.2.refs_0_, s32[128,2048]{1,0:T(8,128)} %owned.1), custom_call_target="tpu_custom_call" | custom-call | flops 15000000512 | bytes 1000000 | tf_op jit(solution)/shard_map/order/pallas_call | solution.py:211
  35.1 0.1 pad_add_fusion.where_ref
  35.2 1.2 %arrange.2 = (bf16[1024,256]{1,0:T(8,128)(2,1)S(1)}, bf16[1024,256]{1,0:T(8,128)(2,1)S(1)}) custom-call(s32[8,1024]{1,0:T(8,128)S(1)} %get-tuple-element.16.place, bf16[1024,256]{1,0:T(8,128)(2,1)S(1)} %copy-done, bf16[1024,256]{1,0:T(8,128)(2,1)S(1)} %collective-permute-done.refs_1_), custom_call_target="tpu_custom_call" | custom-call | flops 2000000000 | bytes 2000000 | tf_op jit(solution)/shard_map/arrange/pallas_call | solution.py:232
  36.5 4.7 %collective-permute-done.2.refs_1_ = bf16[1024,256]{1,0:T(8,128)(2,1)} collective-permute-done((bf16[1024,256]{1,0:T(8,128)(2,1)S(1)}, bf16[1024,256]{1,0:T(8,128)(2,1)}, u32[]{:S(2)}, u32[]{:S(2)}) %collective-permute-start.2) | collective-permute-done | bytes 524320 | tf_op jit(solution)/shard_map/ppermute | solution.py:305
  41.1 1.9 %collective-permute-done.1.refs_0_ = bf16[1024,256]{1,0:T(8,128)(2,1)} collective-permute-done((bf16[1024,256]{1,0:T(8,128)(2,1)S(1)}, bf16[1024,256]{1,0:T(8,128)(2,1)}, u32[]{:S(2)}, u32[]{:S(2)}) %collective-permute-start.1) | collective-permute-done | bytes 524320 | tf_op jit(solution)/shard_map/ppermute | solution.py:305
  43.1 2.4 %arrange.3 = (bf16[1024,256]{1,0:T(8,128)(2,1)S(1)}, bf16[1024,256]{1,0:T(8,128)(2,1)S(1)}) custom-call(s32[8,1024]{1,0:T(8,128)S(1)} %get-tuple-element.16.place, bf16[1024,256]{1,0:T(8,128)(2,1)} %collective-permute-done.1.refs_0_, bf16[1024,256]{1,0:T(8,128)(2,1)} %collective-permute-done.2.refs_1_), custom_call_target="tpu_custom_call" | custom-call | flops 2000000000 | bytes 2000000 | tf_op jit(solution)/shard_map/arrange/pallas_call | solution.py:232
  45.5 11.0 %all-to-all-done.received = bf16[128,16,256]{2,1,0:T(8,128)(2,1)S(1)} async-done(((bf16[128,16,256]{2,1,0:T(8,128)(2,1)}), bf16[128,16,256]{2,1,0:T(8,128)(2,1)S(1)}, u32[]{:S(2)}, u32[]{:S(2)}) %all-to-all-start) | async-done | bytes 1048608 | tf_op jit(solution)/shard_map/all_to_all | solution.py:303
  56.5 1.9 %multiply.1 = (f32[1024,128]{1,0:T(8,128)S(1)}, bf16[128,1024]{1,0:T(8,128)(2,1)S(1)}) custom-call(s32[2]{0:T(128)S(1)} %pad_add_fusion.where_ref, s32[8,128]{1,0:T(8,128)S(1)} %get-tuple-element.15.offsets, bf16[128,16,256]{2,1,0:T(8,128)(2,1)S(1)} %all-to-all-done.received, bf16[1024,256]{1,0:T(8,128)(2,1)S(1)} %get-tuple-element.18.amps0, ...), custom_call_target="tpu_custom_call" | custom-call | tf_op jit(solution)/shard_map/multiply/pallas_call | solution.py:248
  58.5 1.9 %collective-permute-start.3 = (f32[1024,128]{1,0:T(8,128)S(1)}, f32[1024,128]{1,0:T(8,128)S(1)}, u32[]{:S(2)}, u32[]{:S(2)}) collective-permute-start(f32[1024,128]{1,0:T(8,128)S(1)} %get-tuple-element.24), channel_id=1, source_target_pairs={{0,1},{1,0},{2,3},{3,2},{4,5},{5,4},{6,7},{7,6},{8,9},{9,8},{10,11... | collective-permute-start | bytes 1572872 | tf_op jit(solution)/shard_map/ppermute | solution.py:316
  60.4 1.0 %keep.1 = f32[1024,128]{1,0:T(8,128)S(1)} custom-call(s32[2]{0:T(128)S(1)} %pad_add_fusion.where_ref, bf16[128,1024]{1,0:T(8,128)(2,1)S(1)} %get-tuple-element.23.left, bf16[1024,256]{1,0:T(8,128)(2,1)S(1)} %get-tuple-element.18.amps0, bf16[1024,256]{1,0:T(8,128)(2,1)S(1)} %get-tuple-element.20.amps1, bf16[1024,256]{1,0:T(8,128)(2,1)S(1)} %get-tuple-element.21.amps2, ...), custom_call_target="tpu_custom_call" | custom-call | flops 1000000000 | bytes 3000000 | tf_op jit(solution)/shard_map/keep/pallas_call | solution.py:268
  61.5 0.8 collective-permute-done.3
  62.3 0.3 multiply_convert_fusion
  62.6 20.3 %all_to_all.10 = f16[64,16,128]{2,1,0:T(8,128)(2,1)S(1)} all-to-all(f16[64,16,128]{2,1,0:T(8,128)(2,1)S(1)} %bitcast.5), channel_id=1, replica_groups={{0,2,4,6,8,10,12,14,16,18,20,22,24,26,28,30,32,34,36,38,40,42,44,46,48,..., dimensions={0} | all-to-all | bytes 524288 | tf_op jit(solution)/shard_map/all_to_all | solution.py:319
  83.0 0.1 fusion.1
  83.1 0.6 convert_element_type.16
Async XLA Ops:
  0.0 25.7 %collective-permute-start = (bf16[1024,256]{1,0:T(8,128)(2,1)}, bf16[1024,256]{1,0:T(8,128)(2,1)S(1)}, u32[]{:S(2)}, u32[]{:S(2)}) collective-permute-start(bf16[1024,256]{1,0:T(8,128)(2,1)} %refs_0_.1), channel_id=1, source_target_pairs={{256,0},{384,128},{0,256},{128,384},{257,1},{385,129},{1,257},{129... | collective-permute-start | bytes 1572872 | tf_op jit(solution)/shard_map/ppermute | solution.py:305
  7.7 18.0 %copy-start = (bf16[1024,256]{1,0:T(8,128)(2,1)S(1)}, bf16[1024,256]{1,0:T(8,128)(2,1)}, u32[]{:S(2)}) copy-start(bf16[1024,256]{1,0:T(8,128)(2,1)} %refs_0_.1) | copy-start | bytes 1572868
  7.7 48.8 %all-to-all-start = ((bf16[128,16,256]{2,1,0:T(8,128)(2,1)}), bf16[128,16,256]{2,1,0:T(8,128)(2,1)S(1)}, u32[]{:S(2)}, u32[]{:S(2)}) async-start(bf16[128,16,256]{2,1,0:T(8,128)(2,1)} %pack.1), calls=%async_computation | async-start | bytes 2097152 | tf_op jit(solution)/shard_map/all_to_all | solution.py:303
  25.7 15.4 %collective-permute-start.2 = (bf16[1024,256]{1,0:T(8,128)(2,1)S(1)}, bf16[1024,256]{1,0:T(8,128)(2,1)}, u32[]{:S(2)}, u32[]{:S(2)}) collective-permute-start(bf16[1024,256]{1,0:T(8,128)(2,1)S(1)} %copy-done), channel_id=1, source_target_pairs={{384,0},{0,128},{128,256},{256,384},{385,1},{1,129},{129,257},{257... | collective-permute-start | bytes 1572872 | tf_op jit(solution)/shard_map/ppermute | solution.py:305
  27.6 15.4 %collective-permute-start.1 = (bf16[1024,256]{1,0:T(8,128)(2,1)S(1)}, bf16[1024,256]{1,0:T(8,128)(2,1)}, u32[]{:S(2)}, u32[]{:S(2)}) collective-permute-start(bf16[1024,256]{1,0:T(8,128)(2,1)S(1)} %copy-done), channel_id=1, source_target_pairs={{128,0},{256,128},{384,256},{0,384},{129,1},{257,129},{385,257},{1... | collective-permute-start | bytes 1572872 | tf_op jit(solution)/shard_map/ppermute | solution.py:305
  58.5 3.8 %collective-permute-start.3 = (f32[1024,128]{1,0:T(8,128)S(1)}, f32[1024,128]{1,0:T(8,128)S(1)}, u32[]{:S(2)}, u32[]{:S(2)}) collective-permute-start(f32[1024,128]{1,0:T(8,128)S(1)} %get-tuple-element.24), channel_id=1, source_target_pairs={{0,1},{1,0},{2,3},{3,2},{4,5},{5,4},{6,7},{7,6},{8,9},{9,8},{10,11... | collective-permute-start | bytes 1572872 | tf_op jit(solution)/shard_map/ppermute | solution.py:316

commit v7 on v6

--- a/solution.py
+++ b/solution.py
@@ -19,8 +19,8 @@
     return pltpu.with_memory_space_constraint(value, pltpu.HBM)
 
 
-def pack_kernel(where_ref, owned, ints, out, group, staged, slots, firsts, starts, windows, sems):
-    device, width = where_ref[0], where_ref[1]
+def pack_kernel(width, owned, ints, out, group, staged, slots, firsts, starts, windows, sems):
+    device = lax.axis_index("cd")
     devices, capacity, _ = out.shape
     total, chunk = ints.shape[1], 256
     eight = pl.multiple_of((device >> 3) << 3, 8)
@@ -71,10 +71,10 @@
         copy.wait()
 
 
-def order_kernel(capacity, width, base_ref, owned, place_out, offsets_out, held, sem):
+def order_kernel(capacity, width, owned, place_out, offsets_out, held, sem):
     copy = pltpu.make_async_copy(owned, held, sem)
     copy.start()
-    base = base_ref[0]
+    base = lax.axis_index("cd") * width
     holders, total = owned.shape
     beyond = jnp.int32(1 << 30)
     copy.wait()
@@ -134,9 +134,9 @@
 
 
 def multiply_kernel(
-    where_ref, offsets, received, amps0, amps1, amps2, amps3, given, left_kept, rows_ref, left
+    offsets, received, amps0, amps1, amps2, amps3, given, left_kept, rows_ref, left
 ):
-    group, core = where_ref[0], where_ref[1]
+    group, core = lax.axis_index("ij"), lax.rem(lax.axis_index("cd"), 2)
     holders, capacity, pairs = received.shape
     width = amps0.shape[0]
     line = lax.broadcasted_iota(jnp.int32, (8, pairs), 0)
@@ -181,16 +181,16 @@
                 ]
 
 
-def keep_kernel(where_ref, left, amps0, amps1, amps2, amps3, kept):
-    cut_product(where_ref[0], left[...], (amps0, amps1, amps2, amps3), kept)
-
-
-def pack(where, owned_columns, ladder_ints, devices, capacity):
+def keep_kernel(left, amps0, amps1, amps2, amps3, kept):
+    cut_product(lax.axis_index("ij"), left[...], (amps0, amps1, amps2, amps3), kept)
+
+
+def pack(owned_columns, ladder_ints, devices, capacity, width):
     pairs, total = ladder_ints.shape
     return pl.pallas_call(
-        pack_kernel,
+        lambda *refs: pack_kernel(width, *refs),
         out_shape=jax.ShapeDtypeStruct((devices, capacity, pairs), BF16),
-        in_specs=[SMEM, HBM, HBM],
+        in_specs=[HBM, HBM],
         out_specs=HBM,
         scratch_shapes=[
             pltpu.VMEM((8, total), jnp.int32),
@@ -203,10 +203,10 @@
         ],
         compiler_params=pltpu.CompilerParams(vmem_limit_bytes=VMEM_LIMIT),
         name="pack",
-    )(where, in_hbm(owned_columns), in_hbm(ladder_ints))
-
-
-def order(base, owned_columns, capacity, width):
+    )(in_hbm(owned_columns), in_hbm(ladder_ints))
+
+
+def order(owned_columns, capacity, width):
     holders, _ = owned_columns.shape
     return pl.pallas_call(
         lambda *refs: order_kernel(capacity, width, *refs),
@@ -214,7 +214,7 @@
             jax.ShapeDtypeStruct((8, width), jnp.int32),
             jax.ShapeDtypeStruct((8, holders), jnp.int32),
         ],
-        in_specs=[SMEM, HBM],
+        in_specs=[HBM],
         out_specs=[VMEM, VMEM],
         scratch_shapes=[
             pltpu.VMEM(owned_columns.shape, jnp.int32),
@@ -225,7 +225,7 @@
         cost_estimate=pl.CostEstimate(
             flops=15_000_000_000, bytes_accessed=1_000_000, transcendentals=0
         ),
-    )(base, in_hbm(owned_columns))
+    )(in_hbm(owned_columns))
 
 
 def arrange(place, *blocks):
@@ -242,7 +242,7 @@
     )(place, *blocks)
 
 
-def multiply(where, offsets, received, *amps):
+def multiply(offsets, received, *amps):
     _, capacity, pairs = received.shape
     width, pairs_ij = amps[0].shape
     return pl.pallas_call(
@@ -251,7 +251,7 @@
             jax.ShapeDtypeStruct((pairs // 2 * 4 * pairs_ij // 128, 128), F32),
             jax.ShapeDtypeStruct((pairs // 2, width), BF16),
         ],
-        in_specs=[SMEM, SMEM] + [VMEM] * 5,
+        in_specs=[SMEM] + [VMEM] * 5,
         out_specs=[VMEM, VMEM],
         scratch_shapes=[
             pltpu.VMEM((width + capacity + 8, pairs), F32),
@@ -259,23 +259,23 @@
         ],
         compiler_params=pltpu.CompilerParams(vmem_limit_bytes=VMEM_LIMIT),
         name="multiply",
-    )(where, offsets, received, *amps)
-
-
-def keep(where, left, *amps):
+    )(offsets, received, *amps)
+
+
+def keep(left, *amps):
     half, _ = left.shape
     _, pairs_ij = amps[0].shape
     return pl.pallas_call(
         keep_kernel,
         out_shape=jax.ShapeDtypeStruct((half * 4 * pairs_ij // 128, 128), F32),
-        in_specs=[SMEM] + [VMEM] * 5,
+        in_specs=[VMEM] * 5,
         out_specs=VMEM,
         compiler_params=pltpu.CompilerParams(vmem_limit_bytes=VMEM_LIMIT),
         name="keep",
         cost_estimate=pl.CostEstimate(
             flops=1_000_000_000, bytes_accessed=3_000_000, transcendentals=0
         ),
-    )(where, left, *amps)
+    )(left, *amps)
 
 
 SCALE = 2.0 ** 22
@@ -291,28 +291,24 @@
 
 
 def body(amplitudes, owned_columns, ladder_ints):
-    device = lax.axis_index("cd")
-    group = lax.axis_index("ij")
     devices_cd = lax.axis_size("cd")
     groups = lax.axis_size("ij")
     width = amplitudes.shape[0]
     capacity = 2 * width // devices_cd
 
-    own = jnp.stack([device, jnp.int32(width)]).astype(jnp.int32)
-    outgoing = pack(own, owned_columns, ladder_ints, devices_cd, capacity)
+    outgoing = pack(owned_columns, ladder_ints, devices_cd, capacity, width)
     incoming = lax.all_to_all(outgoing, "cd", split_axis=0, concat_axis=0, tiled=True)
     def from_group(value, step):
         return lax.ppermute(value, "ij", [((i + step) % groups, i) for i in range(groups)])
 
     amps2 = from_group(amplitudes, 2)
-    place, offsets = order((device * width)[None].astype(jnp.int32), owned_columns, capacity, width)
+    place, offsets = order(owned_columns, capacity, width)
     later, amps2 = lax.optimization_barrier((amplitudes, amps2))
     amps1, amps3 = from_group(later, 1), from_group(later, 3)
     amps0, amps2 = arrange(place, amplitudes, amps2)
     amps1, amps3 = arrange(place, amps1, amps3)
-    where = jnp.stack([group, lax.rem(device, 2)]).astype(jnp.int32)
-    given, left = multiply(where, offsets, incoming, amps0, amps1, amps2, amps3)
-    kept = keep(where, left, amps0, amps1, amps2, amps3)
+    given, left = multiply(offsets, incoming, amps0, amps1, amps2, amps3)
+    kept = keep(left, amps0, amps1, amps2, amps3)
     taken = lax.ppermute(given, "cd", [(i, i ^ 1) for i in range(devices_cd)])
     both = squeeze(kept + taken).reshape(devices_cd // 2, 16, 128)
     same_core = [[2 * k + c for k in range(devices_cd // 2)] for c in range(2)]

time: 84.1 us -> 83.4 us (level)
  Pallas kernels: 13.8 us -> 11.5 us
  waiting for transfers between devices: 18.4 us -> 20.3 us
    all_to_all x1, waiting for transfers between devices: 11 us -> 12.3 us  [body(): lax.all_to_all(outgoing, 'cd', split_axis=0, concat_axis=0, tiled=True)]
    pallas_call x2, Pallas kernels: 3.7 us -> 2.5 us  [arrange(): pl.pallas_call(arrange_kernel, out_shape=[jax.ShapeDtypeStruct(block.shap...]
  transfers between devices with their start and end apart: 5 -> 5, of which waited for: 4 -> 4; matrix products, arithmetic and copies ran while one was open for 0% -> 0% of each run, Pallas kernels for 14% -> 12%
where the time goes in v7:
time: 83.4 us; the launch traced here: 83.1 us
  starting transfers between devices  29.7 us (36%)
  waiting for transfers between devices  20.3 us (24%)
  blocking collectives  20.3 us (24%)
  Pallas kernels  11.5 us (14%)
    all_to_all x1, blocking collectives, body(): lax.all_to_all(both, 'cd', 0, 0, tiled=True, axis_index_groups=same_core)  20.3 us
    all_to_all x1, starting transfers between devices, body(): lax.all_to_all(outgoing, 'cd', split_axis=0, concat_axis=0, tiled=True)  17.9 us
    all_to_all x1, waiting for transfers between devices, body(): lax.all_to_all(outgoing, 'cd', split_axis=0, concat_axis=0, tiled=True)  12.3 us
    ppermute x3, starting transfers between devices, from_group(): lax.ppermute(value, 'ij', [((i + step) % groups, i) for i in range(groups)])  9.87 us
    ppermute x3, waiting for transfers between devices, from_group(): lax.ppermute(value, 'ij', [((i + step) % groups, i) for i in range(groups)])  6.58 us
    pallas_call x1, Pallas kernels, order(): pl.pallas_call(lambda *refs: order_kernel(capacity, width, *refs), out_sh...  3.57 us
    pallas_call x1, Pallas kernels, pack(): pl.pallas_call(lambda *refs: pack_kernel(width, *refs), out_shape=jax.Sha...  3.04 us
    pallas_call x2, Pallas kernels, arrange(): pl.pallas_call(arrange_kernel, out_shape=[jax.ShapeDtypeStruct(block.shap...  2.5 us
  transfers between devices with their start and end apart: 5, of which 4 were waited for; matrix products, arithmetic and copies ran while one was open for 0% of the time, Pallas kernels for 12%

profile of v7, /device:TPU:2, one launch (start us, length us, event | category | flops | bytes accessed | tf_op | source)
XLA Modules:
  0.0 83.1 jit_solution(3924815407329721418)
XLA Ops:
  0.0 4.0 %collective-permute-start = (bf16[1024,256]{1,0:T(8,128)(2,1)}, bf16[1024,256]{1,0:T(8,128)(2,1)S(1)}, u32[]{:S(2)}, u32[]{:S(2)}) collective-permute-start(bf16[1024,256]{1,0:T(8,128)(2,1)} %refs_0_.5), channel_id=1, source_target_pairs={{256,0},{384,128},{0,256},{128,384},{257,1},{385,129},{1,257},{129... | collective-permute-start | bytes 1572872 | tf_op jit(solution)/shard_map/ppermute | solution.py:302
  4.0 3.0 %pack.1 = bf16[128,16,256]{2,1,0:T(8,128)(2,1)} custom-call(s32[128,2048]{1,0:T(8,128)} %refs_0_.4, bf16[256,2048]{1,0:T(8,128)(2,1)} %refs_1_.1), custom_call_target="tpu_custom_call" | custom-call | tf_op jit(solution)/shard_map/pack/pallas_call | solution.py:190
  7.1 0.0 copy-start
  7.1 17.9 %all-to-all-start = ((bf16[128,16,256]{2,1,0:T(8,128)(2,1)}), bf16[128,16,256]{2,1,0:T(8,128)(2,1)S(1)}, u32[]{:S(2)}, u32[]{:S(2)}) async-start(bf16[128,16,256]{2,1,0:T(8,128)(2,1)} %pack.1), calls=%async_computation | async-start | bytes 2097152 | tf_op jit(solution)/shard_map/all_to_all | solution.py:300
  25.1 0.0 collective-permute-done.refs_1_
  25.1 0.0 copy-done
  25.1 1.9 %collective-permute-start.2 = (bf16[1024,256]{1,0:T(8,128)(2,1)S(1)}, bf16[1024,256]{1,0:T(8,128)(2,1)S(1)}, u32[]{:S(2)}, u32[]{:S(2)}) collective-permute-start(bf16[1024,256]{1,0:T(8,128)(2,1)S(1)} %copy-done), channel_id=1, source_target_pairs={{384,0},{0,128},{128,256},{256,384},{385,1},{1,129},{129,257},{257... | collective-permute-start | bytes 1572872 | tf_op jit(solution)/shard_map/ppermute | solution.py:302
  27.0 3.9 %collective-permute-start.1 = (bf16[1024,256]{1,0:T(8,128)(2,1)S(1)}, bf16[1024,256]{1,0:T(8,128)(2,1)S(1)}, u32[]{:S(2)}, u32[]{:S(2)}) collective-permute-start(bf16[1024,256]{1,0:T(8,128)(2,1)S(1)} %copy-done), channel_id=1, source_target_pairs={{128,0},{256,128},{384,256},{0,384},{129,1},{257,129},{385,257},{1... | collective-permute-start | bytes 1572872 | tf_op jit(solution)/shard_map/ppermute | solution.py:302
  30.9 3.6 %order.1 = (s32[8,1024]{1,0:T(8,128)S(1)}, s32[8,128]{1,0:T(8,128)S(1)}) custom-call(s32[128,2048]{1,0:T(8,128)} %refs_0_.4), custom_call_target="tpu_custom_call" | custom-call | flops 15000000512 | bytes 1000000 | tf_op jit(solution)/shard_map/order/pallas_call | solution.py:211
  34.5 1.3 %arrange.2 = (bf16[1024,256]{1,0:T(8,128)(2,1)S(1)}, bf16[1024,256]{1,0:T(8,128)(2,1)S(1)}) custom-call(s32[8,1024]{1,0:T(8,128)S(1)} %get-tuple-element.16.place, bf16[1024,256]{1,0:T(8,128)(2,1)S(1)} %copy-done, bf16[1024,256]{1,0:T(8,128)(2,1)S(1)} %collective-permute-done.refs_1_), custom_call_target="tpu_custom_call" | custom-call | flops 2000000000 | bytes 2000000 | tf_op jit(solution)/shard_map/arrange/pallas_call | solution.py:232
  35.8 4.6 %collective-permute-done.2.refs_1_ = bf16[1024,256]{1,0:T(8,128)(2,1)S(1)} collective-permute-done((bf16[1024,256]{1,0:T(8,128)(2,1)S(1)}, bf16[1024,256]{1,0:T(8,128)(2,1)S(1)}, u32[]{:S(2)}, u32[]{:S(2)}) %collective-permute-start.2) | collective-permute-done | bytes 524320 | tf_op jit(solution)/shard_map/ppermute | solution.py:302
  40.4 1.9 %collective-permute-done.1.refs_0_ = bf16[1024,256]{1,0:T(8,128)(2,1)S(1)} collective-permute-done((bf16[1024,256]{1,0:T(8,128)(2,1)S(1)}, bf16[1024,256]{1,0:T(8,128)(2,1)S(1)}, u32[]{:S(2)}, u32[]{:S(2)}) %collective-permute-start.1) | collective-permute-done | bytes 524320 | tf_op jit(solution)/shard_map/ppermute | solution.py:302
  42.3 1.2 %arrange.3 = (bf16[1024,256]{1,0:T(8,128)(2,1)S(1)}, bf16[1024,256]{1,0:T(8,128)(2,1)S(1)}) custom-call(s32[8,1024]{1,0:T(8,128)S(1)} %get-tuple-element.16.place, bf16[1024,256]{1,0:T(8,128)(2,1)S(1)} %collective-permute-done.1.refs_0_, bf16[1024,256]{1,0:T(8,128)(2,1)S(1)} %collective-permute-done.2.refs_1_), custom_call_target="tpu_custom_call" | custom-call | flops 2000000000 | bytes 2000000 | tf_op jit(solution)/shard_map/arrange/pallas_call | solution.py:232
  43.6 12.3 %all-to-all-done.received = bf16[128,16,256]{2,1,0:T(8,128)(2,1)S(1)} async-done(((bf16[128,16,256]{2,1,0:T(8,128)(2,1)}), bf16[128,16,256]{2,1,0:T(8,128)(2,1)S(1)}, u32[]{:S(2)}, u32[]{:S(2)}) %all-to-all-start) | async-done | bytes 1048608 | tf_op jit(solution)/shard_map/all_to_all | solution.py:300
  55.9 1.9 %multiply.1 = (f32[1024,128]{1,0:T(8,128)S(1)}, bf16[128,1024]{1,0:T(8,128)(2,1)S(1)}) custom-call(s32[8,128]{1,0:T(8,128)S(1)} %get-tuple-element.15.offsets, bf16[128,16,256]{2,1,0:T(8,128)(2,1)S(1)} %all-to-all-done.received, bf16[1024,256]{1,0:T(8,128)(2,1)S(1)} %get-tuple-element.18.amps0, bf16[1024,256]{1,0:T(8,128)(2,1)S(1)} %get-tuple-element.20.amps1, ...), custom_call_target="tpu_custom_call" | custom-call | tf_op jit(solution)/shard_map/multiply/pallas_call | solution.py:248
  57.9 1.9 %collective-permute-start.3 = (f32[1024,128]{1,0:T(8,128)S(1)}, f32[1024,128]{1,0:T(8,128)S(1)}, u32[]{:S(2)}, u32[]{:S(2)}) collective-permute-start(f32[1024,128]{1,0:T(8,128)S(1)} %get-tuple-element.24), channel_id=1, source_target_pairs={{0,1},{1,0},{2,3},{3,2},{4,5},{5,4},{6,7},{7,6},{8,9},{9,8},{10,11... | collective-permute-start | bytes 1572872 | tf_op jit(solution)/shard_map/ppermute | solution.py:312
  59.8 0.5 keep.1
  60.3 1.4 %collective-permute-done.3 = f32[1024,128]{1,0:T(8,128)S(1)} collective-permute-done((f32[1024,128]{1,0:T(8,128)S(1)}, f32[1024,128]{1,0:T(8,128)S(1)}, u32[]{:S(2)}, u32[]{:S(2)}) %collective-permute-start.3) | collective-permute-done | bytes 524320 | tf_op jit(solution)/shard_map/ppermute | solution.py:312
  61.7 0.3 multiply_convert_fusion
  62.0 20.3 %all_to_all.10 = f16[64,16,128]{2,1,0:T(8,128)(2,1)S(1)} all-to-all(f16[64,16,128]{2,1,0:T(8,128)(2,1)S(1)} %bitcast.1), channel_id=1, replica_groups={{0,2,4,6,8,10,12,14,16,18,20,22,24,26,28,30,32,34,36,38,40,42,44,46,48,..., dimensions={0} | all-to-all | bytes 524288 | tf_op jit(solution)/shard_map/all_to_all | solution.py:315
  82.4 0.1 fusion.1
  82.5 0.6 convert_element_type.16
Async XLA Ops:
  0.0 25.1 %collective-permute-start = (bf16[1024,256]{1,0:T(8,128)(2,1)}, bf16[1024,256]{1,0:T(8,128)(2,1)S(1)}, u32[]{:S(2)}, u32[]{:S(2)}) collective-permute-start(bf16[1024,256]{1,0:T(8,128)(2,1)} %refs_0_.5), channel_id=1, source_target_pairs={{256,0},{384,128},{0,256},{128,384},{257,1},{385,129},{1,257},{129... | collective-permute-start | bytes 1572872 | tf_op jit(solution)/shard_map/ppermute | solution.py:302
  7.1 18.0 %copy-start = (bf16[1024,256]{1,0:T(8,128)(2,1)S(1)}, bf16[1024,256]{1,0:T(8,128)(2,1)}, u32[]{:S(2)}) copy-start(bf16[1024,256]{1,0:T(8,128)(2,1)} %refs_0_.5) | copy-start | bytes 1572868
  7.1 48.8 %all-to-all-start = ((bf16[128,16,256]{2,1,0:T(8,128)(2,1)}), bf16[128,16,256]{2,1,0:T(8,128)(2,1)S(1)}, u32[]{:S(2)}, u32[]{:S(2)}) async-start(bf16[128,16,256]{2,1,0:T(8,128)(2,1)} %pack.1), calls=%async_computation | async-start | bytes 2097152 | tf_op jit(solution)/shard_map/all_to_all | solution.py:300
  25.1 15.3 %collective-permute-start.2 = (bf16[1024,256]{1,0:T(8,128)(2,1)S(1)}, bf16[1024,256]{1,0:T(8,128)(2,1)S(1)}, u32[]{:S(2)}, u32[]{:S(2)}) collective-permute-start(bf16[1024,256]{1,0:T(8,128)(2,1)S(1)} %copy-done), channel_id=1, source_target_pairs={{384,0},{0,128},{128,256},{256,384},{385,1},{1,129},{129,257},{257... | collective-permute-start | bytes 1572872 | tf_op jit(solution)/shard_map/ppermute | solution.py:302
  27.0 15.3 %collective-permute-start.1 = (bf16[1024,256]{1,0:T(8,128)(2,1)S(1)}, bf16[1024,256]{1,0:T(8,128)(2,1)S(1)}, u32[]{:S(2)}, u32[]{:S(2)}) collective-permute-start(bf16[1024,256]{1,0:T(8,128)(2,1)S(1)} %copy-done), channel_id=1, source_target_pairs={{128,0},{256,128},{384,256},{0,384},{129,1},{257,129},{385,257},{1... | collective-permute-start | bytes 1572872 | tf_op jit(solution)/shard_map/ppermute | solution.py:302
  57.9 3.8 %collective-permute-start.3 = (f32[1024,128]{1,0:T(8,128)S(1)}, f32[1024,128]{1,0:T(8,128)S(1)}, u32[]{:S(2)}, u32[]{:S(2)}) collective-permute-start(f32[1024,128]{1,0:T(8,128)S(1)} %get-tuple-element.24), channel_id=1, source_target_pairs={{0,1},{1,0},{2,3},{3,2},{4,5},{5,4},{6,7},{7,6},{8,9},{9,8},{10,11... | collective-permute-start | bytes 1572872 | tf_op jit(solution)/shard_map/ppermute | solution.py:312

commit v8 on v7

--- a/solution.py
+++ b/solution.py
@@ -139,15 +139,6 @@
     group, core = lax.axis_index("ij"), lax.rem(lax.axis_index("cd"), 2)
     holders, capacity, pairs = received.shape
     width = amps0.shape[0]
-    line = lax.broadcasted_iota(jnp.int32, (8, pairs), 0)
-    blank = jnp.zeros((8, pairs), F32)
-    for holder in range(holders):
-        start = offsets[0, holder]
-        aligned = pl.multiple_of((start >> 3) << 3, 8)
-        window = jnp.concatenate([received[holder].astype(F32), blank], axis=0)
-        window = pltpu.roll(window, start & 7, 0)
-        pltpu.store(rows_ref.at[pl.ds(aligned, 8)], window[:8], mask=line >= (start & 7))
-        rows_ref[pl.ds(aligned + 8, capacity), :] = window[8:]
     new = lax.broadcasted_iota(jnp.int32, (pairs, pairs), 0)
     old = lax.broadcasted_iota(jnp.int32, (pairs, pairs), 1)
     half = pairs // 2
@@ -158,13 +149,24 @@
     chip = jnp.where(in_half < chips, in_half, in_half - chips)
     pick = jnp.where(old == 4 * chip + 2 * side + row, 1.0, 0.0).astype(BF16)
     chunk = 256
-    for step in range(width // chunk):
-        left[:, step * chunk:(step + 1) * chunk] = lax.dot_general(
-            pick,
-            rows_ref[pl.ds(step * chunk, chunk), :].astype(BF16),
-            NT,
-            preferred_element_type=F32,
-        ).astype(BF16)
+    done = 0
+    line = lax.broadcasted_iota(jnp.int32, (8, pairs), 0)
+    blank = jnp.zeros((8, pairs), F32)
+    for holder in range(holders):
+        start = offsets[0, holder]
+        aligned = pl.multiple_of((start >> 3) << 3, 8)
+        window = jnp.concatenate([received[holder].astype(F32), blank], axis=0)
+        window = pltpu.roll(window, start & 7, 0)
+        pltpu.store(rows_ref.at[pl.ds(aligned, 8)], window[:8], mask=line >= (start & 7))
+        rows_ref[pl.ds(aligned + 8, capacity), :] = window[8:]
+        while done + chunk <= width - capacity * (holders - 1 - holder):
+            left[:, done:done + chunk] = lax.dot_general(
+                pick,
+                rows_ref[pl.ds(done, chunk), :].astype(BF16),
+                NT,
+                preferred_element_type=F32,
+            ).astype(BF16)
+            done += chunk
     left_kept[...] = left[:half, :]
     cut_product(group, left[half:, :], (amps0, amps1, amps2, amps3), given)
 

time: 83.4 us -> 83.4 us (level)
  no operation moved by 1% of the time
where the time goes in v8:
time: 83.4 us; the launch traced here: 83 us
  starting transfers between devices  29.7 us (36%)
  waiting for transfers between devices  20.3 us (24%)
  blocking collectives  20.3 us (24%)
  Pallas kernels  11.5 us (14%)
    all_to_all x1, blocking collectives, body(): lax.all_to_all(both, 'cd', 0, 0, tiled=True, axis_index_groups=same_core)  20.3 us
    all_to_all x1, starting transfers between devices, body(): lax.all_to_all(outgoing, 'cd', split_axis=0, concat_axis=0, tiled=True)  17.9 us
    all_to_all x1, waiting for transfers between devices, body(): lax.all_to_all(outgoing, 'cd', split_axis=0, concat_axis=0, tiled=True)  12.3 us
    ppermute x3, starting transfers between devices, from_group(): lax.ppermute(value, 'ij', [((i + step) % groups, i) for i in range(groups)])  9.87 us
    ppermute x3, waiting for transfers between devices, from_group(): lax.ppermute(value, 'ij', [((i + step) % groups, i) for i in range(groups)])  6.58 us
    pallas_call x1, Pallas kernels, order(): pl.pallas_call(lambda *refs: order_kernel(capacity, width, *refs), out_sh...  3.57 us
    pallas_call x1, Pallas kernels, pack(): pl.pallas_call(lambda *refs: pack_kernel(width, *refs), out_shape=jax.Sha...  3.04 us
    pallas_call x2, Pallas kernels, arrange(): pl.pallas_call(arrange_kernel, out_shape=[jax.ShapeDtypeStruct(block.shap...  2.5 us
  transfers between devices with their start and end apart: 5, of which 4 were waited for; matrix products, arithmetic and copies ran while one was open for 0% of the time, Pallas kernels for 12%

profile of v8, /device:TPU:2, one launch (start us, length us, event | category | flops | bytes accessed | tf_op | source)
XLA Modules:
  0.0 83.0 jit_solution(5381185590971866098)
XLA Ops:
  0.0 4.0 %collective-permute-start = (bf16[1024,256]{1,0:T(8,128)(2,1)}, bf16[1024,256]{1,0:T(8,128)(2,1)S(1)}, u32[]{:S(2)}, u32[]{:S(2)}) collective-permute-start(bf16[1024,256]{1,0:T(8,128)(2,1)} %refs_0_.5), channel_id=1, source_target_pairs={{256,0},{384,128},{0,256},{128,384},{257,1},{385,129},{1,257},{129... | collective-permute-start | bytes 1572872 | tf_op jit(solution)/shard_map/ppermute | solution.py:304
  4.0 3.0 %pack.1 = bf16[128,16,256]{2,1,0:T(8,128)(2,1)} custom-call(s32[128,2048]{1,0:T(8,128)} %refs_0_.4, bf16[256,2048]{1,0:T(8,128)(2,1)} %refs_1_.1), custom_call_target="tpu_custom_call" | custom-call | tf_op jit(solution)/shard_map/pack/pallas_call | solution.py:192
  7.1 0.0 copy-start
  7.1 17.9 %all-to-all-start = ((bf16[128,16,256]{2,1,0:T(8,128)(2,1)}), bf16[128,16,256]{2,1,0:T(8,128)(2,1)S(1)}, u32[]{:S(2)}, u32[]{:S(2)}) async-start(bf16[128,16,256]{2,1,0:T(8,128)(2,1)} %pack.1), calls=%async_computation | async-start | bytes 2097152 | tf_op jit(solution)/shard_map/all_to_all | solution.py:302
  25.1 0.0 collective-permute-done.refs_1_
  25.1 0.0 copy-done
  25.1 1.9 %collective-permute-start.2 = (bf16[1024,256]{1,0:T(8,128)(2,1)S(1)}, bf16[1024,256]{1,0:T(8,128)(2,1)S(1)}, u32[]{:S(2)}, u32[]{:S(2)}) collective-permute-start(bf16[1024,256]{1,0:T(8,128)(2,1)S(1)} %copy-done), channel_id=1, source_target_pairs={{384,0},{0,128},{128,256},{256,384},{385,1},{1,129},{129,257},{257... | collective-permute-start | bytes 1572872 | tf_op jit(solution)/shard_map/ppermute | solution.py:304
  27.0 3.9 %collective-permute-start.1 = (bf16[1024,256]{1,0:T(8,128)(2,1)S(1)}, bf16[1024,256]{1,0:T(8,128)(2,1)S(1)}, u32[]{:S(2)}, u32[]{:S(2)}) collective-permute-start(bf16[1024,256]{1,0:T(8,128)(2,1)S(1)} %copy-done), channel_id=1, source_target_pairs={{128,0},{256,128},{384,256},{0,384},{129,1},{257,129},{385,257},{1... | collective-permute-start | bytes 1572872 | tf_op jit(solution)/shard_map/ppermute | solution.py:304
  30.9 3.6 %order.1 = (s32[8,1024]{1,0:T(8,128)S(1)}, s32[8,128]{1,0:T(8,128)S(1)}) custom-call(s32[128,2048]{1,0:T(8,128)} %refs_0_.4), custom_call_target="tpu_custom_call" | custom-call | flops 15000000512 | bytes 1000000 | tf_op jit(solution)/shard_map/order/pallas_call | solution.py:213
  34.5 1.3 %arrange.2 = (bf16[1024,256]{1,0:T(8,128)(2,1)S(1)}, bf16[1024,256]{1,0:T(8,128)(2,1)S(1)}) custom-call(s32[8,1024]{1,0:T(8,128)S(1)} %get-tuple-element.16.place, bf16[1024,256]{1,0:T(8,128)(2,1)S(1)} %copy-done, bf16[1024,256]{1,0:T(8,128)(2,1)S(1)} %collective-permute-done.refs_1_), custom_call_target="tpu_custom_call" | custom-call | flops 2000000000 | bytes 2000000 | tf_op jit(solution)/shard_map/arrange/pallas_call | solution.py:234
  35.8 4.6 %collective-permute-done.2.refs_1_ = bf16[1024,256]{1,0:T(8,128)(2,1)S(1)} collective-permute-done((bf16[1024,256]{1,0:T(8,128)(2,1)S(1)}, bf16[1024,256]{1,0:T(8,128)(2,1)S(1)}, u32[]{:S(2)}, u32[]{:S(2)}) %collective-permute-start.2) | collective-permute-done | bytes 524320 | tf_op jit(solution)/shard_map/ppermute | solution.py:304
  40.4 1.9 %collective-permute-done.1.refs_0_ = bf16[1024,256]{1,0:T(8,128)(2,1)S(1)} collective-permute-done((bf16[1024,256]{1,0:T(8,128)(2,1)S(1)}, bf16[1024,256]{1,0:T(8,128)(2,1)S(1)}, u32[]{:S(2)}, u32[]{:S(2)}) %collective-permute-start.1) | collective-permute-done | bytes 524320 | tf_op jit(solution)/shard_map/ppermute | solution.py:304
  42.3 1.2 %arrange.3 = (bf16[1024,256]{1,0:T(8,128)(2,1)S(1)}, bf16[1024,256]{1,0:T(8,128)(2,1)S(1)}) custom-call(s32[8,1024]{1,0:T(8,128)S(1)} %get-tuple-element.16.place, bf16[1024,256]{1,0:T(8,128)(2,1)S(1)} %collective-permute-done.1.refs_0_, bf16[1024,256]{1,0:T(8,128)(2,1)S(1)} %collective-permute-done.2.refs_1_), custom_call_target="tpu_custom_call" | custom-call | flops 2000000000 | bytes 2000000 | tf_op jit(solution)/shard_map/arrange/pallas_call | solution.py:234
  43.6 12.3 %all-to-all-done.received = bf16[128,16,256]{2,1,0:T(8,128)(2,1)S(1)} async-done(((bf16[128,16,256]{2,1,0:T(8,128)(2,1)}), bf16[128,16,256]{2,1,0:T(8,128)(2,1)S(1)}, u32[]{:S(2)}, u32[]{:S(2)}) %all-to-all-start) | async-done | bytes 1048608 | tf_op jit(solution)/shard_map/all_to_all | solution.py:302
  55.9 1.8 %multiply.1 = (f32[1024,128]{1,0:T(8,128)S(1)}, bf16[128,1024]{1,0:T(8,128)(2,1)S(1)}) custom-call(s32[8,128]{1,0:T(8,128)S(1)} %get-tuple-element.15.offsets, bf16[128,16,256]{2,1,0:T(8,128)(2,1)S(1)} %all-to-all-done.received, bf16[1024,256]{1,0:T(8,128)(2,1)S(1)} %get-tuple-element.18.amps0, bf16[1024,256]{1,0:T(8,128)(2,1)S(1)} %get-tuple-element.20.amps1, ...), custom_call_target="tpu_custom_call" | custom-call | tf_op jit(solution)/shard_map/multiply/pallas_call | solution.py:250
  57.8 1.9 %collective-permute-start.3 = (f32[1024,128]{1,0:T(8,128)S(1)}, f32[1024,128]{1,0:T(8,128)S(1)}, u32[]{:S(2)}, u32[]{:S(2)}) collective-permute-start(f32[1024,128]{1,0:T(8,128)S(1)} %get-tuple-element.24), channel_id=1, source_target_pairs={{0,1},{1,0},{2,3},{3,2},{4,5},{5,4},{6,7},{7,6},{8,9},{9,8},{10,11... | collective-permute-start | bytes 1572872 | tf_op jit(solution)/shard_map/ppermute | solution.py:314
  59.7 0.5 keep.1
  60.2 1.4 %collective-permute-done.3 = f32[1024,128]{1,0:T(8,128)S(1)} collective-permute-done((f32[1024,128]{1,0:T(8,128)S(1)}, f32[1024,128]{1,0:T(8,128)S(1)}, u32[]{:S(2)}, u32[]{:S(2)}) %collective-permute-start.3) | collective-permute-done | bytes 524320 | tf_op jit(solution)/shard_map/ppermute | solution.py:314
  61.6 0.3 multiply_convert_fusion
  61.9 20.3 %all_to_all.10 = f16[64,16,128]{2,1,0:T(8,128)(2,1)S(1)} all-to-all(f16[64,16,128]{2,1,0:T(8,128)(2,1)S(1)} %bitcast.1), channel_id=1, replica_groups={{0,2,4,6,8,10,12,14,16,18,20,22,24,26,28,30,32,34,36,38,40,42,44,46,48,..., dimensions={0} | all-to-all | bytes 524288 | tf_op jit(solution)/shard_map/all_to_all | solution.py:317
  82.3 0.1 fusion.1
  82.4 0.6 convert_element_type.16
Async XLA Ops:
  0.0 25.1 %collective-permute-start = (bf16[1024,256]{1,0:T(8,128)(2,1)}, bf16[1024,256]{1,0:T(8,128)(2,1)S(1)}, u32[]{:S(2)}, u32[]{:S(2)}) collective-permute-start(bf16[1024,256]{1,0:T(8,128)(2,1)} %refs_0_.5), channel_id=1, source_target_pairs={{256,0},{384,128},{0,256},{128,384},{257,1},{385,129},{1,257},{129... | collective-permute-start | bytes 1572872 | tf_op jit(solution)/shard_map/ppermute | solution.py:304
  7.1 18.0 %copy-start = (bf16[1024,256]{1,0:T(8,128)(2,1)S(1)}, bf16[1024,256]{1,0:T(8,128)(2,1)}, u32[]{:S(2)}) copy-start(bf16[1024,256]{1,0:T(8,128)(2,1)} %refs_0_.5) | copy-start | bytes 1572868
  7.1 48.8 %all-to-all-start = ((bf16[128,16,256]{2,1,0:T(8,128)(2,1)}), bf16[128,16,256]{2,1,0:T(8,128)(2,1)S(1)}, u32[]{:S(2)}, u32[]{:S(2)}) async-start(bf16[128,16,256]{2,1,0:T(8,128)(2,1)} %pack.1), calls=%async_computation | async-start | bytes 2097152 | tf_op jit(solution)/shard_map/all_to_all | solution.py:302
  25.1 15.3 %collective-permute-start.2 = (bf16[1024,256]{1,0:T(8,128)(2,1)S(1)}, bf16[1024,256]{1,0:T(8,128)(2,1)S(1)}, u32[]{:S(2)}, u32[]{:S(2)}) collective-permute-start(bf16[1024,256]{1,0:T(8,128)(2,1)S(1)} %copy-done), channel_id=1, source_target_pairs={{384,0},{0,128},{128,256},{256,384},{385,1},{1,129},{129,257},{257... | collective-permute-start | bytes 1572872 | tf_op jit(solution)/shard_map/ppermute | solution.py:304
  27.0 15.3 %collective-permute-start.1 = (bf16[1024,256]{1,0:T(8,128)(2,1)S(1)}, bf16[1024,256]{1,0:T(8,128)(2,1)S(1)}, u32[]{:S(2)}, u32[]{:S(2)}) collective-permute-start(bf16[1024,256]{1,0:T(8,128)(2,1)S(1)} %copy-done), channel_id=1, source_target_pairs={{128,0},{256,128},{384,256},{0,384},{129,1},{257,129},{385,257},{1... | collective-permute-start | bytes 1572872 | tf_op jit(solution)/shard_map/ppermute | solution.py:304
  57.8 3.8 %collective-permute-start.3 = (f32[1024,128]{1,0:T(8,128)S(1)}, f32[1024,128]{1,0:T(8,128)S(1)}, u32[]{:S(2)}, u32[]{:S(2)}) collective-permute-start(f32[1024,128]{1,0:T(8,128)S(1)} %get-tuple-element.24), channel_id=1, source_target_pairs={{0,1},{1,0},{2,3},{3,2},{4,5},{5,4},{6,7},{7,6},{8,9},{9,8},{10,11... | collective-permute-start | bytes 1572872 | tf_op jit(solution)/shard_map/ppermute | solution.py:314

commit v9 on v8

--- a/solution.py
+++ b/solution.py
@@ -26,8 +26,12 @@
     eight = pl.multiple_of((device >> 3) << 3, 8)
     own_copy = pltpu.make_async_copy(owned.at[pl.ds(eight, 8)], group, sems.at[0])
     own_copy.start()
-    ints_copy = pltpu.make_async_copy(ints, staged, sems.at[1])
-    ints_copy.start()
+    quarter = total // 4
+    ints_copies = []
+    for part in range(4):
+        at = pl.ds(part * quarter, quarter)
+        ints_copies.append(pltpu.make_async_copy(ints.at[:, at], staged.at[:, at], sems.at[11 + part]))
+        ints_copies[-1].start()
     slots[pl.ds(total, capacity + 8), :] = jnp.zeros((capacity + 8, slots.shape[1]), F32)
     rows = lax.broadcasted_iota(jnp.int32, (chunk, chunk), 0)
     cols = lax.broadcasted_iota(jnp.int32, (chunk, chunk), 1)
@@ -49,12 +53,13 @@
     firsts[...] = jnp.broadcast_to(first, firsts.shape)
     starts_copy = pltpu.make_async_copy(firsts, starts, sems.at[2])
     starts_copy.start()
-    ints_copy.wait()
     for step in range(total // chunk):
+        if step * chunk % quarter == 0:
+            ints_copies[step * chunk // quarter].wait()
         at = pl.ds(step * chunk, chunk)
         slots[at, :] = lax.dot_general(eye, staged[:, at], NT, preferred_element_type=F32)
     starts_copy.wait()
-    pieces = sems.shape[0] - 3
+    pieces = 8
     each = devices // pieces
     copies = []
     for piece in range(pieces):
@@ -201,7 +206,7 @@
             pltpu.VMEM((8, 128), jnp.int32),
             pltpu.SMEM((8, 128), jnp.int32),
             pltpu.VMEM((devices, capacity, pairs), BF16),
-            pltpu.SemaphoreType.DMA((11,)),
+            pltpu.SemaphoreType.DMA((15,)),
         ],
         compiler_params=pltpu.CompilerParams(vmem_limit_bytes=VMEM_LIMIT),
         name="pack",
@@ -311,8 +316,8 @@
     amps1, amps3 = arrange(place, amps1, amps3)
     given, left = multiply(offsets, incoming, amps0, amps1, amps2, amps3)
     kept = keep(left, amps0, amps1, amps2, amps3)
-    taken = lax.ppermute(given, "cd", [(i, i ^ 1) for i in range(devices_cd)])
-    both = squeeze(kept + taken).reshape(devices_cd // 2, 16, 128)
+    taken = lax.ppermute(squeeze(given), "cd", [(i, i ^ 1) for i in range(devices_cd)])
+    both = squeeze(kept + unsqueeze(taken)).reshape(devices_cd // 2, 16, 128)
     same_core = [[2 * k + c for k in range(devices_cd // 2)] for c in range(2)]
     shares = lax.all_to_all(both, "cd", 0, 0, tiled=True, axis_index_groups=same_core)
     summed = jnp.sum(unsqueeze(shares), axis=0)

time: 83.4 us -> 83.8 us (level)
  no operation moved by 1% of the time
where the time goes in v9:
time: 83.8 us; the launch traced here: 83.5 us
  starting transfers between devices  29.7 us (35%)
  blocking collectives  20.3 us (24%)
  waiting for transfers between devices  19.9 us (24%)
  Pallas kernels  11.9 us (14%)
  other arithmetic  0.84 us (1%)
    all_to_all x1, blocking collectives, body(): lax.all_to_all(both, 'cd', 0, 0, tiled=True, axis_index_groups=same_core)  20.3 us
    all_to_all x1, starting transfers between devices, body(): lax.all_to_all(outgoing, 'cd', split_axis=0, concat_axis=0, tiled=True)  18 us
    all_to_all x1, waiting for transfers between devices, body(): lax.all_to_all(outgoing, 'cd', split_axis=0, concat_axis=0, tiled=True)  12.3 us
    ppermute x3, starting transfers between devices, from_group(): lax.ppermute(value, 'ij', [((i + step) % groups, i) for i in range(groups)])  9.87 us
    ppermute x3, waiting for transfers between devices, from_group(): lax.ppermute(value, 'ij', [((i + step) % groups, i) for i in range(groups)])  6.58 us
    pallas_call x1, Pallas kernels, order(): pl.pallas_call(lambda *refs: order_kernel(capacity, width, *refs), out_sh...  3.57 us
    pallas_call x1, Pallas kernels, pack(): pl.pallas_call(lambda *refs: pack_kernel(width, *refs), out_shape=jax.Sha...  3.51 us
    pallas_call x2, Pallas kernels, arrange(): pl.pallas_call(arrange_kernel, out_shape=[jax.ShapeDtypeStruct(block.shap...  2.5 us
  transfers between devices with their start and end apart: 5, of which 4 were waited for; matrix products, arithmetic and copies ran while one was open for 0% of the time, Pallas kernels for 12%

profile of v9, /device:TPU:2, one launch (start us, length us, event | category | flops | bytes accessed | tf_op | source)
XLA Modules:
  0.0 83.5 jit_solution(6683687523188388355)
XLA Ops:
  0.0 4.0 %collective-permute-start = (bf16[1024,256]{1,0:T(8,128)(2,1)}, bf16[1024,256]{1,0:T(8,128)(2,1)S(1)}, u32[]{:S(2)}, u32[]{:S(2)}) collective-permute-start(bf16[1024,256]{1,0:T(8,128)(2,1)} %refs_0_.5), channel_id=1, source_target_pairs={{256,0},{384,128},{0,256},{128,384},{257,1},{385,129},{1,257},{129... | collective-permute-start | bytes 1572872 | tf_op jit(solution)/shard_map/ppermute | solution.py:309
  4.0 3.5 %pack.1 = bf16[128,16,256]{2,1,0:T(8,128)(2,1)} custom-call(s32[128,2048]{1,0:T(8,128)} %refs_0_.4, bf16[256,2048]{1,0:T(8,128)(2,1)} %refs_1_.1), custom_call_target="tpu_custom_call" | custom-call | tf_op jit(solution)/shard_map/pack/pallas_call | solution.py:197
  7.5 0.0 copy-start
  7.6 18.0 %all-to-all-start = ((bf16[128,16,256]{2,1,0:T(8,128)(2,1)}), bf16[128,16,256]{2,1,0:T(8,128)(2,1)S(1)}, u32[]{:S(2)}, u32[]{:S(2)}) async-start(bf16[128,16,256]{2,1,0:T(8,128)(2,1)} %pack.1), calls=%async_computation | async-start | bytes 2097152 | tf_op jit(solution)/shard_map/all_to_all | solution.py:307
  25.5 0.0 collective-permute-done.refs_1_
  25.5 0.0 copy-done
  25.5 1.9 %collective-permute-start.2 = (bf16[1024,256]{1,0:T(8,128)(2,1)S(1)}, bf16[1024,256]{1,0:T(8,128)(2,1)S(1)}, u32[]{:S(2)}, u32[]{:S(2)}) collective-permute-start(bf16[1024,256]{1,0:T(8,128)(2,1)S(1)} %copy-done), channel_id=1, source_target_pairs={{384,0},{0,128},{128,256},{256,384},{385,1},{1,129},{129,257},{257... | collective-permute-start | bytes 1572872 | tf_op jit(solution)/shard_map/ppermute | solution.py:309
  27.5 3.9 %collective-permute-start.1 = (bf16[1024,256]{1,0:T(8,128)(2,1)S(1)}, bf16[1024,256]{1,0:T(8,128)(2,1)S(1)}, u32[]{:S(2)}, u32[]{:S(2)}) collective-permute-start(bf16[1024,256]{1,0:T(8,128)(2,1)S(1)} %copy-done), channel_id=1, source_target_pairs={{128,0},{256,128},{384,256},{0,384},{129,1},{257,129},{385,257},{1... | collective-permute-start | bytes 1572872 | tf_op jit(solution)/shard_map/ppermute | solution.py:309
  31.4 3.6 %order.1 = (s32[8,1024]{1,0:T(8,128)S(1)}, s32[8,128]{1,0:T(8,128)S(1)}) custom-call(s32[128,2048]{1,0:T(8,128)} %refs_0_.4), custom_call_target="tpu_custom_call" | custom-call | flops 15000000512 | bytes 1000000 | tf_op jit(solution)/shard_map/order/pallas_call | solution.py:218
  35.0 1.3 %arrange.2 = (bf16[1024,256]{1,0:T(8,128)(2,1)S(1)}, bf16[1024,256]{1,0:T(8,128)(2,1)S(1)}) custom-call(s32[8,1024]{1,0:T(8,128)S(1)} %get-tuple-element.16.place, bf16[1024,256]{1,0:T(8,128)(2,1)S(1)} %copy-done, bf16[1024,256]{1,0:T(8,128)(2,1)S(1)} %collective-permute-done.refs_1_), custom_call_target="tpu_custom_call" | custom-call | flops 2000000000 | bytes 2000000 | tf_op jit(solution)/shard_map/arrange/pallas_call | solution.py:239
  36.2 4.6 %collective-permute-done.2.refs_1_ = bf16[1024,256]{1,0:T(8,128)(2,1)S(1)} collective-permute-done((bf16[1024,256]{1,0:T(8,128)(2,1)S(1)}, bf16[1024,256]{1,0:T(8,128)(2,1)S(1)}, u32[]{:S(2)}, u32[]{:S(2)}) %collective-permute-start.2) | collective-permute-done | bytes 524320 | tf_op jit(solution)/shard_map/ppermute | solution.py:309
  40.9 1.9 %collective-permute-done.1.refs_0_ = bf16[1024,256]{1,0:T(8,128)(2,1)S(1)} collective-permute-done((bf16[1024,256]{1,0:T(8,128)(2,1)S(1)}, bf16[1024,256]{1,0:T(8,128)(2,1)S(1)}, u32[]{:S(2)}, u32[]{:S(2)}) %collective-permute-start.1) | collective-permute-done | bytes 524320 | tf_op jit(solution)/shard_map/ppermute | solution.py:309
  42.8 1.2 %arrange.3 = (bf16[1024,256]{1,0:T(8,128)(2,1)S(1)}, bf16[1024,256]{1,0:T(8,128)(2,1)S(1)}) custom-call(s32[8,1024]{1,0:T(8,128)S(1)} %get-tuple-element.16.place, bf16[1024,256]{1,0:T(8,128)(2,1)S(1)} %collective-permute-done.1.refs_0_, bf16[1024,256]{1,0:T(8,128)(2,1)S(1)} %collective-permute-done.2.refs_1_), custom_call_target="tpu_custom_call" | custom-call | flops 2000000000 | bytes 2000000 | tf_op jit(solution)/shard_map/arrange/pallas_call | solution.py:239
  44.1 12.3 %all-to-all-done.received = bf16[128,16,256]{2,1,0:T(8,128)(2,1)S(1)} async-done(((bf16[128,16,256]{2,1,0:T(8,128)(2,1)}), bf16[128,16,256]{2,1,0:T(8,128)(2,1)S(1)}, u32[]{:S(2)}, u32[]{:S(2)}) %all-to-all-start) | async-done | bytes 1048608 | tf_op jit(solution)/shard_map/all_to_all | solution.py:307
  56.4 1.8 %multiply.1 = (f32[1024,128]{1,0:T(8,128)S(1)}, bf16[128,1024]{1,0:T(8,128)(2,1)S(1)}) custom-call(s32[8,128]{1,0:T(8,128)S(1)} %get-tuple-element.15.offsets, bf16[128,16,256]{2,1,0:T(8,128)(2,1)S(1)} %all-to-all-done.received, bf16[1024,256]{1,0:T(8,128)(2,1)S(1)} %get-tuple-element.18.amps0, bf16[1024,256]{1,0:T(8,128)(2,1)S(1)} %get-tuple-element.20.amps1, ...), custom_call_target="tpu_custom_call" | custom-call | tf_op jit(solution)/shard_map/multiply/pallas_call | solution.py:255
  58.3 0.3 multiply_convert_fusion.1
  58.6 1.9 %collective-permute-start.3 = (f16[1024,128]{1,0:T(8,128)(2,1)S(1)}, f16[1024,128]{1,0:T(8,128)(2,1)S(1)}, u32[]{:S(2)}, u32[]{:S(2)}) collective-permute-start(f16[1024,128]{1,0:T(8,128)(2,1)S(1)} %multiply_convert_fusion.1), channel_id=1, source_target_pairs={{0,1},{1,0},{2,3},{3,2},{4,5},{5,4},{6,7},{7,6},{8,9},{9,8},{10,11... | collective-permute-start | bytes 786440 | tf_op jit(solution)/shard_map/ppermute | solution.py:319
  60.5 0.5 keep.1
  61.0 1.0 %collective-permute-done.3 = f16[1024,128]{1,0:T(8,128)(2,1)S(1)} collective-permute-done((f16[1024,128]{1,0:T(8,128)(2,1)S(1)}, f16[1024,128]{1,0:T(8,128)(2,1)S(1)}, u32[]{:S(2)}, u32[]{:S(2)}) %collective-permute-start.3) | collective-permute-done | bytes 262176 | tf_op jit(solution)/shard_map/ppermute | solution.py:319
  62.0 0.4 multiply_convert_fusion
  62.4 20.3 %all_to_all.10 = f16[64,16,128]{2,1,0:T(8,128)(2,1)S(1)} all-to-all(f16[64,16,128]{2,1,0:T(8,128)(2,1)S(1)} %bitcast.1), channel_id=1, replica_groups={{0,2,4,6,8,10,12,14,16,18,20,22,24,26,28,30,32,34,36,38,40,42,44,46,48,..., dimensions={0} | all-to-all | bytes 524288 | tf_op jit(solution)/shard_map/all_to_all | solution.py:322
  82.8 0.1 fusion.3
  82.9 0.6 convert_element_type.24
Async XLA Ops:
  0.0 25.5 %collective-permute-start = (bf16[1024,256]{1,0:T(8,128)(2,1)}, bf16[1024,256]{1,0:T(8,128)(2,1)S(1)}, u32[]{:S(2)}, u32[]{:S(2)}) collective-permute-start(bf16[1024,256]{1,0:T(8,128)(2,1)} %refs_0_.5), channel_id=1, source_target_pairs={{256,0},{384,128},{0,256},{128,384},{257,1},{385,129},{1,257},{129... | collective-permute-start | bytes 1572872 | tf_op jit(solution)/shard_map/ppermute | solution.py:309
  7.5 18.0 %copy-start = (bf16[1024,256]{1,0:T(8,128)(2,1)S(1)}, bf16[1024,256]{1,0:T(8,128)(2,1)}, u32[]{:S(2)}) copy-start(bf16[1024,256]{1,0:T(8,128)(2,1)} %refs_0_.5) | copy-start | bytes 1572868
  7.6 48.8 %all-to-all-start = ((bf16[128,16,256]{2,1,0:T(8,128)(2,1)}), bf16[128,16,256]{2,1,0:T(8,128)(2,1)S(1)}, u32[]{:S(2)}, u32[]{:S(2)}) async-start(bf16[128,16,256]{2,1,0:T(8,128)(2,1)} %pack.1), calls=%async_computation | async-start | bytes 2097152 | tf_op jit(solution)/shard_map/all_to_all | solution.py:307
  25.5 15.3 %collective-permute-start.2 = (bf16[1024,256]{1,0:T(8,128)(2,1)S(1)}, bf16[1024,256]{1,0:T(8,128)(2,1)S(1)}, u32[]{:S(2)}, u32[]{:S(2)}) collective-permute-start(bf16[1024,256]{1,0:T(8,128)(2,1)S(1)} %copy-done), channel_id=1, source_target_pairs={{384,0},{0,128},{128,256},{256,384},{385,1},{1,129},{129,257},{257... | collective-permute-start | bytes 1572872 | tf_op jit(solution)/shard_map/ppermute | solution.py:309
  27.5 15.3 %collective-permute-start.1 = (bf16[1024,256]{1,0:T(8,128)(2,1)S(1)}, bf16[1024,256]{1,0:T(8,128)(2,1)S(1)}, u32[]{:S(2)}, u32[]{:S(2)}) collective-permute-start(bf16[1024,256]{1,0:T(8,128)(2,1)S(1)} %copy-done), channel_id=1, source_target_pairs={{128,0},{256,128},{384,256},{0,384},{129,1},{257,129},{385,257},{1... | collective-permute-start | bytes 1572872 | tf_op jit(solution)/shard_map/ppermute | solution.py:309
  58.6 3.4 %collective-permute-start.3 = (f16[1024,128]{1,0:T(8,128)(2,1)S(1)}, f16[1024,128]{1,0:T(8,128)(2,1)S(1)}, u32[]{:S(2)}, u32[]{:S(2)}) collective-permute-start(f16[1024,128]{1,0:T(8,128)(2,1)S(1)} %multiply_convert_fusion.1), channel_id=1, source_target_pairs={{0,1},{1,0},{2,3},{3,2},{4,5},{5,4},{6,7},{7,6},{8,9},{9,8},{10,11... | collective-permute-start | bytes 786440 | tf_op jit(solution)/shard_map/ppermute | solution.py:319

commit v10 on v8

--- a/solution.py
+++ b/solution.py
@@ -311,8 +311,8 @@
     amps1, amps3 = arrange(place, amps1, amps3)
     given, left = multiply(offsets, incoming, amps0, amps1, amps2, amps3)
     kept = keep(left, amps0, amps1, amps2, amps3)
-    taken = lax.ppermute(given, "cd", [(i, i ^ 1) for i in range(devices_cd)])
-    both = squeeze(kept + taken).reshape(devices_cd // 2, 16, 128)
+    taken = lax.ppermute(squeeze(given), "cd", [(i, i ^ 1) for i in range(devices_cd)])
+    both = squeeze(kept + unsqueeze(taken)).reshape(devices_cd // 2, 16, 128)
     same_core = [[2 * k + c for k in range(devices_cd // 2)] for c in range(2)]
     shares = lax.all_to_all(both, "cd", 0, 0, tiled=True, axis_index_groups=same_core)
     summed = jnp.sum(unsqueeze(shares), axis=0)

time: 83.4 us -> 83.4 us (level)
  no operation moved by 1% of the time
where the time goes in v10:
time: 83.4 us; the launch traced here: 83 us
  starting transfers between devices  29.7 us (36%)
  blocking collectives  20.3 us (24%)
  waiting for transfers between devices  19.9 us (24%)
  Pallas kernels  11.5 us (14%)
  other arithmetic  0.84 us (1%)
    all_to_all x1, blocking collectives, body(): lax.all_to_all(both, 'cd', 0, 0, tiled=True, axis_index_groups=same_core)  20.3 us
    all_to_all x1, starting transfers between devices, body(): lax.all_to_all(outgoing, 'cd', split_axis=0, concat_axis=0, tiled=True)  17.9 us
    all_to_all x1, waiting for transfers between devices, body(): lax.all_to_all(outgoing, 'cd', split_axis=0, concat_axis=0, tiled=True)  12.3 us
    ppermute x3, starting transfers between devices, from_group(): lax.ppermute(value, 'ij', [((i + step) % groups, i) for i in range(groups)])  9.87 us
    ppermute x3, waiting for transfers between devices, from_group(): lax.ppermute(value, 'ij', [((i + step) % groups, i) for i in range(groups)])  6.58 us
    pallas_call x1, Pallas kernels, order(): pl.pallas_call(lambda *refs: order_kernel(capacity, width, *refs), out_sh...  3.57 us
    pallas_call x1, Pallas kernels, pack(): pl.pallas_call(lambda *refs: pack_kernel(width, *refs), out_shape=jax.Sha...  3.04 us
    pallas_call x2, Pallas kernels, arrange(): pl.pallas_call(arrange_kernel, out_shape=[jax.ShapeDtypeStruct(block.shap...  2.5 us
  transfers between devices with their start and end apart: 5, of which 4 were waited for; matrix products, arithmetic and copies ran while one was open for 0% of the time, Pallas kernels for 12%

profile of v10, /device:TPU:2, one launch (start us, length us, event | category | flops | bytes accessed | tf_op | source)
XLA Modules:
  0.0 83.0 jit_solution(8651024945472516198)
XLA Ops:
  0.0 4.0 %collective-permute-start = (bf16[1024,256]{1,0:T(8,128)(2,1)}, bf16[1024,256]{1,0:T(8,128)(2,1)S(1)}, u32[]{:S(2)}, u32[]{:S(2)}) collective-permute-start(bf16[1024,256]{1,0:T(8,128)(2,1)} %refs_0_.5), channel_id=1, source_target_pairs={{256,0},{384,128},{0,256},{128,384},{257,1},{385,129},{1,257},{129... | collective-permute-start | bytes 1572872 | tf_op jit(solution)/shard_map/ppermute | solution.py:304
  4.0 3.0 %pack.1 = bf16[128,16,256]{2,1,0:T(8,128)(2,1)} custom-call(s32[128,2048]{1,0:T(8,128)} %refs_0_.4, bf16[256,2048]{1,0:T(8,128)(2,1)} %refs_1_.1), custom_call_target="tpu_custom_call" | custom-call | tf_op jit(solution)/shard_map/pack/pallas_call | solution.py:192
  7.1 0.0 copy-start
  7.1 17.9 %all-to-all-start = ((bf16[128,16,256]{2,1,0:T(8,128)(2,1)}), bf16[128,16,256]{2,1,0:T(8,128)(2,1)S(1)}, u32[]{:S(2)}, u32[]{:S(2)}) async-start(bf16[128,16,256]{2,1,0:T(8,128)(2,1)} %pack.1), calls=%async_computation | async-start | bytes 2097152 | tf_op jit(solution)/shard_map/all_to_all | solution.py:302
  25.1 0.0 collective-permute-done.refs_1_
  25.1 0.0 copy-done
  25.1 1.9 %collective-permute-start.2 = (bf16[1024,256]{1,0:T(8,128)(2,1)S(1)}, bf16[1024,256]{1,0:T(8,128)(2,1)S(1)}, u32[]{:S(2)}, u32[]{:S(2)}) collective-permute-start(bf16[1024,256]{1,0:T(8,128)(2,1)S(1)} %copy-done), channel_id=1, source_target_pairs={{384,0},{0,128},{128,256},{256,384},{385,1},{1,129},{129,257},{257... | collective-permute-start | bytes 1572872 | tf_op jit(solution)/shard_map/ppermute | solution.py:304
  27.0 3.9 %collective-permute-start.1 = (bf16[1024,256]{1,0:T(8,128)(2,1)S(1)}, bf16[1024,256]{1,0:T(8,128)(2,1)S(1)}, u32[]{:S(2)}, u32[]{:S(2)}) collective-permute-start(bf16[1024,256]{1,0:T(8,128)(2,1)S(1)} %copy-done), channel_id=1, source_target_pairs={{128,0},{256,128},{384,256},{0,384},{129,1},{257,129},{385,257},{1... | collective-permute-start | bytes 1572872 | tf_op jit(solution)/shard_map/ppermute | solution.py:304
  30.9 3.6 %order.1 = (s32[8,1024]{1,0:T(8,128)S(1)}, s32[8,128]{1,0:T(8,128)S(1)}) custom-call(s32[128,2048]{1,0:T(8,128)} %refs_0_.4), custom_call_target="tpu_custom_call" | custom-call | flops 15000000512 | bytes 1000000 | tf_op jit(solution)/shard_map/order/pallas_call | solution.py:213
  34.5 1.3 %arrange.2 = (bf16[1024,256]{1,0:T(8,128)(2,1)S(1)}, bf16[1024,256]{1,0:T(8,128)(2,1)S(1)}) custom-call(s32[8,1024]{1,0:T(8,128)S(1)} %get-tuple-element.16.place, bf16[1024,256]{1,0:T(8,128)(2,1)S(1)} %copy-done, bf16[1024,256]{1,0:T(8,128)(2,1)S(1)} %collective-permute-done.refs_1_), custom_call_target="tpu_custom_call" | custom-call | flops 2000000000 | bytes 2000000 | tf_op jit(solution)/shard_map/arrange/pallas_call | solution.py:234
  35.8 4.6 %collective-permute-done.2.refs_1_ = bf16[1024,256]{1,0:T(8,128)(2,1)S(1)} collective-permute-done((bf16[1024,256]{1,0:T(8,128)(2,1)S(1)}, bf16[1024,256]{1,0:T(8,128)(2,1)S(1)}, u32[]{:S(2)}, u32[]{:S(2)}) %collective-permute-start.2) | collective-permute-done | bytes 524320 | tf_op jit(solution)/shard_map/ppermute | solution.py:304
  40.4 1.9 %collective-permute-done.1.refs_0_ = bf16[1024,256]{1,0:T(8,128)(2,1)S(1)} collective-permute-done((bf16[1024,256]{1,0:T(8,128)(2,1)S(1)}, bf16[1024,256]{1,0:T(8,128)(2,1)S(1)}, u32[]{:S(2)}, u32[]{:S(2)}) %collective-permute-start.1) | collective-permute-done | bytes 524320 | tf_op jit(solution)/shard_map/ppermute | solution.py:304
  42.3 1.2 %arrange.3 = (bf16[1024,256]{1,0:T(8,128)(2,1)S(1)}, bf16[1024,256]{1,0:T(8,128)(2,1)S(1)}) custom-call(s32[8,1024]{1,0:T(8,128)S(1)} %get-tuple-element.16.place, bf16[1024,256]{1,0:T(8,128)(2,1)S(1)} %collective-permute-done.1.refs_0_, bf16[1024,256]{1,0:T(8,128)(2,1)S(1)} %collective-permute-done.2.refs_1_), custom_call_target="tpu_custom_call" | custom-call | flops 2000000000 | bytes 2000000 | tf_op jit(solution)/shard_map/arrange/pallas_call | solution.py:234
  43.6 12.3 %all-to-all-done.received = bf16[128,16,256]{2,1,0:T(8,128)(2,1)S(1)} async-done(((bf16[128,16,256]{2,1,0:T(8,128)(2,1)}), bf16[128,16,256]{2,1,0:T(8,128)(2,1)S(1)}, u32[]{:S(2)}, u32[]{:S(2)}) %all-to-all-start) | async-done | bytes 1048608 | tf_op jit(solution)/shard_map/all_to_all | solution.py:302
  55.9 1.8 %multiply.1 = (f32[1024,128]{1,0:T(8,128)S(1)}, bf16[128,1024]{1,0:T(8,128)(2,1)S(1)}) custom-call(s32[8,128]{1,0:T(8,128)S(1)} %get-tuple-element.15.offsets, bf16[128,16,256]{2,1,0:T(8,128)(2,1)S(1)} %all-to-all-done.received, bf16[1024,256]{1,0:T(8,128)(2,1)S(1)} %get-tuple-element.18.amps0, bf16[1024,256]{1,0:T(8,128)(2,1)S(1)} %get-tuple-element.20.amps1, ...), custom_call_target="tpu_custom_call" | custom-call | tf_op jit(solution)/shard_map/multiply/pallas_call | solution.py:250
  57.8 0.3 multiply_convert_fusion.1
  58.1 1.9 %collective-permute-start.3 = (f16[1024,128]{1,0:T(8,128)(2,1)S(1)}, f16[1024,128]{1,0:T(8,128)(2,1)S(1)}, u32[]{:S(2)}, u32[]{:S(2)}) collective-permute-start(f16[1024,128]{1,0:T(8,128)(2,1)S(1)} %multiply_convert_fusion.1), channel_id=1, source_target_pairs={{0,1},{1,0},{2,3},{3,2},{4,5},{5,4},{6,7},{7,6},{8,9},{9,8},{10,11... | collective-permute-start | bytes 786440 | tf_op jit(solution)/shard_map/ppermute | solution.py:314
  60.0 0.5 keep.1
  60.6 1.0 %collective-permute-done.3 = f16[1024,128]{1,0:T(8,128)(2,1)S(1)} collective-permute-done((f16[1024,128]{1,0:T(8,128)(2,1)S(1)}, f16[1024,128]{1,0:T(8,128)(2,1)S(1)}, u32[]{:S(2)}, u32[]{:S(2)}) %collective-permute-start.3) | collective-permute-done | bytes 262176 | tf_op jit(solution)/shard_map/ppermute | solution.py:314
  61.5 0.4 multiply_convert_fusion
  62.0 20.3 %all_to_all.10 = f16[64,16,128]{2,1,0:T(8,128)(2,1)S(1)} all-to-all(f16[64,16,128]{2,1,0:T(8,128)(2,1)S(1)} %bitcast.1), channel_id=1, replica_groups={{0,2,4,6,8,10,12,14,16,18,20,22,24,26,28,30,32,34,36,38,40,42,44,46,48,..., dimensions={0} | all-to-all | bytes 524288 | tf_op jit(solution)/shard_map/all_to_all | solution.py:317
  82.3 0.1 fusion.3
  82.4 0.6 convert_element_type.24
Async XLA Ops:
  0.0 25.1 %collective-permute-start = (bf16[1024,256]{1,0:T(8,128)(2,1)}, bf16[1024,256]{1,0:T(8,128)(2,1)S(1)}, u32[]{:S(2)}, u32[]{:S(2)}) collective-permute-start(bf16[1024,256]{1,0:T(8,128)(2,1)} %refs_0_.5), channel_id=1, source_target_pairs={{256,0},{384,128},{0,256},{128,384},{257,1},{385,129},{1,257},{129... | collective-permute-start | bytes 1572872 | tf_op jit(solution)/shard_map/ppermute | solution.py:304
  7.1 18.0 %copy-start = (bf16[1024,256]{1,0:T(8,128)(2,1)S(1)}, bf16[1024,256]{1,0:T(8,128)(2,1)}, u32[]{:S(2)}) copy-start(bf16[1024,256]{1,0:T(8,128)(2,1)} %refs_0_.5) | copy-start | bytes 1572868
  7.1 48.8 %all-to-all-start = ((bf16[128,16,256]{2,1,0:T(8,128)(2,1)}), bf16[128,16,256]{2,1,0:T(8,128)(2,1)S(1)}, u32[]{:S(2)}, u32[]{:S(2)}) async-start(bf16[128,16,256]{2,1,0:T(8,128)(2,1)} %pack.1), calls=%async_computation | async-start | bytes 2097152 | tf_op jit(solution)/shard_map/all_to_all | solution.py:302
  25.1 15.3 %collective-permute-start.2 = (bf16[1024,256]{1,0:T(8,128)(2,1)S(1)}, bf16[1024,256]{1,0:T(8,128)(2,1)S(1)}, u32[]{:S(2)}, u32[]{:S(2)}) collective-permute-start(bf16[1024,256]{1,0:T(8,128)(2,1)S(1)} %copy-done), channel_id=1, source_target_pairs={{384,0},{0,128},{128,256},{256,384},{385,1},{1,129},{129,257},{257... | collective-permute-start | bytes 1572872 | tf_op jit(solution)/shard_map/ppermute | solution.py:304
  27.0 15.3 %collective-permute-start.1 = (bf16[1024,256]{1,0:T(8,128)(2,1)S(1)}, bf16[1024,256]{1,0:T(8,128)(2,1)S(1)}, u32[]{:S(2)}, u32[]{:S(2)}) collective-permute-start(bf16[1024,256]{1,0:T(8,128)(2,1)S(1)} %copy-done), channel_id=1, source_target_pairs={{128,0},{256,128},{384,256},{0,384},{129,1},{257,129},{385,257},{1... | collective-permute-start | bytes 1572872 | tf_op jit(solution)/shard_map/ppermute | solution.py:304
  58.1 3.4 %collective-permute-start.3 = (f16[1024,128]{1,0:T(8,128)(2,1)S(1)}, f16[1024,128]{1,0:T(8,128)(2,1)S(1)}, u32[]{:S(2)}, u32[]{:S(2)}) collective-permute-start(f16[1024,128]{1,0:T(8,128)(2,1)S(1)} %multiply_convert_fusion.1), channel_id=1, source_target_pairs={{0,1},{1,0},{2,3},{3,2},{4,5},{5,4},{6,7},{7,6},{8,9},{9,8},{10,11... | collective-permute-start | bytes 786440 | tf_op jit(solution)/shard_map/ppermute | solution.py:314

commit v11 on v8

--- a/solution.py
+++ b/solution.py
@@ -201,7 +201,7 @@
             pltpu.VMEM((8, 128), jnp.int32),
             pltpu.SMEM((8, 128), jnp.int32),
             pltpu.VMEM((devices, capacity, pairs), BF16),
-            pltpu.SemaphoreType.DMA((11,)),
+            pltpu.SemaphoreType.DMA((19,)),
         ],
         compiler_params=pltpu.CompilerParams(vmem_limit_bytes=VMEM_LIMIT),
         name="pack",

time: 83.4 us -> 83.4 us (level)
  no operation moved by 1% of the time
where the time goes in v11:
time: 83.4 us; the launch traced here: 83 us
  starting transfers between devices  29.7 us (36%)
  waiting for transfers between devices  20.3 us (24%)
  blocking collectives  20.3 us (24%)
  Pallas kernels  11.5 us (14%)
    all_to_all x1, blocking collectives, body(): lax.all_to_all(both, 'cd', 0, 0, tiled=True, axis_index_groups=same_core)  20.3 us
    all_to_all x1, starting transfers between devices, body(): lax.all_to_all(outgoing, 'cd', split_axis=0, concat_axis=0, tiled=True)  17.9 us
    all_to_all x1, waiting for transfers between devices, body(): lax.all_to_all(outgoing, 'cd', split_axis=0, concat_axis=0, tiled=True)  12.3 us
    ppermute x3, starting transfers between devices, from_group(): lax.ppermute(value, 'ij', [((i + step) % groups, i) for i in range(groups)])  9.87 us
    ppermute x3, waiting for transfers between devices, from_group(): lax.ppermute(value, 'ij', [((i + step) % groups, i) for i in range(groups)])  6.58 us
    pallas_call x1, Pallas kernels, order(): pl.pallas_call(lambda *refs: order_kernel(capacity, width, *refs), out_sh...  3.57 us
    pallas_call x1, Pallas kernels, pack(): pl.pallas_call(lambda *refs: pack_kernel(width, *refs), out_shape=jax.Sha...  3.09 us
    pallas_call x2, Pallas kernels, arrange(): pl.pallas_call(arrange_kernel, out_shape=[jax.ShapeDtypeStruct(block.shap...  2.5 us
  transfers between devices with their start and end apart: 5, of which 4 were waited for; matrix products, arithmetic and copies ran while one was open for 0% of the time, Pallas kernels for 12%

profile of v11, /device:TPU:2, one launch (start us, length us, event | category | flops | bytes accessed | tf_op | source)
XLA Modules:
  0.0 83.0 jit_solution(11272129494030747130)
XLA Ops:
  0.0 4.0 %collective-permute-start = (bf16[1024,256]{1,0:T(8,128)(2,1)}, bf16[1024,256]{1,0:T(8,128)(2,1)S(1)}, u32[]{:S(2)}, u32[]{:S(2)}) collective-permute-start(bf16[1024,256]{1,0:T(8,128)(2,1)} %refs_0_.5), channel_id=1, source_target_pairs={{256,0},{384,128},{0,256},{128,384},{257,1},{385,129},{1,257},{129... | collective-permute-start | bytes 1572872 | tf_op jit(solution)/shard_map/ppermute | solution.py:304
  4.0 3.1 %pack.1 = bf16[128,16,256]{2,1,0:T(8,128)(2,1)} custom-call(s32[128,2048]{1,0:T(8,128)} %refs_0_.4, bf16[256,2048]{1,0:T(8,128)(2,1)} %refs_1_.1), custom_call_target="tpu_custom_call" | custom-call | tf_op jit(solution)/shard_map/pack/pallas_call | solution.py:192
  7.1 0.0 copy-start
  7.1 17.9 %all-to-all-start = ((bf16[128,16,256]{2,1,0:T(8,128)(2,1)}), bf16[128,16,256]{2,1,0:T(8,128)(2,1)S(1)}, u32[]{:S(2)}, u32[]{:S(2)}) async-start(bf16[128,16,256]{2,1,0:T(8,128)(2,1)} %pack.1), calls=%async_computation | async-start | bytes 2097152 | tf_op jit(solution)/shard_map/all_to_all | solution.py:302
  25.1 0.0 collective-permute-done.refs_1_
  25.1 0.0 copy-done
  25.1 1.9 %collective-permute-start.2 = (bf16[1024,256]{1,0:T(8,128)(2,1)S(1)}, bf16[1024,256]{1,0:T(8,128)(2,1)S(1)}, u32[]{:S(2)}, u32[]{:S(2)}) collective-permute-start(bf16[1024,256]{1,0:T(8,128)(2,1)S(1)} %copy-done), channel_id=1, source_target_pairs={{384,0},{0,128},{128,256},{256,384},{385,1},{1,129},{129,257},{257... | collective-permute-start | bytes 1572872 | tf_op jit(solution)/shard_map/ppermute | solution.py:304
  27.1 3.9 %collective-permute-start.1 = (bf16[1024,256]{1,0:T(8,128)(2,1)S(1)}, bf16[1024,256]{1,0:T(8,128)(2,1)S(1)}, u32[]{:S(2)}, u32[]{:S(2)}) collective-permute-start(bf16[1024,256]{1,0:T(8,128)(2,1)S(1)} %copy-done), channel_id=1, source_target_pairs={{128,0},{256,128},{384,256},{0,384},{129,1},{257,129},{385,257},{1... | collective-permute-start | bytes 1572872 | tf_op jit(solution)/shard_map/ppermute | solution.py:304
  31.0 3.6 %order.1 = (s32[8,1024]{1,0:T(8,128)S(1)}, s32[8,128]{1,0:T(8,128)S(1)}) custom-call(s32[128,2048]{1,0:T(8,128)} %refs_0_.4), custom_call_target="tpu_custom_call" | custom-call | flops 15000000512 | bytes 1000000 | tf_op jit(solution)/shard_map/order/pallas_call | solution.py:213
  34.6 1.3 %arrange.2 = (bf16[1024,256]{1,0:T(8,128)(2,1)S(1)}, bf16[1024,256]{1,0:T(8,128)(2,1)S(1)}) custom-call(s32[8,1024]{1,0:T(8,128)S(1)} %get-tuple-element.16.place, bf16[1024,256]{1,0:T(8,128)(2,1)S(1)} %copy-done, bf16[1024,256]{1,0:T(8,128)(2,1)S(1)} %collective-permute-done.refs_1_), custom_call_target="tpu_custom_call" | custom-call | flops 2000000000 | bytes 2000000 | tf_op jit(solution)/shard_map/arrange/pallas_call | solution.py:234
  35.8 4.6 %collective-permute-done.2.refs_1_ = bf16[1024,256]{1,0:T(8,128)(2,1)S(1)} collective-permute-done((bf16[1024,256]{1,0:T(8,128)(2,1)S(1)}, bf16[1024,256]{1,0:T(8,128)(2,1)S(1)}, u32[]{:S(2)}, u32[]{:S(2)}) %collective-permute-start.2) | collective-permute-done | bytes 524320 | tf_op jit(solution)/shard_map/ppermute | solution.py:304
  40.5 1.9 %collective-permute-done.1.refs_0_ = bf16[1024,256]{1,0:T(8,128)(2,1)S(1)} collective-permute-done((bf16[1024,256]{1,0:T(8,128)(2,1)S(1)}, bf16[1024,256]{1,0:T(8,128)(2,1)S(1)}, u32[]{:S(2)}, u32[]{:S(2)}) %collective-permute-start.1) | collective-permute-done | bytes 524320 | tf_op jit(solution)/shard_map/ppermute | solution.py:304
  42.4 1.2 %arrange.3 = (bf16[1024,256]{1,0:T(8,128)(2,1)S(1)}, bf16[1024,256]{1,0:T(8,128)(2,1)S(1)}) custom-call(s32[8,1024]{1,0:T(8,128)S(1)} %get-tuple-element.16.place, bf16[1024,256]{1,0:T(8,128)(2,1)S(1)} %collective-permute-done.1.refs_0_, bf16[1024,256]{1,0:T(8,128)(2,1)S(1)} %collective-permute-done.2.refs_1_), custom_call_target="tpu_custom_call" | custom-call | flops 2000000000 | bytes 2000000 | tf_op jit(solution)/shard_map/arrange/pallas_call | solution.py:234
  43.6 12.3 %all-to-all-done.received = bf16[128,16,256]{2,1,0:T(8,128)(2,1)S(1)} async-done(((bf16[128,16,256]{2,1,0:T(8,128)(2,1)}), bf16[128,16,256]{2,1,0:T(8,128)(2,1)S(1)}, u32[]{:S(2)}, u32[]{:S(2)}) %all-to-all-start) | async-done | bytes 1048608 | tf_op jit(solution)/shard_map/all_to_all | solution.py:302
  56.0 1.8 %multiply.1 = (f32[1024,128]{1,0:T(8,128)S(1)}, bf16[128,1024]{1,0:T(8,128)(2,1)S(1)}) custom-call(s32[8,128]{1,0:T(8,128)S(1)} %get-tuple-element.15.offsets, bf16[128,16,256]{2,1,0:T(8,128)(2,1)S(1)} %all-to-all-done.received, bf16[1024,256]{1,0:T(8,128)(2,1)S(1)} %get-tuple-element.18.amps0, bf16[1024,256]{1,0:T(8,128)(2,1)S(1)} %get-tuple-element.20.amps1, ...), custom_call_target="tpu_custom_call" | custom-call | tf_op jit(solution)/shard_map/multiply/pallas_call | solution.py:250
  57.8 1.9 %collective-permute-start.3 = (f32[1024,128]{1,0:T(8,128)S(1)}, f32[1024,128]{1,0:T(8,128)S(1)}, u32[]{:S(2)}, u32[]{:S(2)}) collective-permute-start(f32[1024,128]{1,0:T(8,128)S(1)} %get-tuple-element.24), channel_id=1, source_target_pairs={{0,1},{1,0},{2,3},{3,2},{4,5},{5,4},{6,7},{7,6},{8,9},{9,8},{10,11... | collective-permute-start | bytes 1572872 | tf_op jit(solution)/shard_map/ppermute | solution.py:314
  59.8 0.5 keep.1
  60.3 1.4 %collective-permute-done.3 = f32[1024,128]{1,0:T(8,128)S(1)} collective-permute-done((f32[1024,128]{1,0:T(8,128)S(1)}, f32[1024,128]{1,0:T(8,128)S(1)}, u32[]{:S(2)}, u32[]{:S(2)}) %collective-permute-start.3) | collective-permute-done | bytes 524320 | tf_op jit(solution)/shard_map/ppermute | solution.py:314
  61.6 0.3 multiply_convert_fusion
  62.0 20.3 %all_to_all.10 = f16[64,16,128]{2,1,0:T(8,128)(2,1)S(1)} all-to-all(f16[64,16,128]{2,1,0:T(8,128)(2,1)S(1)} %bitcast.1), channel_id=1, replica_groups={{0,2,4,6,8,10,12,14,16,18,20,22,24,26,28,30,32,34,36,38,40,42,44,46,48,..., dimensions={0} | all-to-all | bytes 524288 | tf_op jit(solution)/shard_map/all_to_all | solution.py:317
  82.3 0.1 fusion.1
  82.4 0.6 convert_element_type.16
Async XLA Ops:
  0.0 25.1 %collective-permute-start = (bf16[1024,256]{1,0:T(8,128)(2,1)}, bf16[1024,256]{1,0:T(8,128)(2,1)S(1)}, u32[]{:S(2)}, u32[]{:S(2)}) collective-permute-start(bf16[1024,256]{1,0:T(8,128)(2,1)} %refs_0_.5), channel_id=1, source_target_pairs={{256,0},{384,128},{0,256},{128,384},{257,1},{385,129},{1,257},{129... | collective-permute-start | bytes 1572872 | tf_op jit(solution)/shard_map/ppermute | solution.py:304
  7.1 18.0 %copy-start = (bf16[1024,256]{1,0:T(8,128)(2,1)S(1)}, bf16[1024,256]{1,0:T(8,128)(2,1)}, u32[]{:S(2)}) copy-start(bf16[1024,256]{1,0:T(8,128)(2,1)} %refs_0_.5) | copy-start | bytes 1572868
  7.1 48.8 %all-to-all-start = ((bf16[128,16,256]{2,1,0:T(8,128)(2,1)}), bf16[128,16,256]{2,1,0:T(8,128)(2,1)S(1)}, u32[]{:S(2)}, u32[]{:S(2)}) async-start(bf16[128,16,256]{2,1,0:T(8,128)(2,1)} %pack.1), calls=%async_computation | async-start | bytes 2097152 | tf_op jit(solution)/shard_map/all_to_all | solution.py:302
  25.1 15.3 %collective-permute-start.2 = (bf16[1024,256]{1,0:T(8,128)(2,1)S(1)}, bf16[1024,256]{1,0:T(8,128)(2,1)S(1)}, u32[]{:S(2)}, u32[]{:S(2)}) collective-permute-start(bf16[1024,256]{1,0:T(8,128)(2,1)S(1)} %copy-done), channel_id=1, source_target_pairs={{384,0},{0,128},{128,256},{256,384},{385,1},{1,129},{129,257},{257... | collective-permute-start | bytes 1572872 | tf_op jit(solution)/shard_map/ppermute | solution.py:304
  27.1 15.3 %collective-permute-start.1 = (bf16[1024,256]{1,0:T(8,128)(2,1)S(1)}, bf16[1024,256]{1,0:T(8,128)(2,1)S(1)}, u32[]{:S(2)}, u32[]{:S(2)}) collective-permute-start(bf16[1024,256]{1,0:T(8,128)(2,1)S(1)} %copy-done), channel_id=1, source_target_pairs={{128,0},{256,128},{384,256},{0,384},{129,1},{257,129},{385,257},{1... | collective-permute-start | bytes 1572872 | tf_op jit(solution)/shard_map/ppermute | solution.py:304
  57.8 3.8 %collective-permute-start.3 = (f32[1024,128]{1,0:T(8,128)S(1)}, f32[1024,128]{1,0:T(8,128)S(1)}, u32[]{:S(2)}, u32[]{:S(2)}) collective-permute-start(f32[1024,128]{1,0:T(8,128)S(1)} %get-tuple-element.24), channel_id=1, source_target_pairs={{0,1},{1,0},{2,3},{3,2},{4,5},{5,4},{6,7},{7,6},{8,9},{9,8},{10,11... | collective-permute-start | bytes 1572872 | tf_op jit(solution)/shard_map/ppermute | solution.py:314
